TPU v7x, 128 devices: a whole 4x4x4 slice. The times are simulated.
128 devices in a mesh: section: 2 (over y_lo), ctx: 16 (over x, y_hi, core), fsdp: 4 (over z).
Axes of the slice: x: 4, y: 4 (y_hi: 2, y_lo: 2; y = y_hi * 2 + y_lo), z: 4, core: 2. Of those that a mesh axis runs over, the one named last changes fastest.
Arguments:
- inputs: bfloat16 [4, 4, 1024, 768], P(None, 'fsdp', 'ctx'), may hold values from -6 to 6
- cotangent: bfloat16 [4, 4, 1024, 768], P(None, 'fsdp', 'ctx'), may hold values from -6 to 6
- plan: int32 [4], replicated, may hold values from 0 to 3, each once
- block_table: int32 [32], replicated, may hold values from 0 to 31, each once
- attn_in: bfloat16 [2, 768, 2304], P('section', 'fsdp'), may hold values from -0.21875 to 0.21875
- attn_out: bfloat16 [2, 768, 768], P('section', 'fsdp'), may hold values from -1.25 to 1.25
- mlp_in: bfloat16 [2, 768, 3072], P('section', 'fsdp'), may hold values from -0.21875 to 0.21875
- mlp_out: bfloat16 [2, 3072, 768], P('section', 'fsdp'), may hold values from -0.15625 to 0.15625
- norm_gains: bfloat16 [2, 2, 768], P('section', None, 'fsdp'), may hold values from 0.5 to 1.5
- biases: bfloat16 [2, 6, 768], P('section', None, 'fsdp'), may hold values from -3 to 3
- mlp_bias: bfloat16 [2, 3072], P('section', 'fsdp'), may hold values from -3 to 3
Outputs:
- layer_out: bfloat16 [2, 4, 4, 1024, 768], P('section', None, 'fsdp', 'ctx')
- input_grad: bfloat16 [2, 4, 4, 1024, 768], P('section', None, 'fsdp', 'ctx')
- grad_attn_in: float32 [2, 768, 2304], P('section', 'fsdp')
- grad_attn_out: float32 [2, 768, 768], P('section', 'fsdp')
- grad_mlp_in: float32 [2, 768, 3072], P('section', 'fsdp')
- grad_mlp_out: float32 [2, 3072, 768], P('section', 'fsdp')
- grad_gains: float32 [2, 2, 768], P('section', None, 'fsdp')
- grad_biases: float32 [2, 6, 768], P('section', None, 'fsdp')
- grad_mlp_bias: float32 [2, 3072], P('section', 'fsdp')
Inputs may be any that keep to these rules, and one draw needn't show every extreme that they name: `plan`: every micro-batch is taken at exactly one step. `block_table`: every block number occurs exactly once.
All inputs are finite; a program needn't handle non-finite values.
Results may differ from a plain program's by a relative error of at most 0.02.
Values may be sent and summed in bfloat16 or wider, within the bound.
No kernel may reach another device: no remote copies, remote signals or barrier semaphores. Data moves between devices by JAX's collectives and lax.ppermute only.
A program may use at most 256 MiB of HBM per device.

v0:
```python
import jax
import jax.numpy as jnp
from jax import lax
from jax.sharding import PartitionSpec as P

HEADS = 12
HDIM = 64


epsilon = 1e-05
neg_fill = -1e30


def shifted(value, axis, steps):
    count = lax.axis_size(axis)
    leading, last = (max(0, -steps), min(count, count - steps))
    return lax.ppermute(value, axis, [(source, source + steps) for source in range(leading, last)])


def cross(left_side, right_side, pattern):
    return jnp.einsum(pattern, left_side, right_side, preferred_element_type=jnp.float32)


def normalize(values, gain_row, shift_row):
    center = values - jnp.mean(values, -1, keepdims=True)
    spread = lax.rsqrt(jnp.mean(center * center, -1, keepdims=True) + epsilon)
    unit_rows = center * spread
    return (unit_rows * gain_row + shift_row, unit_rows, spread)


def normalize_back(grad_out, unit_rows, spread, gain_row):
    grad_unit = grad_out * gain_row
    grad_in = spread * (
        grad_unit
        - jnp.mean(grad_unit, -1, keepdims=True)
        - unit_rows * jnp.mean(grad_unit * unit_rows, -1, keepdims=True)
    )
    return (grad_in, jnp.sum(grad_out * unit_rows, 0), jnp.sum(grad_out, 0))


def positions(block_table, block_len):
    offsets = jnp.arange(block_len, dtype=jnp.int32)
    return (block_table[:, None] * block_len + offsets[None, :]).reshape(-1)


def shards(
    inputs,
    cotangent,
    plan,
    block_table,
    attn_in,
    attn_out,
    mlp_in,
    mlp_out,
    norm_gains,
    biases,
    mlp_bias,
):
    gathered = (
        lax.all_gather(attn_in, "fsdp", axis=1, tiled=True),
        lax.all_gather(attn_out, "fsdp", axis=1, tiled=True),
        lax.all_gather(mlp_in, "fsdp", axis=1, tiled=True),
        lax.all_gather(mlp_out, "fsdp", axis=1, tiled=True),
        lax.all_gather(norm_gains, "fsdp", axis=2, tiled=True),
        lax.all_gather(biases, "fsdp", axis=2, tiled=True),
        lax.all_gather(mlp_bias, "fsdp", axis=1, tiled=True),
    )
    w_qkv = gathered[0][0]
    w_out = gathered[1][0]
    w_up = gathered[2][0]
    w_down = gathered[3][0]
    gain_rows = gathered[4][0].astype(jnp.float32)
    bias_rows = gathered[5][0].astype(jnp.float32)
    up_bias = gathered[6][0].astype(jnp.float32)
    model_width = w_out.shape[0]
    micro_count = inputs.shape[0]
    local_rows = inputs.shape[2]
    section_id = lax.axis_index("section")
    sections = lax.axis_size("section")
    score_scale = float(HDIM) ** (-0.5)
    places = positions(block_table, local_rows // 2)
    seq_len = places.shape[0]
    my_places = lax.dynamic_slice_in_dim(places, lax.axis_index("ctx") * local_rows, local_rows)
    allowed = (places[None, :] <= my_places[:, None])[None]
    qkv_bias = jnp.concatenate([bias_rows[1], jnp.zeros_like(bias_rows[1]), bias_rows[2]])

    def scores_of(query_rows, key_all):
        query_heads = query_rows.reshape(local_rows, HEADS, HDIM)
        key_heads = key_all.reshape(seq_len, HEADS, HDIM)
        return jnp.where(
            allowed, cross(query_heads, key_heads, "thd,shd->hts") * score_scale, neg_fill
        )

    tick_count = micro_count + sections - 1
    zero_rows = jnp.zeros((local_rows, model_width), jnp.bfloat16)
    sent_rows = zero_rows
    results = []
    kept_list = []
    for tick_num in range(tick_count):
        received = shifted(sent_rows, "section", 1)
        slot_num = tick_num - section_id
        is_valid = (slot_num >= 0) & (slot_num < micro_count)
        safe_slot = jnp.clip(slot_num, 0, micro_count - 1)
        chosen = plan[safe_slot]
        fresh_rows = lax.dynamic_index_in_dim(inputs, chosen, 0, keepdims=False)[0]
        entering = jnp.where(is_valid, jnp.where(section_id == 0, fresh_rows, received), zero_rows)
        stream = entering.astype(jnp.float32)
        normed, unit_one, spread_one = normalize(stream, gain_rows[0], bias_rows[0])
        normed_low = normed.astype(jnp.bfloat16)
        joined = cross(normed_low, w_qkv, "td,de->te") + qkv_bias
        queries = joined[:, :model_width].astype(jnp.bfloat16)
        keys_local = joined[:, model_width : 2 * model_width].astype(jnp.bfloat16)
        values_local = joined[:, 2 * model_width :].astype(jnp.bfloat16)
        forward_key_all = lax.all_gather(keys_local, "ctx", axis=0, tiled=True)
        forward_value_all = lax.all_gather(values_local, "ctx", axis=0, tiled=True)
        forward_scores = scores_of(queries, forward_key_all)
        row_max = jnp.max(forward_scores, -1, keepdims=True)
        powers = jnp.exp(forward_scores - row_max)
        row_total = jnp.sum(powers, -1, keepdims=True)
        forward_attn_weights = powers / row_total
        log_total = row_max + jnp.log(row_total)
        mixed = cross(
            forward_attn_weights.astype(jnp.bfloat16),
            forward_value_all.reshape(seq_len, HEADS, HDIM),
            "hts,shd->thd",
        )
        mixed = mixed.reshape(local_rows, model_width).astype(jnp.bfloat16)
        middle = stream + (cross(mixed, w_out, "td,de->te") + bias_rows[3])
        normed_two, unit_two, spread_two = normalize(middle, gain_rows[1], bias_rows[4])
        normed_two_low = normed_two.astype(jnp.bfloat16)
        hidden_pre = cross(normed_two_low, w_up, "td,df->tf") + up_bias
        active_low = jax.nn.gelu(hidden_pre).astype(jnp.bfloat16)
        result = (middle + (cross(active_low, w_down, "tf,fd->td") + bias_rows[5])).astype(
            jnp.bfloat16
        )
        forward_saved = {
            "unit_one": unit_one,
            "spread_one": spread_one,
            "normed_low": normed_low,
            "queries": queries,
            "keys_local": keys_local,
            "values_local": values_local,
            "log_total": log_total,
            "mixed": mixed,
            "unit_two": unit_two,
            "spread_two": spread_two,
            "normed_two_low": normed_two_low,
            "hidden_pre": hidden_pre,
            "active_low": active_low,
        }
        sent_rows = result
        results.append(sent_rows)
        kept_list.append(forward_saved)
    stacked = jax.tree.map(lambda *members: jnp.stack(members), *kept_list)
    result_stack = jnp.stack(results)
    layer_out = jnp.stack(
        [
            lax.dynamic_index_in_dim(result_stack, step_num + section_id, 0, keepdims=False)
            for step_num in range(micro_count)
        ]
    )
    sent_back = zero_rows
    totals = None
    back_list = []
    for tick_num in range(tick_count):
        received = shifted(sent_back, "section", -1)
        slot_num = tick_num - (sections - 1 - section_id)
        is_valid = (slot_num >= 0) & (slot_num < micro_count)
        safe_slot = jnp.clip(slot_num, 0, micro_count - 1)
        own_cot = lax.dynamic_index_in_dim(cotangent, safe_slot, 0, keepdims=False)[0]
        grad_top = jnp.where(
            is_valid, jnp.where(section_id == sections - 1, own_cot, received), zero_rows
        ).astype(jnp.float32)
        picked = jax.tree.map(
            lambda member: lax.dynamic_index_in_dim(
                member, safe_slot + section_id, 0, keepdims=False
            ),
            stacked,
        )
        grad_branch = grad_top.astype(jnp.bfloat16)
        d_down = cross(picked["active_low"], grad_branch, "tf,td->fd")
        d_shift_out = jnp.sum(grad_branch.astype(jnp.float32), 0)
        grad_active = cross(grad_branch, w_down, "td,fd->tf")
        unused, gelu_pull = jax.vjp(jax.nn.gelu, picked["hidden_pre"])
        grad_hidden = gelu_pull(grad_active)[0].astype(jnp.bfloat16)
        d_up = cross(picked["normed_two_low"], grad_hidden, "td,tf->df")
        d_up_bias = jnp.sum(grad_hidden.astype(jnp.float32), 0)
        grad_normed_two = cross(grad_hidden, w_up, "tf,df->td")
        grad_norm_two, d_gain_two, d_shift_two = normalize_back(
            grad_normed_two, picked["unit_two"], picked["spread_two"], gain_rows[1]
        )
        grad_middle = grad_top + grad_norm_two
        grad_attn = grad_middle.astype(jnp.bfloat16)
        d_out = cross(picked["mixed"], grad_attn, "td,te->de")
        d_shift_attn = jnp.sum(grad_attn.astype(jnp.float32), 0)
        grad_mixed_rows = cross(grad_attn, w_out, "te,de->td").astype(jnp.bfloat16)
        grad_mixed = grad_mixed_rows.reshape(local_rows, HEADS, HDIM)
        backward_key_all = lax.all_gather(picked["keys_local"], "ctx", axis=0, tiled=True)
        value_all = lax.all_gather(picked["values_local"], "ctx", axis=0, tiled=True)
        backward_key_heads = backward_key_all.reshape(seq_len, HEADS, HDIM)
        value_heads = value_all.reshape(seq_len, HEADS, HDIM)
        backward_query_heads = picked["queries"].reshape(local_rows, HEADS, HDIM)
        scores = scores_of(picked["queries"], backward_key_all)
        attn_weights = jnp.exp(scores - picked["log_total"])
        grad_weights = cross(grad_mixed, value_heads, "thd,shd->hts")
        inner_sum = jnp.sum(attn_weights * grad_weights, -1, keepdims=True)
        grad_scores = (attn_weights * (grad_weights - inner_sum)).astype(jnp.bfloat16)
        grad_queries = (
            (cross(grad_scores, backward_key_heads, "hts,shd->thd") * score_scale)
            .reshape(local_rows, model_width)
            .astype(jnp.bfloat16)
        )
        weights_low = attn_weights.astype(jnp.bfloat16)
        grad_values_all = cross(weights_low, grad_mixed, "hts,thd->shd").reshape(
            seq_len, model_width
        )
        grad_keys_all = (
            cross(grad_scores, backward_query_heads, "hts,thd->shd") * score_scale
        ).reshape(seq_len, model_width)
        grad_keys = lax.psum_scatter(
            grad_keys_all.astype(jnp.bfloat16), "ctx", scatter_dimension=0, tiled=True
        )
        grad_values = lax.psum_scatter(
            grad_values_all.astype(jnp.bfloat16), "ctx", scatter_dimension=0, tiled=True
        )
        grad_joined = jnp.concatenate([grad_queries, grad_keys, grad_values], -1)
        d_qkv = cross(picked["normed_low"], grad_joined, "td,te->de")
        d_shift_query = jnp.sum(grad_queries.astype(jnp.float32), 0)
        d_shift_value = jnp.sum(grad_values.astype(jnp.float32), 0)
        grad_normed = cross(grad_joined, w_qkv, "te,de->td")
        grad_norm_one, d_gain_one, d_shift_one = normalize_back(
            grad_normed, picked["unit_one"], picked["spread_one"], gain_rows[0]
        )
        grad_in = (grad_middle + grad_norm_one).astype(jnp.bfloat16)
        gain_grads = jnp.stack([d_gain_one, d_gain_two])
        shift_grads = jnp.stack(
            [d_shift_one, d_shift_query, d_shift_value, d_shift_attn, d_shift_two, d_shift_out]
        )
        sent_back = grad_in
        layer_grads = (d_qkv, d_out, d_up, d_down, gain_grads, shift_grads, d_up_bias)
        totals = layer_grads if totals is None else jax.tree.map(jnp.add, totals, layer_grads)
        back_list.append(sent_back)
    back_stack = jnp.stack(back_list)
    input_grad = jnp.stack(
        [
            lax.dynamic_index_in_dim(
                back_stack, step_num + sections - 1 - section_id, 0, keepdims=False
            )
            for step_num in range(micro_count)
        ]
    )
    shares = (
        lax.psum_scatter(
            totals[0].astype(jnp.bfloat16), "fsdp", scatter_dimension=0, tiled=True
        ).astype(jnp.float32),
        lax.psum_scatter(
            totals[1].astype(jnp.bfloat16), "fsdp", scatter_dimension=0, tiled=True
        ).astype(jnp.float32),
        lax.psum_scatter(
            totals[2].astype(jnp.bfloat16), "fsdp", scatter_dimension=0, tiled=True
        ).astype(jnp.float32),
        lax.psum_scatter(
            totals[3].astype(jnp.bfloat16), "fsdp", scatter_dimension=0, tiled=True
        ).astype(jnp.float32),
        lax.psum_scatter(
            totals[4].astype(jnp.bfloat16), "fsdp", scatter_dimension=1, tiled=True
        ).astype(jnp.float32),
        lax.psum_scatter(
            totals[5].astype(jnp.bfloat16), "fsdp", scatter_dimension=1, tiled=True
        ).astype(jnp.float32),
        lax.psum_scatter(
            totals[6].astype(jnp.bfloat16), "fsdp", scatter_dimension=0, tiled=True
        ).astype(jnp.float32),
    )
    finals = (
        lax.psum(shares[0].astype(jnp.bfloat16), "ctx").astype(jnp.float32),
        lax.psum(shares[1].astype(jnp.bfloat16), "ctx").astype(jnp.float32),
        lax.psum(shares[2].astype(jnp.bfloat16), "ctx").astype(jnp.float32),
        lax.psum(shares[3].astype(jnp.bfloat16), "ctx").astype(jnp.float32),
        lax.psum(shares[4].astype(jnp.bfloat16), "ctx").astype(jnp.float32),
        lax.psum(shares[5].astype(jnp.bfloat16), "ctx").astype(jnp.float32),
        lax.psum(shares[6].astype(jnp.bfloat16), "ctx").astype(jnp.float32),
    )
    return (
        layer_out[None, :, None],
        input_grad[None, :, None],
        finals[0][None],
        finals[1][None],
        finals[2][None],
        finals[3][None],
        finals[4][None],
        finals[5][None],
        finals[6][None],
    )


def solution(mesh):
    placed = (
        P(None, "fsdp", "ctx", None),
        P(None, "fsdp", "ctx", None),
        P(),
        P(),
        P("section", "fsdp", None),
        P("section", "fsdp", None),
        P("section", "fsdp", None),
        P("section", "fsdp", None),
        P("section", None, "fsdp"),
        P("section", None, "fsdp"),
        P("section", "fsdp"),
    )
    return jax.shard_map(
        shards,
        mesh=mesh,
        in_specs=placed,
        out_specs=(
            P("section", None, "fsdp", "ctx", None),
            P("section", None, "fsdp", "ctx", None),
            P("section", "fsdp", None),
            P("section", "fsdp", None),
            P("section", "fsdp", None),
            P("section", "fsdp", None),
            P("section", None, "fsdp"),
            P("section", None, "fsdp"),
            P("section", "fsdp"),
        ),
        check_vma=False,
    )
```

profile of v0, /device:TPU:1, one launch (start us, length us, event | category | flops | bytes accessed | tf_op | source)
XLA Modules:
  0.0 2465.7 jit_solution(2768077701531078191)
XLA Ops:
  15.7 11.5 all_gather.82
  28.5 13.0 all_gather.81
  47.1 13.4 slice_reduce_fusion.1
  68.9 9.5 all_gather.88
  79.4 39.5 %all-gather.37.cloned.1.call-done = bf16[1024,768]{1,0:T(8,128)(2,1)} async-done(((bf16[64,768]{1,0:T(8,128)(2,1)}), bf16[1024,768]{1,0:T(8,128)(2,1)}) %all-gather.37.cloned.1.call-update) | async-done | bytes 1572880 | tf_op jit(solution)/shard_map/all_gather | solution.py:115
  120.6 46.7 %all-gather.39.cloned.1.call-done = bf16[1024,768]{1,0:T(8,128)(2,1)} async-done(((bf16[64,768]{1,0:T(8,128)(2,1)}), bf16[1024,768]{1,0:T(8,128)(2,1)}) %all-gather.39.cloned.1.call-update) | async-done | bytes 1572880 | tf_op jit(solution)/shard_map/all_gather | solution.py:114
  173.0 18.0 all-gather.41.cloned.1.call-done
  193.0 53.8 %all-gather.43.cloned.1.call-done = bf16[1,768,3072]{2,1,0:T(8,128)(2,1)} async-done(((bf16[1,192,3072]{2,1,0:T(8,128)(2,1)}), bf16[1,768,3072]{2,1,0:T(8,128)(2,1)}) %all-gather.43.cloned.1.call-update) | async-done | bytes 4718608 | tf_op jit(solution)/shard_map/all_gather | solution.py:62
  251.3 50.1 %all-gather.45.cloned.1.call-done = bf16[1,3072,768]{2,1,0:T(8,128)(2,1)} async-done(((bf16[1,768,768]{2,1,0:T(8,128)(2,1)}), bf16[1,3072,768]{2,1,0:T(8,128)(2,1)}) %all-gather.45.cloned.1.call-update) | async-done | bytes 4718608 | tf_op jit(solution)/shard_map/all_gather | solution.py:63
  316.7 47.4 %all-gather.49.cloned.1.call-done = bf16[1024,768]{1,0:T(8,128)(2,1)} async-done(((bf16[64,768]{1,0:T(8,128)(2,1)}), bf16[1024,768]{1,0:T(8,128)(2,1)}) %all-gather.49.cloned.1.call-update) | async-done | bytes 1572880 | tf_op jit(solution)/shard_map/all_gather | solution.py:114
  369.1 43.4 %all-gather.47.cloned.1.call-done = bf16[1024,768]{1,0:T(8,128)(2,1)} async-done(((bf16[64,768]{1,0:T(8,128)(2,1)}), bf16[1024,768]{1,0:T(8,128)(2,1)}) %all-gather.47.cloned.1.call-update) | async-done | bytes 1572880 | tf_op jit(solution)/shard_map/all_gather | solution.py:115
  424.7 13.0 collective-permute-start.2
  444.5 46.0 %all-gather.53.cloned.1.call-done = bf16[1024,768]{1,0:T(8,128)(2,1)} async-done(((bf16[64,768]{1,0:T(8,128)(2,1)}), bf16[1024,768]{1,0:T(8,128)(2,1)}) %all-gather.53.cloned.1.call-update) | async-done | bytes 1572880 | tf_op jit(solution)/shard_map/all_gather | solution.py:114
  495.5 43.3 %all-gather.51.cloned.1.call-done = bf16[1024,768]{1,0:T(8,128)(2,1)} async-done(((bf16[64,768]{1,0:T(8,128)(2,1)}), bf16[1024,768]{1,0:T(8,128)(2,1)}) %all-gather.51.cloned.1.call-update) | async-done | bytes 1572880 | tf_op jit(solution)/shard_map/all_gather | solution.py:115
  560.8 47.0 %all-gather.57.cloned.1.call-done = bf16[1024,768]{1,0:T(8,128)(2,1)} async-done(((bf16[64,768]{1,0:T(8,128)(2,1)}), bf16[1024,768]{1,0:T(8,128)(2,1)}) %all-gather.57.cloned.1.call-update) | async-done | bytes 1572880 | tf_op jit(solution)/shard_map/all_gather | solution.py:114
  612.9 42.7 %all-gather.55.cloned.1.call-done = bf16[1024,768]{1,0:T(8,128)(2,1)} async-done(((bf16[64,768]{1,0:T(8,128)(2,1)}), bf16[1024,768]{1,0:T(8,128)(2,1)}) %all-gather.55.cloned.1.call-update) | async-done | bytes 1572880 | tf_op jit(solution)/shard_map/all_gather | solution.py:115
  693.7 31.1 %all-gather.61.cloned.1.call-done = bf16[1024,768]{1,0:T(8,128)(2,1)} async-done(((bf16[64,768]{1,0:T(8,128)(2,1)}), bf16[1024,768]{1,0:T(8,128)(2,1)}) %all-gather.61.cloned.1.call-update) | async-done | bytes 1572880 | tf_op jit(solution)/shard_map/all_gather | solution.py:114
  729.8 42.7 %all-gather.59.cloned.1.call-done = bf16[1024,768]{1,0:T(8,128)(2,1)} async-done(((bf16[64,768]{1,0:T(8,128)(2,1)}), bf16[1024,768]{1,0:T(8,128)(2,1)}) %all-gather.59.cloned.1.call-update) | async-done | bytes 1572880 | tf_op jit(solution)/shard_map/all_gather | solution.py:115
  790.9 29.9 %all-gather.65.cloned.1.call-done = bf16[1,1024,768]{2,1,0:T(8,128)(2,1)} async-done(((bf16[1,64,768]{2,1,0:T(8,128)(2,1)}), bf16[1,1024,768]{2,1,0:T(8,128)(2,1)}) %all-gather.65.cloned.1.call-update) | async-done | bytes 1572880 | tf_op jit(solution)/shard_map/all_gather | solution.py:199
  825.5 43.7 %all-gather.63.cloned.1.call-done = bf16[1,1024,768]{2,1,0:T(8,128)(2,1)} async-done(((bf16[1,64,768]{2,1,0:T(8,128)(2,1)}), bf16[1,1024,768]{2,1,0:T(8,128)(2,1)}) %all-gather.63.cloned.1.call-update) | async-done | bytes 1572880 | tf_op jit(solution)/shard_map/all_gather | solution.py:198
  908.5 38.6 %reduce-scatter.21.cloned.1.call-done = bf16[64,768]{1,0:T(8,128)(2,1)} async-done(((bf16[1024,768]{1,0:T(8,128)(2,1)}), bf16[64,768]{1,0:T(8,128)(2,1)}) %reduce-scatter.21.cloned.1.call-update) | async-done | bytes 98320 | tf_op jit(solution)/shard_map/reduce_scatter | solution.py:220
  948.7 70.0 %reduce-scatter.23.cloned.1.call-done = bf16[64,768]{1,0:T(8,128)(2,1)} async-done(((bf16[1024,768]{1,0:T(8,128)(2,1)}), bf16[64,768]{1,0:T(8,128)(2,1)}) %reduce-scatter.23.cloned.1.call-update) | async-done | bytes 98320 | tf_op jit(solution)/shard_map/reduce_scatter | solution.py:223
  1028.0 41.2 %all-gather.67.cloned.1.call-done = bf16[1,1024,768]{2,1,0:T(8,128)(2,1)} async-done(((bf16[1,64,768]{2,1,0:T(8,128)(2,1)}), bf16[1,1024,768]{2,1,0:T(8,128)(2,1)}) %all-gather.67.cloned.1.call-update) | async-done | bytes 1572880 | tf_op jit(solution)/shard_map/all_gather | solution.py:198
  1071.8 45.1 %all-gather.69.cloned.1.call-done = bf16[1,1024,768]{2,1,0:T(8,128)(2,1)} async-done(((bf16[1,64,768]{2,1,0:T(8,128)(2,1)}), bf16[1,1024,768]{2,1,0:T(8,128)(2,1)}) %all-gather.69.cloned.1.call-update) | async-done | bytes 1572880 | tf_op jit(solution)/shard_map/all_gather | solution.py:199
  1160.6 50.3 %reduce-scatter.25.cloned.1.call-done = bf16[64,768]{1,0:T(8,128)(2,1)} async-done(((bf16[1024,768]{1,0:T(8,128)(2,1)}), bf16[64,768]{1,0:T(8,128)(2,1)}) %reduce-scatter.25.cloned.1.call-update) | async-done | bytes 98320 | tf_op jit(solution)/shard_map/reduce_scatter | solution.py:220
  1212.5 70.2 %reduce-scatter.27.cloned.1.call-done = bf16[64,768]{1,0:T(8,128)(2,1)} async-done(((bf16[1024,768]{1,0:T(8,128)(2,1)}), bf16[64,768]{1,0:T(8,128)(2,1)}) %reduce-scatter.27.cloned.1.call-update) | async-done | bytes 98320 | tf_op jit(solution)/shard_map/reduce_scatter | solution.py:223
  1292.2 41.1 %all-gather.71.cloned.1.call-done = bf16[1,1024,768]{2,1,0:T(8,128)(2,1)} async-done(((bf16[1,64,768]{2,1,0:T(8,128)(2,1)}), bf16[1,1024,768]{2,1,0:T(8,128)(2,1)}) %all-gather.71.cloned.1.call-update) | async-done | bytes 1572880 | tf_op jit(solution)/shard_map/all_gather | solution.py:198
  1335.8 45.2 %all-gather.73.cloned.1.call-done = bf16[1,1024,768]{2,1,0:T(8,128)(2,1)} async-done(((bf16[1,64,768]{2,1,0:T(8,128)(2,1)}), bf16[1,1024,768]{2,1,0:T(8,128)(2,1)}) %all-gather.73.cloned.1.call-update) | async-done | bytes 1572880 | tf_op jit(solution)/shard_map/all_gather | solution.py:199
  1424.7 50.3 %reduce-scatter.29.cloned.1.call-done = bf16[64,768]{1,0:T(8,128)(2,1)} async-done(((bf16[1024,768]{1,0:T(8,128)(2,1)}), bf16[64,768]{1,0:T(8,128)(2,1)}) %reduce-scatter.29.cloned.1.call-update) | async-done | bytes 98320 | tf_op jit(solution)/shard_map/reduce_scatter | solution.py:220
  1476.5 70.1 %reduce-scatter.31.cloned.1.call-done = bf16[64,768]{1,0:T(8,128)(2,1)} async-done(((bf16[1024,768]{1,0:T(8,128)(2,1)}), bf16[64,768]{1,0:T(8,128)(2,1)}) %reduce-scatter.31.cloned.1.call-update) | async-done | bytes 98320 | tf_op jit(solution)/shard_map/reduce_scatter | solution.py:223
  1556.3 40.7 %all-gather.75.cloned.1.call-done = bf16[1,1024,768]{2,1,0:T(8,128)(2,1)} async-done(((bf16[1,64,768]{2,1,0:T(8,128)(2,1)}), bf16[1,1024,768]{2,1,0:T(8,128)(2,1)}) %all-gather.75.cloned.1.call-update) | async-done | bytes 1572880 | tf_op jit(solution)/shard_map/all_gather | solution.py:198
  1599.5 45.3 %all-gather.77.cloned.1.call-done = bf16[1,1024,768]{2,1,0:T(8,128)(2,1)} async-done(((bf16[1,64,768]{2,1,0:T(8,128)(2,1)}), bf16[1,1024,768]{2,1,0:T(8,128)(2,1)}) %all-gather.77.cloned.1.call-update) | async-done | bytes 1572880 | tf_op jit(solution)/shard_map/all_gather | solution.py:199
  1688.7 50.2 %reduce-scatter.33.cloned.1.call-done = bf16[64,768]{1,0:T(8,128)(2,1)} async-done(((bf16[1024,768]{1,0:T(8,128)(2,1)}), bf16[64,768]{1,0:T(8,128)(2,1)}) %reduce-scatter.33.cloned.1.call-update) | async-done | bytes 98320 | tf_op jit(solution)/shard_map/reduce_scatter | solution.py:220
  1740.4 70.0 %reduce-scatter.35.cloned.1.call-done = bf16[64,768]{1,0:T(8,128)(2,1)} async-done(((bf16[1024,768]{1,0:T(8,128)(2,1)}), bf16[64,768]{1,0:T(8,128)(2,1)}) %reduce-scatter.35.cloned.1.call-update) | async-done | bytes 98320 | tf_op jit(solution)/shard_map/reduce_scatter | solution.py:223
  1819.9 41.0 %all-gather.79.cloned.1.call-done = bf16[1,1024,768]{2,1,0:T(8,128)(2,1)} async-done(((bf16[1,64,768]{2,1,0:T(8,128)(2,1)}), bf16[1,1024,768]{2,1,0:T(8,128)(2,1)}) %all-gather.79.cloned.1.call-update) | async-done | bytes 1572880 | tf_op jit(solution)/shard_map/all_gather | solution.py:198
  1863.5 45.3 %all-gather.81.cloned.1.call-done = bf16[1,1024,768]{2,1,0:T(8,128)(2,1)} async-done(((bf16[1,64,768]{2,1,0:T(8,128)(2,1)}), bf16[1,1024,768]{2,1,0:T(8,128)(2,1)}) %all-gather.81.cloned.1.call-update) | async-done | bytes 1572880 | tf_op jit(solution)/shard_map/all_gather | solution.py:199
  1974.7 28.2 %reduce-scatter.37.cloned.1.call-done = bf16[64,768]{1,0:T(8,128)(2,1)} async-done(((bf16[1024,768]{1,0:T(8,128)(2,1)}), bf16[64,768]{1,0:T(8,128)(2,1)}) %reduce-scatter.37.cloned.1.call-update) | async-done | bytes 98320 | tf_op jit(solution)/shard_map/reduce_scatter | solution.py:220
  2004.4 70.2 %reduce-scatter.39.cloned.1.call-done = bf16[64,768]{1,0:T(8,128)(2,1)} async-done(((bf16[1024,768]{1,0:T(8,128)(2,1)}), bf16[64,768]{1,0:T(8,128)(2,1)}) %reduce-scatter.39.cloned.1.call-update) | async-done | bytes 98320 | tf_op jit(solution)/shard_map/reduce_scatter | solution.py:223
  2091.2 9.5 add_convert_fusion.2
  2122.5 15.7 add_convert_fusion.1
  2161.9 15.8 add_convert_fusion
  2184.1 15.7 reduce-scatter.45.cloned.1.call-done
  2199.8 53.3 %reduce-scatter.47.cloned.1.call-done = bf16[768,768]{1,0:T(8,128)(2,1)} async-done(((bf16[3072,768]{1,0:T(8,128)(2,1)}), bf16[768,768]{1,0:T(8,128)(2,1)}) %reduce-scatter.47.cloned.1.call-update) | async-done | bytes 1179664 | tf_op jit(solution)/shard_map/reduce_scatter | solution.py:262
  2258.7 6.6 all-reduce
  2266.3 7.7 reduce-scatter.49.cloned.1.call-done
  2274.8 22.6 reduce-scatter.51.cloned.1.call-done
  2298.3 36.0 %all-reduce.1 = (bf16[1,6,192]{2,1,0:T(8,128)(2,1)S(1)}, bf16[1,2,192]{2,1,0:T(2,128)(2,1)S(1)}, bf16[1,768]{1,0:T(2,128)(2,1)S(1)}) all-reduce(bf16[1,6,192]{2,1,0:T(8,128)(2,1)S(1)} %bitcast.1061, bf16[1,2,192]{2,1,0:T(2,128)(2,1)S(1)} %bitcast.1062, ...), channel_id=1, replica_groups=mesh['section'=2,'ctx'=16,'fsdp'=4] {'ctx'}, use_global_device_ids=true, to_apply=%region_116.117 | all-reduce | flops 2304 | bytes 9216 | tf_op jit(solution)/shard_map/psum | solution.py:281
  2336.0 114.7 %all-reduce.5.cloned.1.call-done = (bf16[1,192,2304]{2,1,0:T(8,128)(2,1)}, bf16[1,192,768]{2,1,0:T(8,128)(2,1)}, bf16[1,192,3072]{2,1,0:T(8,128)(2,1)}, bf16[1,768,768]{2,1,0:T(8,128)(2,1)}) async-done(((bf16[1,192,2304]{2,1,0:T(8,128)(2,1)}, bf16[1,192,768]{2,1,0:T(8,128)(2,1)}, bf16[1,192,3072]{2,1,0:T(8,128)(2,1)}, bf16[1,768,768]{2,1,0:T(8,128)(2,1)}), (bf16[1,192,2304]{2,1,0:T(8,128)(2,1)}, ...) | async-done | bytes 3538960 | tf_op jit(solution)/shard_map/psum | solution.py:276
  (1109 shorter events, 539.3 us)
Async XLA Ops:
  7.2 54.7 %all-gather.35.cloned.1.call-start = ((), (), s32[]{:S(2)}) async-start(), calls=%async_computation.16 | async-start | bytes 4423680 | tf_op jit(solution)/shard_map/all_gather | solution.py:60
  7.9 111.0 %all-gather.37.cloned.1.call-start = ((), (), s32[]{:S(2)}) async-start(), calls=%async_computation.17 | async-start | bytes 1671168 | tf_op jit(solution)/shard_map/all_gather | solution.py:115
  8.0 52.5 %collective-permute-start = (bf16[64,768]{1,0:T(8,128)(2,1)S(1)}, bf16[64,768]{1,0:T(8,128)(2,1)S(1)}, u32[]{:S(2)}, u32[]{:S(2)}) collective-permute-start(bf16[64,768]{1,0:T(8,128)(2,1)S(1)} %broadcast_in_dim.171), channel_id=1, source_target_pairs={{0,64},{1,65},{2,66},{3,67},{4,68},{5,69},{6,70},{7,71},{8,72},{9,... | collective-permute-start | bytes 294920 | tf_op jit(solution)/shard_map/ppermute | solution.py:17
  66.1 101.3 %all-gather.39.cloned.1.call-start = ((), (), s32[]{:S(2)}) async-start(), calls=%async_computation.18 | async-start | bytes 1671168 | tf_op jit(solution)/shard_map/all_gather | solution.py:114
  66.9 124.1 %all-gather.41.cloned.1.call-start = ((), (), s32[]{:S(2)}) async-start(), calls=%async_computation.19 | async-start | bytes 1474560 | tf_op jit(solution)/shard_map/all_gather | solution.py:61
  67.4 179.3 %all-gather.43.cloned.1.call-start = ((), (), s32[]{:S(2)}) async-start(), calls=%async_computation.20 | async-start | bytes 5898240 | tf_op jit(solution)/shard_map/all_gather | solution.py:62
  68.0 233.4 %all-gather.45.cloned.1.call-start = ((), (), s32[]{:S(2)}) async-start(), calls=%async_computation.21 | async-start | bytes 5898240 | tf_op jit(solution)/shard_map/all_gather | solution.py:63
  68.6 295.4 %all-gather.49.cloned.1.call-start = ((), (), s32[]{:S(2)}) async-start(), calls=%async_computation.23 | async-start | bytes 1671168 | tf_op jit(solution)/shard_map/all_gather | solution.py:114
  305.8 5.7 collective-permute-start.1
  315.7 96.8 %all-gather.47.cloned.1.call-start = ((), (), s32[]{:S(2)}) async-start(), calls=%async_computation.22 | async-start | bytes 1671168 | tf_op jit(solution)/shard_map/all_gather | solution.py:115
  316.4 174.0 %all-gather.53.cloned.1.call-start = ((), (), s32[]{:S(2)}) async-start(), calls=%async_computation.25 | async-start | bytes 1671168 | tf_op jit(solution)/shard_map/all_gather | solution.py:114
  424.7 14.9 collective-permute-start.2
  443.7 95.1 %all-gather.51.cloned.1.call-start = ((), (), s32[]{:S(2)}) async-start(), calls=%async_computation.24 | async-start | bytes 1671168 | tf_op jit(solution)/shard_map/all_gather | solution.py:115
  444.3 163.5 %all-gather.57.cloned.1.call-start = ((), (), s32[]{:S(2)}) async-start(), calls=%async_computation.27 | async-start | bytes 1671168 | tf_op jit(solution)/shard_map/all_gather | solution.py:114
  560.0 95.6 %all-gather.55.cloned.1.call-start = ((), (), s32[]{:S(2)}) async-start(), calls=%async_computation.26 | async-start | bytes 1671168 | tf_op jit(solution)/shard_map/all_gather | solution.py:115
  560.6 164.2 %all-gather.61.cloned.1.call-start = ((), (), s32[]{:S(2)}) async-start(), calls=%async_computation.29 | async-start | bytes 1671168 | tf_op jit(solution)/shard_map/all_gather | solution.py:114
  676.8 95.7 %all-gather.59.cloned.1.call-start = ((), (), s32[]{:S(2)}) async-start(), calls=%async_computation.28 | async-start | bytes 1671168 | tf_op jit(solution)/shard_map/all_gather | solution.py:115
  677.4 143.4 %all-gather.65.cloned.1.call-start = ((), (), s32[]{:S(2)}) async-start(), calls=%async_computation.45 | async-start | bytes 1671168 | tf_op jit(solution)/shard_map/all_gather | solution.py:199
  688.6 180.5 %all-gather.63.cloned.1.call-start = ((), (), s32[]{:S(2)}) async-start(), calls=%async_computation.44 | async-start | bytes 1671168 | tf_op jit(solution)/shard_map/all_gather | solution.py:198
  693.2 253.9 %reduce-scatter.21.cloned.1.call-start = ((), (), s32[]{:S(2)}) async-start(), calls=%async_computation.30 | async-start | bytes 1671168 | tf_op jit(solution)/shard_map/reduce_scatter | solution.py:220
  881.7 137.0 %reduce-scatter.23.cloned.1.call-start = ((), (), s32[]{:S(2)}) async-start(), calls=%async_computation.31 | async-start | bytes 1671168 | tf_op jit(solution)/shard_map/reduce_scatter | solution.py:223
  886.2 183.0 %all-gather.67.cloned.1.call-start = ((), (), s32[]{:S(2)}) async-start(), calls=%async_computation.46 | async-start | bytes 1671168 | tf_op jit(solution)/shard_map/all_gather | solution.py:198
  886.9 230.0 %all-gather.69.cloned.1.call-start = ((), (), s32[]{:S(2)}) async-start(), calls=%async_computation.47 | async-start | bytes 1671168 | tf_op jit(solution)/shard_map/all_gather | solution.py:199
  893.0 318.0 %reduce-scatter.25.cloned.1.call-start = ((), (), s32[]{:S(2)}) async-start(), calls=%async_computation.32 | async-start | bytes 1671168 | tf_op jit(solution)/shard_map/reduce_scatter | solution.py:220
  1025.0 94.5 %collective-permute-start.6 = (bf16[64,768]{1,0:T(8,128)(2,1)}, bf16[64,768]{1,0:T(8,128)(2,1)}, u32[]{:S(2)}, u32[]{:S(2)}) collective-permute-start(bf16[64,768]{1,0:T(8,128)(2,1)} %get-tuple-element.127), channel_id=1, source_target_pairs={{64,0},{65,1},{66,2},{67,3},{68,4},{69,5},{70,6},{71,7},{72,8},{73... | collective-permute-start | bytes 294920 | tf_op jit(solution)/shard_map/ppermute | solution.py:17
  1145.6 137.0 %reduce-scatter.27.cloned.1.call-start = ((), (), s32[]{:S(2)}) async-start(), calls=%async_computation.33 | async-start | bytes 1671168 | tf_op jit(solution)/shard_map/reduce_scatter | solution.py:223
  1152.0 181.2 %all-gather.71.cloned.1.call-start = ((), (), s32[]{:S(2)}) async-start(), calls=%async_computation.48 | async-start | bytes 1671168 | tf_op jit(solution)/shard_map/all_gather | solution.py:198
  1152.7 228.2 %all-gather.73.cloned.1.call-start = ((), (), s32[]{:S(2)}) async-start(), calls=%async_computation.49 | async-start | bytes 1671168 | tf_op jit(solution)/shard_map/all_gather | solution.py:199
  1153.3 321.6 %reduce-scatter.29.cloned.1.call-start = ((), (), s32[]{:S(2)}) async-start(), calls=%async_computation.34 | async-start | bytes 1671168 | tf_op jit(solution)/shard_map/reduce_scatter | solution.py:220
  1289.0 94.6 %collective-permute-start.7 = (bf16[64,768]{1,0:T(8,128)(2,1)}, bf16[64,768]{1,0:T(8,128)(2,1)}, u32[]{:S(2)}, u32[]{:S(2)}) collective-permute-start(bf16[64,768]{1,0:T(8,128)(2,1)} %get-tuple-element.125), channel_id=1, source_target_pairs={{64,0},{65,1},{66,2},{67,3},{68,4},{69,5},{70,6},{71,7},{72,8},{73... | collective-permute-start | bytes 294920 | tf_op jit(solution)/shard_map/ppermute | solution.py:17
  1409.6 137.0 %reduce-scatter.31.cloned.1.call-start = ((), (), s32[]{:S(2)}) async-start(), calls=%async_computation.35 | async-start | bytes 1671168 | tf_op jit(solution)/shard_map/reduce_scatter | solution.py:223
  1416.0 181.0 %all-gather.75.cloned.1.call-start = ((), (), s32[]{:S(2)}) async-start(), calls=%async_computation.50 | async-start | bytes 1671168 | tf_op jit(solution)/shard_map/all_gather | solution.py:198
  1416.6 228.3 %all-gather.77.cloned.1.call-start = ((), (), s32[]{:S(2)}) async-start(), calls=%async_computation.51 | async-start | bytes 1671168 | tf_op jit(solution)/shard_map/all_gather | solution.py:199
  1417.3 321.5 %reduce-scatter.33.cloned.1.call-start = ((), (), s32[]{:S(2)}) async-start(), calls=%async_computation.36 | async-start | bytes 1671168 | tf_op jit(solution)/shard_map/reduce_scatter | solution.py:220
  1552.9 94.6 %collective-permute-start.8 = (bf16[64,768]{1,0:T(8,128)(2,1)}, bf16[64,768]{1,0:T(8,128)(2,1)}, u32[]{:S(2)}, u32[]{:S(2)}) collective-permute-start(bf16[64,768]{1,0:T(8,128)(2,1)} %get-tuple-element.123), channel_id=1, source_target_pairs={{64,0},{65,1},{66,2},{67,3},{68,4},{69,5},{70,6},{71,7},{72,8},{73... | collective-permute-start | bytes 294920 | tf_op jit(solution)/shard_map/ppermute | solution.py:17
  1673.5 136.9 %reduce-scatter.35.cloned.1.call-start = ((), (), s32[]{:S(2)}) async-start(), calls=%async_computation.37 | async-start | bytes 1671168 | tf_op jit(solution)/shard_map/reduce_scatter | solution.py:223
  1679.9 181.1 %all-gather.79.cloned.1.call-start = ((), (), s32[]{:S(2)}) async-start(), calls=%async_computation.52 | async-start | bytes 1671168 | tf_op jit(solution)/shard_map/all_gather | solution.py:198
  1680.6 228.2 %all-gather.81.cloned.1.call-start = ((), (), s32[]{:S(2)}) async-start(), calls=%async_computation.53 | async-start | bytes 1671168 | tf_op jit(solution)/shard_map/all_gather | solution.py:199
  1681.3 321.5 %reduce-scatter.37.cloned.1.call-start = ((), (), s32[]{:S(2)}) async-start(), calls=%async_computation.38 | async-start | bytes 1671168 | tf_op jit(solution)/shard_map/reduce_scatter | solution.py:220
  1816.7 94.7 %collective-permute-start.9 = (bf16[64,768]{1,0:T(8,128)(2,1)}, bf16[64,768]{1,0:T(8,128)(2,1)}, u32[]{:S(2)}, u32[]{:S(2)}) collective-permute-start(bf16[64,768]{1,0:T(8,128)(2,1)} %get-tuple-element.121), channel_id=1, source_target_pairs={{64,0},{65,1},{66,2},{67,3},{68,4},{69,5},{70,6},{71,7},{72,8},{73... | collective-permute-start | bytes 294920 | tf_op jit(solution)/shard_map/ppermute | solution.py:17
  1937.5 137.1 %reduce-scatter.39.cloned.1.call-start = ((), (), s32[]{:S(2)}) async-start(), calls=%async_computation.39 | async-start | bytes 1671168 | tf_op jit(solution)/shard_map/reduce_scatter | solution.py:223
  1947.1 236.9 %reduce-scatter.43.cloned.1.call-start = ((), (), s32[]{:S(2)}) async-start(), calls=%async_computation.41 | async-start | bytes 1474560 | tf_op jit(solution)/shard_map/reduce_scatter | solution.py:256
  1974.4 209.6 %reduce-scatter.41.cloned.1.call-start = ((), (), s32[]{:S(2)}) async-start(), calls=%async_computation.40 | async-start | bytes 4423680 | tf_op jit(solution)/shard_map/reduce_scatter | solution.py:253
  2100.9 98.8 %reduce-scatter.45.cloned.1.call-start = ((), (), s32[]{:S(2)}) async-start(), calls=%async_computation.42 | async-start | bytes 5898240 | tf_op jit(solution)/shard_map/reduce_scatter | solution.py:259
  2138.2 114.9 %reduce-scatter.47.cloned.1.call-start = ((), (), s32[]{:S(2)}) async-start(), calls=%async_computation.43 | async-start | bytes 5898240 | tf_op jit(solution)/shard_map/reduce_scatter | solution.py:262
  2178.2 95.7 %reduce-scatter.49.cloned.1.call-start = ((), (), s32[]{:S(2)}) async-start(), calls=%async_computation.54 | async-start | bytes 245760
  2183.0 114.4 %reduce-scatter.51.cloned.1.call-start = ((), (), s32[]{:S(2)}) async-start(), calls=%async_computation.55 | async-start | bytes 245760
  2184.0 266.7 %all-reduce.5.cloned.1.call-start = ((), (), s32[]{:S(2)}) async-start(), calls=%async_computation.56 | async-start | bytes 7077888 | tf_op jit(solution)/shard_map/psum | solution.py:276
  (312 other events, 3210.3 us)
Sparse Core Ops, SparseCore 0:
  9.7 50.7 all-gather.34
  66.2 52.6 all-gather.36
  121.9 45.4 all-gather.38
  168.9 22.0 all-gather.40
  192.5 54.2 all-gather.42
  248.3 53.0 all-gather.44
  315.8 48.2 all-gather.48
  367.0 45.4 all-gather.46
  443.8 46.5 all-gather.52
  493.3 45.4 all-gather.50
  560.1 47.6 all-gather.56
  610.1 45.4 all-gather.54
  677.0 47.7 all-gather.60
  727.0 45.4 all-gather.58
  775.3 45.4 all-gather.64
  823.7 45.4 all-gather.62
  881.9 65.2 reduce-scatter.20
  950.8 67.8 reduce-scatter.22
  1021.1 48.0 all-gather.66
  1071.4 45.4 all-gather.68
  1145.7 65.1 reduce-scatter.24
  1214.8 67.7 reduce-scatter.26
  1285.1 48.1 all-gather.70
  1335.5 45.4 all-gather.72
  1409.8 65.1 reduce-scatter.28
  1478.7 67.8 reduce-scatter.30
  1548.8 48.0 all-gather.74
  1599.4 45.4 all-gather.76
  1673.6 65.2 reduce-scatter.32
  1742.6 67.7 reduce-scatter.34
  1812.8 48.0 all-gather.78
  1863.3 45.4 all-gather.80
  1937.6 65.1 reduce-scatter.36
  2006.7 67.8 reduce-scatter.38
  2077.6 24.1 reduce-scatter.42
  2104.1 42.3 reduce-scatter.40
  2148.8 50.8 reduce-scatter.44
  2202.2 50.8 reduce-scatter.46
  2255.9 17.9 reduce-scatter.48
  2277.0 20.3 reduce-scatter.50
  2300.2 150.4 all-reduce.4
where the time goes:
time: 2480 us; the launch traced here: 2470 us
  waiting for transfers between devices  1770 us (71%)
  matrix products  297 us (12%)
  local copies, waits for them, and re-layouts  194 us (8%)
  blocking collectives  76.6 us (3%)
  other arithmetic  65.2 us (3%)
  starting transfers between devices  36.3 us (1%)
  between operations  30.1 us (1%)
    reduce_scatter x5, waiting for transfers between devices, shards(): lax.psum_scatter(grad_values_all.astype(jnp.bfloat16), 'ctx', scatter_dim...  350 us
    dot_general x95, matrix products, cross(): jnp.einsum(pattern, left_side, right_side, preferred_element_type=jnp.flo...  297 us
    all_gather x5, waiting for transfers between devices, shards(): forward_key_all = lax.all_gather(keys_local, 'ctx', axis=0, tiled=True)  218 us
    reduce_scatter x5, waiting for transfers between devices, shards(): lax.psum_scatter(grad_keys_all.astype(jnp.bfloat16), 'ctx', scatter_dimen...  218 us
    all_gather x5, waiting for transfers between devices, shards(): forward_value_all = lax.all_gather(values_local, 'ctx', axis=0, tiled=True)  212 us
    all_gather x5, waiting for transfers between devices, shards(): lax.all_gather(picked['values_local'], 'ctx', axis=0, tiled=True)  211 us
    all_gather x5, waiting for transfers between devices, shards(): lax.all_gather(picked['keys_local'], 'ctx', axis=0, tiled=True)  208 us
    psum x1, waiting for transfers between devices, shards(): lax.psum(shares[0].astype(jnp.bfloat16), 'ctx').astype(jnp.float32)  115 us
  transfers between devices with their start and end apart: 51, of which 39 were waited for; matrix products, arithmetic and copies ran while one was open for 15% of the time, Pallas kernels for 0%

commit v1 on v0

v1 whole, which is shorter than its diff:
```python
import jax
import jax.numpy as jnp
from jax import lax
from jax.experimental import pallas as pl
from jax.experimental.pallas import tpu as pltpu
from jax.sharding import Mesh
from jax.sharding import PartitionSpec as P

HEADS = 12
HDIM = 64
GROUPS = 4
GROUP_HEADS = HEADS // GROUPS
WIDTH = GROUP_HEADS * HDIM
QUERY_BLOCK = 256
CTX = ("x", "yh", "core")

epsilon = 1e-05
neg_fill = -1e30


def dot(left_side, right_side, left_dim, right_dim):
    return lax.dot_general(
        left_side,
        right_side,
        (((left_dim,), (right_dim,)), ((), ())),
        preferred_element_type=jnp.float32,
    )


def head_columns(part, head):
    start = part * WIDTH + head * HDIM
    return slice(start, start + HDIM)


def attend_body(row_places, column_places, joined, mixed, log_total):
    rows = pl.ds(pl.multiple_of(pl.program_id(0) * QUERY_BLOCK, QUERY_BLOCK), QUERY_BLOCK)
    hidden = jnp.where(column_places[...] <= row_places[...], 0.0, neg_fill)
    parts = []
    for head in range(GROUP_HEADS):
        queries = joined[rows, head_columns(0, head)] * jnp.bfloat16(HDIM ** (-0.5))
        keys = joined[:, head_columns(1, head)]
        values = joined[:, head_columns(2, head)]
        scores = dot(keys, queries, 1, 1) + hidden
        top = jnp.max(scores, 0, keepdims=True)
        powers = jnp.exp(scores - top)
        total = jnp.sum(powers, 0, keepdims=True)
        parts.append(dot(values, powers.astype(jnp.bfloat16), 0, 0) / total)
        log_total[head : head + 1, :] = top + jnp.log(total)
    mixed[...] = jnp.concatenate(parts, 0).T.astype(jnp.bfloat16)


def attend(joined, row_places, column_places):
    count = joined.shape[0]
    return pl.pallas_call(
        attend_body,
        grid=(count // QUERY_BLOCK,),
        in_specs=[
            pl.BlockSpec((1, QUERY_BLOCK), lambda i: (0, i)),
            pl.BlockSpec((count, 1), lambda i: (0, 0)),
            pl.BlockSpec((count, 3 * WIDTH), lambda i: (0, 0)),
        ],
        out_specs=[
            pl.BlockSpec((QUERY_BLOCK, WIDTH), lambda i: (i, 0)),
            pl.BlockSpec((8, QUERY_BLOCK), lambda i: (0, i)),
        ],
        out_shape=[
            jax.ShapeDtypeStruct((count, WIDTH), jnp.bfloat16),
            jax.ShapeDtypeStruct((8, count), jnp.float32),
        ],
        compiler_params=pltpu.CompilerParams(vmem_limit_bytes=40 << 20),
        cost_estimate=pl.CostEstimate(
            flops=4 * count * count * WIDTH,
            bytes_accessed=8 * count * WIDTH,
            transcendentals=count * count * GROUP_HEADS,
        ),
    )(row_places, column_places, joined)


def attend_back_body(
    row_places, column_places, joined, grad_mixed, log_total, grad_joined, key_sums, value_sums
):
    step = pl.program_id(0)
    rows = pl.ds(pl.multiple_of(step * QUERY_BLOCK, QUERY_BLOCK), QUERY_BLOCK)

    @pl.when(step == 0)
    def _():
        key_sums[...] = jnp.zeros_like(key_sums)
        value_sums[...] = jnp.zeros_like(value_sums)

    hidden = jnp.where(column_places[...] <= row_places[...], 0.0, neg_fill)
    parts = []
    for head in range(GROUP_HEADS):
        queries = joined[rows, head_columns(0, head)] * jnp.bfloat16(HDIM ** (-0.5))
        keys = joined[:, head_columns(1, head)]
        values = joined[:, head_columns(2, head)]
        grads = grad_mixed[:, head_columns(0, head)]
        weights = jnp.exp(dot(keys, queries, 1, 1) + hidden - log_total[head : head + 1, :])
        grad_weights = dot(values, grads, 1, 1)
        inner_sum = jnp.sum(weights * grad_weights, 0, keepdims=True)
        grad_scores = (weights * (grad_weights - inner_sum)).astype(jnp.bfloat16)
        value_sums[head] += dot(weights.astype(jnp.bfloat16), grads, 1, 0)
        key_sums[head] += dot(grad_scores, queries, 1, 0)
        parts.append(dot(keys, grad_scores, 0, 0) * (HDIM ** (-0.5)))
    grad_joined[rows, :WIDTH] = jnp.concatenate(parts, 0).T.astype(jnp.bfloat16)

    @pl.when(step == pl.num_programs(0) - 1)
    def _():
        for head in range(GROUP_HEADS):
            grad_joined[:, head_columns(1, head)] = key_sums[head].astype(jnp.bfloat16)
            grad_joined[:, head_columns(2, head)] = value_sums[head].astype(jnp.bfloat16)


def attend_back(joined, grad_mixed, log_total, row_places, column_places):
    count = joined.shape[0]
    return pl.pallas_call(
        attend_back_body,
        grid=(count // QUERY_BLOCK,),
        in_specs=[
            pl.BlockSpec((1, QUERY_BLOCK), lambda i: (0, i)),
            pl.BlockSpec((count, 1), lambda i: (0, 0)),
            pl.BlockSpec((count, 3 * WIDTH), lambda i: (0, 0)),
            pl.BlockSpec((QUERY_BLOCK, WIDTH), lambda i: (i, 0)),
            pl.BlockSpec((8, QUERY_BLOCK), lambda i: (0, i)),
        ],
        out_specs=pl.BlockSpec((count, 3 * WIDTH), lambda i: (0, 0)),
        out_shape=jax.ShapeDtypeStruct((count, 3 * WIDTH), jnp.bfloat16),
        scratch_shapes=[
            pltpu.VMEM((GROUP_HEADS, count, HDIM), jnp.float32),
            pltpu.VMEM((GROUP_HEADS, count, HDIM), jnp.float32),
        ],
        compiler_params=pltpu.CompilerParams(vmem_limit_bytes=40 << 20),
        cost_estimate=pl.CostEstimate(
            flops=10 * count * count * WIDTH,
            bytes_accessed=16 * count * WIDTH,
            transcendentals=count * count * GROUP_HEADS,
        ),
    )(row_places, column_places, joined, grad_mixed, log_total)


def cross(left_side, right_side, pattern):
    return jnp.einsum(pattern, left_side, right_side, preferred_element_type=jnp.float32)


def normalize(values, gain_row, shift_row):
    center = values - jnp.mean(values, -1, keepdims=True)
    spread = lax.rsqrt(jnp.mean(center * center, -1, keepdims=True) + epsilon)
    unit_rows = center * spread
    return (unit_rows * gain_row + shift_row, unit_rows, spread)


def normalize_back(grad_out, unit_rows, spread, gain_row):
    grad_unit = grad_out * gain_row
    grad_in = spread * (
        grad_unit
        - jnp.mean(grad_unit, -1, keepdims=True)
        - unit_rows * jnp.mean(grad_unit * unit_rows, -1, keepdims=True)
    )
    return (grad_in, jnp.sum(grad_out * unit_rows, 0), jnp.sum(grad_out, 0))


def positions(block_table, block_len):
    offsets = jnp.arange(block_len, dtype=jnp.int32)
    return (block_table[:, None] * block_len + offsets[None, :]).reshape(-1)


def to_heads(rows, micro_count, parts):
    local = rows.shape[0] // micro_count
    split = rows.reshape(micro_count, local, parts, GROUPS, WIDTH).transpose(0, 3, 1, 2, 4)
    split = split.reshape(micro_count * GROUPS, local, parts * WIDTH)
    return lax.all_to_all(split, CTX, 0, 0, tiled=True).reshape(-1, parts * WIDTH)


def from_heads(columns, micro_count, parts):
    members = micro_count * GROUPS
    local = columns.shape[0] // members
    split = lax.all_to_all(columns.reshape(members, local, parts * WIDTH), CTX, 0, 0, tiled=True)
    split = split.reshape(micro_count, GROUPS, local, parts, WIDTH).transpose(0, 2, 3, 1, 4)
    return split.reshape(micro_count * local, parts * GROUPS * WIDTH)


def gather_weight(weight):
    return lax.all_gather(weight[0], "fsdp", axis=0, tiled=True)


def scatter_grad(grad):
    share = lax.psum_scatter(grad.astype(jnp.bfloat16), "fsdp", scatter_dimension=0, tiled=True)
    return lax.psum(share, CTX).astype(jnp.float32)[None]


def shards(
    inputs,
    cotangent,
    plan,
    block_table,
    attn_in,
    attn_out,
    mlp_in,
    mlp_out,
    norm_gains,
    biases,
    mlp_bias,
):
    shard = norm_gains.shape[2]
    small = jnp.concatenate([norm_gains[0], biases[0], mlp_bias.reshape(-1, shard)], 0)
    small_all = lax.all_gather(small, "fsdp", axis=0).astype(jnp.float32)
    w_qkv = gather_weight(attn_in)
    w_out = gather_weight(attn_out)
    w_up = gather_weight(mlp_in)
    w_down = gather_weight(mlp_out)
    model_width = w_out.shape[0]
    vector_rows = small_all[:, :8].transpose(1, 0, 2).reshape(8, model_width)
    gain_rows, bias_rows = vector_rows[:2], vector_rows[2:]
    up_bias = small_all[:, 8:].reshape(-1)
    qkv_bias = jnp.concatenate([bias_rows[1], jnp.zeros_like(bias_rows[1]), bias_rows[2]])

    micro_count, _, local_rows, _ = inputs.shape
    rows = micro_count * local_rows
    section_id = lax.axis_index("section")
    sections = lax.axis_size("section")
    places = positions(block_table, local_rows // 2)
    row_places, column_places = places[None, :], places[:, None]
    fresh = jnp.stack(
        [lax.dynamic_index_in_dim(inputs, plan[step], 0, keepdims=False) for step in range(micro_count)]
    ).reshape(rows, model_width)
    top_grad = cotangent.reshape(rows, model_width)

    def forward(entering):
        stream = entering.astype(jnp.float32)
        normed, unit_one, spread_one = normalize(stream, gain_rows[0], bias_rows[0])
        normed_low = normed.astype(jnp.bfloat16)
        joined = (cross(normed_low, w_qkv, "td,de->te") + qkv_bias).astype(jnp.bfloat16)
        joined_heads = to_heads(joined, micro_count, 3)
        mixed_heads, log_total = attend(joined_heads, row_places, column_places)
        mixed = from_heads(mixed_heads, micro_count, 1)
        middle = stream + (cross(mixed, w_out, "td,de->te") + bias_rows[3])
        normed_two, unit_two, spread_two = normalize(middle, gain_rows[1], bias_rows[4])
        normed_two_low = normed_two.astype(jnp.bfloat16)
        hidden_pre = cross(normed_two_low, w_up, "td,df->tf") + up_bias
        active_low = jax.nn.gelu(hidden_pre).astype(jnp.bfloat16)
        result = (middle + (cross(active_low, w_down, "tf,fd->td") + bias_rows[5])).astype(
            jnp.bfloat16
        )
        saved = (
            unit_one,
            spread_one,
            normed_low,
            joined_heads,
            log_total,
            mixed,
            unit_two,
            spread_two,
            normed_two_low,
            hidden_pre,
            active_low,
        )
        return result, saved

    def backward(grad_low, saved):
        (
            unit_one,
            spread_one,
            normed_low,
            joined_heads,
            log_total,
            mixed,
            unit_two,
            spread_two,
            normed_two_low,
            hidden_pre,
            active_low,
        ) = saved
        grad_top = grad_low.astype(jnp.float32)
        d_down = cross(active_low, grad_low, "tf,td->fd")
        d_shift_out = jnp.sum(grad_top, 0)
        grad_active = cross(grad_low, w_down, "td,fd->tf")
        _, gelu_pull = jax.vjp(jax.nn.gelu, hidden_pre)
        grad_hidden = gelu_pull(grad_active)[0].astype(jnp.bfloat16)
        d_up = cross(normed_two_low, grad_hidden, "td,tf->df")
        d_up_bias = jnp.sum(grad_hidden.astype(jnp.float32), 0)
        grad_normed_two = cross(grad_hidden, w_up, "tf,df->td")
        grad_norm_two, d_gain_two, d_shift_two = normalize_back(
            grad_normed_two, unit_two, spread_two, gain_rows[1]
        )
        grad_middle = grad_top + grad_norm_two
        grad_attn = grad_middle.astype(jnp.bfloat16)
        d_out = cross(mixed, grad_attn, "td,te->de")
        d_shift_attn = jnp.sum(grad_attn.astype(jnp.float32), 0)
        grad_mixed = cross(grad_attn, w_out, "te,de->td").astype(jnp.bfloat16)
        grad_mixed_heads = to_heads(grad_mixed, micro_count, 1)
        grad_heads = attend_back(
            joined_heads, grad_mixed_heads, log_total, row_places, column_places
        )
        grad_joined = from_heads(grad_heads, micro_count, 3)
        d_qkv = cross(normed_low, grad_joined, "td,te->de")
        joined_sums = jnp.sum(grad_joined.astype(jnp.float32), 0)
        grad_normed = cross(grad_joined, w_qkv, "te,de->td")
        grad_norm_one, d_gain_one, d_shift_one = normalize_back(
            grad_normed, unit_one, spread_one, gain_rows[0]
        )
        grad_in = (grad_middle + grad_norm_one).astype(jnp.bfloat16)
        vectors = jnp.stack(
            [
                d_gain_one,
                d_gain_two,
                d_shift_one,
                joined_sums[:model_width],
                joined_sums[2 * model_width :],
                d_shift_attn,
                d_shift_two,
                d_shift_out,
            ]
        )
        return grad_in, (d_qkv, d_out, d_up, d_down, vectors, d_up_bias)

    forward_pairs = [(i, i + 1) for i in range(sections - 1)]
    entering = fresh
    for _ in range(sections - 1):
        result, _ = forward(entering)
        received = lax.ppermute(result, "section", forward_pairs)
        entering = jnp.where(section_id == 0, fresh, received)
    layer_out, saved = forward(entering)

    back_pairs = [(i + 1, i) for i in range(sections - 1)]
    grad_low = top_grad
    for _ in range(sections - 1):
        result, _ = backward(grad_low, saved)
        received = lax.ppermute(result, "section", back_pairs)
        grad_low = jnp.where(section_id == sections - 1, top_grad, received)
    input_grad, (d_qkv, d_out, d_up, d_down, vectors, d_up_bias) = backward(grad_low, saved)

    vector_grads = jnp.concatenate([vectors, d_up_bias.reshape(-1, model_width)], 0)
    vector_grads = lax.psum(vector_grads, CTX + ("fsdp",))
    fsdp_id = lax.axis_index("fsdp")
    own_vectors = lax.dynamic_slice_in_dim(vector_grads[:8], fsdp_id * shard, shard, 1)
    up_len = mlp_bias.shape[1]
    own_up_bias = lax.dynamic_slice_in_dim(vector_grads[8:].reshape(-1), fsdp_id * up_len, up_len, 0)
    out_shape = (1, micro_count, 1, local_rows, model_width)
    return (
        layer_out.reshape(out_shape),
        input_grad.reshape(out_shape),
        scatter_grad(d_qkv),
        scatter_grad(d_out),
        scatter_grad(d_up),
        scatter_grad(d_down),
        own_vectors[None, :2],
        own_vectors[None, 2:],
        own_up_bias[None],
    )


def solution(mesh):
    fine = Mesh(
        mesh.devices.reshape(2, 4, 2, 2, 4), ("section", "x", "yh", "core", "fsdp")
    )
    rows = P(None, "fsdp", CTX, None)
    weight = P("section", "fsdp", None)
    vector = P("section", None, "fsdp")
    row = P("section", "fsdp")
    out_rows = P("section", None, "fsdp", CTX, None)
    return jax.shard_map(
        shards,
        mesh=fine,
        in_specs=(rows, rows, P(), P(), weight, weight, weight, weight, vector, vector, row),
        out_specs=(out_rows, out_rows, weight, weight, weight, weight, vector, vector, row),
        check_vma=False,
    )
```

time: 2480 us -> 984 us (0.40)
  waiting for transfers between devices: 1770 us -> 278 us
  blocking collectives: 76.6 us -> 453 us
  matrix products: 297 us -> 79.3 us
  local copies, waits for them, and re-layouts: 194 us -> 57.6 us
  other arithmetic: 65.2 us -> 15.7 us
  Pallas kernels: 0 us -> 42.4 us
    all_gather x24 -> x4, waiting for transfers between devices: 970 us -> 94.7 us  [gather_weight(): return lax.all_gather(weight[0], 'fsdp', axis=0, tiled=True)]
    reduce_scatter x14 -> x4, waiting for transfers between devices: 637 us -> 132 us  [scatter_grad(): lax.psum_scatter(grad.astype(jnp.bfloat16), 'fsdp', scatter_dimension=0,...]
    psum x1, blocking collectives: 36 us -> 319 us  [shards(): vector_grads = lax.psum(vector_grads, CTX + ('fsdp',))]
    dot_general x95 -> x18, matrix products: 297 us -> 79.3 us  [cross(): jnp.einsum(pattern, left_side, right_side, preferred_element_type=jnp.flo...]
    all_to_all x0 -> x6, blocking collectives: none -> 122 us  [the longest x3 63.5 us: from_heads(): lax.all_to_all(columns.reshape(members, local, parts * WIDTH), CTX, 0, 0,...]
    psum x1, waiting for transfers between devices: 115 us -> 0.01 us  [scatter_grad(): return lax.psum(share, CTX).astype(jnp.float32)[None]]
    unnamed x645 -> x32, local copies, waits for them, and re-layouts: 53.6 us -> 1.83 us
    all_gather x20 -> x0, local copies, waits for them, and re-layouts: 43.1 us -> none  [the longest x5 12.9 us: shards(): lax.all_gather(picked['keys_local'], 'ctx', axis=0, tiled=True)]
  transfers between devices with their start and end apart: 51 -> 13, of which waited for: 39 -> 10; matrix products, arithmetic and copies ran while one was open for 15% -> 7% of each run, Pallas kernels for 0% -> 2%
where the time goes in v1:
time: 984 us; the launch traced here: 966 us
  blocking collectives  453 us (46%)
  waiting for transfers between devices  278 us (28%)
  matrix products  79.3 us (8%)
  local copies, waits for them, and re-layouts  57.6 us (6%)
  Pallas kernels  42.4 us (4%)
  between operations  22.5 us (2%)
  starting transfers between devices  17.3 us (2%)
  other arithmetic  15.7 us (2%)
    psum x1, blocking collectives, shards(): vector_grads = lax.psum(vector_grads, CTX + ('fsdp',))  319 us
    reduce_scatter x4, waiting for transfers between devices, scatter_grad(): lax.psum_scatter(grad.astype(jnp.bfloat16), 'fsdp', scatter_dimension=0,...  132 us
    all_gather x4, waiting for transfers between devices, gather_weight(): return lax.all_gather(weight[0], 'fsdp', axis=0, tiled=True)  94.7 us
    dot_general x18, matrix products, cross(): jnp.einsum(pattern, left_side, right_side, preferred_element_type=jnp.flo...  79.3 us
    all_to_all x3, blocking collectives, from_heads(): lax.all_to_all(columns.reshape(members, local, parts * WIDTH), CTX, 0, 0,...  63.5 us
    all_to_all x3, blocking collectives, to_heads(): lax.all_to_all(split, CTX, 0, 0, tiled=True).reshape(-1, parts * WIDTH)  58.5 us
    pallas_call x2, Pallas kernels, attend_back(): pl.pallas_call(attend_back_body, grid=(count // QUERY_BLOCK,), in_specs=[...  24 us
  transfers between devices with their start and end apart: 13, of which 10 were waited for; matrix products, arithmetic and copies ran while one was open for 7% of the time, Pallas kernels for 2%

profile of v1, /device:TPU:1, one launch (start us, length us, event | category | flops | bytes accessed | tf_op | source)
XLA Modules:
  0.0 966.2 jit_solution(11999334169851201411)
XLA Ops:
  19.1 11.8 %all-gather.5 = bf16[4,12,192]{2,1,0:T(8,128)(2,1)S(1)} all-gather(bf16[1,12,192]{2,1,0:T(8,128)(2,1)S(1)} %maximum_bitcast_fusion), channel_id=2, replica_groups=mesh['section'=2,'x'=4,'yh'=2,'core'=2,'fsdp'=4] {'fsdp'}, dimensions={0}, use_global_device_ids=true | all-gather | bytes 23040 | tf_op jit(solution)/shard_map/all_gather | solution.py:205
  31.4 24.7 %all-gather.11.cloned.1.call-done = bf16[1,768,2304]{2,1,0:T(8,128)(2,1)} async-done(((bf16[1,192,2304]{2,1,0:T(8,128)(2,1)}), bf16[1,768,2304]{2,1,0:T(8,128)(2,1)}) %all-gather.11.cloned.1.call-update) | async-done | bytes 3538960 | tf_op jit(solution)/shard_map/all_gather | solution.py:182
  56.1 3.2 fusion.22
  64.0 2.7 reshape.361
  66.7 7.5 all-to-all-start
  74.9 19.3 %all-to-all-done = bf16[16,64,576]{2,1,0:T(8,128)(2,1)S(1)} async-done(((bf16[16,64,576]{2,1,0:T(8,128)(2,1)}), bf16[16,64,576]{2,1,0:T(8,128)(2,1)S(1)}, u32[]{:S(2)}, u32[]{:S(2)}) %all-to-all-start) | async-done | bytes 1179680 | tf_op jit(solution)/shard_map/all_to_all | solution.py:170
  94.2 9.5 shard_map.178
  103.8 4.4 all-to-all-start.1
  108.7 10.7 %all-to-all-done.1 = bf16[16,64,192]{2,1,0:T(8,128)(2,1)S(1)} async-done(((bf16[16,64,192]{2,1,0:T(8,128)(2,1)}), bf16[16,64,192]{2,1,0:T(8,128)(2,1)S(1)}, u32[]{:S(2)}, u32[]{:S(2)}) %all-to-all-start.1) | async-done | bytes 393248 | tf_op jit(solution)/shard_map/all_to_all | solution.py:176
  122.3 15.3 %all-gather.15.cloned.1.call-done = bf16[1,768,3072]{2,1,0:T(8,128)(2,1)} async-done(((bf16[1,192,3072]{2,1,0:T(8,128)(2,1)}), bf16[1,768,3072]{2,1,0:T(8,128)(2,1)}) %all-gather.15.cloned.1.call-update) | async-done | bytes 4718608 | tf_op jit(solution)/shard_map/all_gather | solution.py:182
  137.6 54.7 %all-gather.17.cloned.1.call-done = bf16[1,3072,768]{2,1,0:T(8,128)(2,1)} async-done(((bf16[1,768,768]{2,1,0:T(8,128)(2,1)}), bf16[1,3072,768]{2,1,0:T(8,128)(2,1)}) %all-gather.17.cloned.1.call-update) | async-done | bytes 4718608 | tf_op jit(solution)/shard_map/all_gather | solution.py:182
  192.3 6.8 fusion.73
  199.1 3.5 collective-permute-start
  202.6 7.4 collective-permute-done
  210.5 4.2 fusion.23
  214.7 3.5 reshape.366
  220.4 5.1 reshape.367
  225.5 28.1 %all_to_all.40 = bf16[16,64,576]{2,1,0:T(8,128)(2,1)S(1)} all-to-all(bf16[16,64,576]{2,1,0:T(8,128)(2,1)} %reshape.367), channel_id=1, replica_groups=mesh['section'=2,'x'=4,'yh'=2,'core'=2,'fsdp'=4] {'x','yh','core'}, dimensions={0} | all-to-all | bytes 2359296 | tf_op jit(solution)/shard_map/all_to_all | solution.py:170
  253.6 8.8 shard_map.179
  262.5 14.0 %all_to_all.41 = bf16[16,64,192]{2,1,0:T(8,128)(2,1)S(1)} all-to-all(bf16[16,64,192]{2,1,0:T(8,128)(2,1)S(1)} %bitcast.162), channel_id=1, replica_groups=mesh['section'=2,'x'=4,'yh'=2,'core'=2,'fsdp'=4] {'x','yh','core'}, dimensions={0} | all-to-all | bytes 786432 | tf_op jit(solution)/shard_map/all_to_all | solution.py:176
  279.4 5.5 fusion.19
  284.9 9.4 fusion.141
  301.5 15.0 %all_to_all.42 = bf16[16,64,192]{2,1,0:T(8,128)(2,1)S(1)} all-to-all(bf16[16,64,192]{2,1,0:T(8,128)(2,1)S(1)} %bitcast.174), channel_id=1, replica_groups=mesh['section'=2,'x'=4,'yh'=2,'core'=2,'fsdp'=4] {'x','yh','core'}, dimensions={0} | all-to-all | bytes 786432 | tf_op jit(solution)/shard_map/all_to_all | solution.py:170
  316.6 12.0 %shard_map.180 = bf16[1024,576]{1,0:T(8,128)(2,1)S(1)} custom-call(s32[1,1024]{1,0:T(1,128)S(1)} %add.246.row_places, s32[1024,1]{1,0:T(8,128)S(1)} %add.289.column_places, bf16[1024,576]{1,0:T(8,128)(2,1)S(1)} %bitcast.156, bf16[1024,192]{1,0:T(8,128)(2,1)S(1)} %bitcast.163, f32[8,1024]{1,0:T(8,128)S(1)} %get-tuple-element.14.log_total), custom_call_target="tpu_custom_call" | custom-call | flops 2013265920 | bytes 3145728 | tf_op jit(solution)/shard_map/pallas_call | solution.py:115
  328.6 24.8 %all_to_all.43 = bf16[16,64,576]{2,1,0:T(8,128)(2,1)} all-to-all(bf16[16,64,576]{2,1,0:T(8,128)(2,1)S(1)} %bitcast.160), channel_id=1, replica_groups=mesh['section'=2,'x'=4,'yh'=2,'core'=2,'fsdp'=4] {'x','yh','core'}, dimensions={0} | all-to-all | bytes 2359296 | tf_op jit(solution)/shard_map/all_to_all | solution.py:176
  353.4 5.3 reshape.378
  358.7 4.8 copy.60
  363.4 4.0 reshape.379
  367.4 3.7 fusion.140
  373.4 11.2 %collective-permute-done.1 = bf16[256,768]{1,0:T(8,128)(2,1)} collective-permute-done((bf16[256,768]{1,0:T(8,128)(2,1)}, bf16[256,768]{1,0:T(8,128)(2,1)}, u32[]{:S(2)}, u32[]{:S(2)}) %collective-permute-start.1) | collective-permute-done | bytes 393248 | tf_op jit(solution)/shard_map/ppermute | solution.py:327
  385.9 7.0 convert_reduce_fusion.1
  392.9 4.6 multiply_reduce_fusion
  404.8 15.4 %all_to_all.44 = bf16[16,64,192]{2,1,0:T(8,128)(2,1)S(1)} all-to-all(bf16[16,64,192]{2,1,0:T(8,128)(2,1)S(1)} %bitcast.175), channel_id=1, replica_groups=mesh['section'=2,'x'=4,'yh'=2,'core'=2,'fsdp'=4] {'x','yh','core'}, dimensions={0} | all-to-all | bytes 786432 | tf_op jit(solution)/shard_map/all_to_all | solution.py:170
  420.2 12.0 %shard_map.181 = bf16[1024,576]{1,0:T(8,128)(2,1)S(1)} custom-call(s32[1,1024]{1,0:T(1,128)S(1)} %add.246.row_places, s32[1024,1]{1,0:T(8,128)S(1)} %add.289.column_places, bf16[1024,576]{1,0:T(8,128)(2,1)S(1)} %bitcast.157, bf16[1024,192]{1,0:T(8,128)(2,1)S(1)} %bitcast.161, f32[8,1024]{1,0:T(8,128)S(1)} %get-tuple-element.14.log_total), custom_call_target="tpu_custom_call" | custom-call | flops 2013265920 | bytes 3145728 | tf_op jit(solution)/shard_map/pallas_call | solution.py:115
  432.2 24.6 %all_to_all.45 = bf16[16,64,576]{2,1,0:T(8,128)(2,1)} all-to-all(bf16[16,64,576]{2,1,0:T(8,128)(2,1)S(1)} %bitcast.159), channel_id=1, replica_groups=mesh['section'=2,'x'=4,'yh'=2,'core'=2,'fsdp'=4] {'x','yh','core'}, dimensions={0} | all-to-all | bytes 2359296 | tf_op jit(solution)/shard_map/all_to_all | solution.py:176
  456.8 4.3 reshape.384
  461.2 3.2 copy.63
  464.3 4.0 reshape.385
  468.3 4.3 convolution_convert_fusion.2
  472.7 6.4 convolution_convert_fusion
  479.4 5.2 convolution_convert_fusion.1
  484.7 25.8 %reduce-scatter.5.cloned.1.call-done = bf16[192,2304]{1,0:T(8,128)(2,1)} async-done(((bf16[768,2304]{1,0:T(8,128)(2,1)}), bf16[192,2304]{1,0:T(8,128)(2,1)}) %reduce-scatter.5.cloned.1.call-update) | async-done | bytes 884752 | tf_op jit(solution)/shard_map/reduce_scatter | solution.py:186
  510.5 53.3 %reduce-scatter.11.cloned.1.call-done = bf16[768,768]{1,0:T(8,128)(2,1)} async-done(((bf16[3072,768]{1,0:T(8,128)(2,1)}), bf16[768,768]{1,0:T(8,128)(2,1)}) %reduce-scatter.11.cloned.1.call-update) | async-done | bytes 1179664 | tf_op jit(solution)/shard_map/reduce_scatter | solution.py:186
  563.8 53.3 %reduce-scatter.9.cloned.1.call-done = bf16[192,3072]{1,0:T(8,128)(2,1)} async-done(((bf16[768,3072]{1,0:T(8,128)(2,1)}), bf16[192,3072]{1,0:T(8,128)(2,1)}) %reduce-scatter.9.cloned.1.call-update) | async-done | bytes 1179664 | tf_op jit(solution)/shard_map/reduce_scatter | solution.py:186
  617.2 6.0 fusion.70
  623.2 4.5 fusion.104
  629.0 319.2 %psum.39 = f32[12,768]{1,0:T(8,128)S(1)} all-reduce(f32[12,768]{1,0:T(8,128)S(1)} %concatenate.20), channel_id=1, replica_groups=mesh['section'=2,'x'=4,'yh'=2,'core'=2,'fsdp'=4] {'x','yh','core','fsdp'}, use_global_device_ids=true, to_apply=%region_32.33 | all-reduce | flops 9216 | bytes 73728 | tf_op jit(solution)/shard_map/psum | solution.py:332
  952.3 3.1 broadcast_in_dim.62
  (145 shorter events, 46.7 us)
Async XLA Ops:
  7.2 2.8 copy-start.11
  7.2 11.2 %copy-start.9 = (bf16[4,1,64,768]{3,2,1,0:T(8,128)(2,1)S(1)}, bf16[4,1,64,768]{3,2,1,0:T(8,128)(2,1)}, u32[]{:S(2)}) copy-start(bf16[4,1,64,768]{3,2,1,0:T(8,128)(2,1)} %param.11) | copy-start | bytes 1179652
  7.2 11.8 %copy-start.13 = (bf16[1,768]{1,0:T(2,128)(2,1)S(1)}, bf16[1,768]{1,0:T(2,128)(2,1)}, u32[]{:S(2)}) copy-start(bf16[1,768]{1,0:T(2,128)(2,1)} %param.21) | copy-start | bytes 4612
  7.2 11.9 %copy-start.14 = (bf16[1,2,192]{2,1,0:T(2,128)(2,1)S(1)}, bf16[1,2,192]{2,1,0:T(2,128)(2,1)}, u32[]{:S(2)}) copy-start(bf16[1,2,192]{2,1,0:T(2,128)(2,1)} %param.19) | copy-start | bytes 2308
  7.2 11.9 %copy-start.12 = (bf16[1,6,192]{2,1,0:T(8,128)(2,1)S(1)}, bf16[1,6,192]{2,1,0:T(8,128)(2,1)}, u32[]{:S(2)}) copy-start(bf16[1,6,192]{2,1,0:T(8,128)(2,1)} %param.20) | copy-start | bytes 6916
  7.2 48.9 %all-gather.11.cloned.1.call-start = ((), (), s32[]{:S(2)}) async-start(), calls=%async_computation.16 | async-start | bytes 4423680 | tf_op jit(solution)/shard_map/all_gather | solution.py:182
  8.0 112.3 %all-gather.13.cloned.1.call-start = ((), (), s32[]{:S(2)}) async-start(), calls=%async_computation.17 | async-start | bytes 1474560 | tf_op jit(solution)/shard_map/all_gather | solution.py:182
  8.7 128.9 %all-gather.15.cloned.1.call-start = ((), (), s32[]{:S(2)}) async-start(), calls=%async_computation.18 | async-start | bytes 5898240 | tf_op jit(solution)/shard_map/all_gather | solution.py:182
  9.4 182.8 %all-gather.17.cloned.1.call-start = ((), (), s32[]{:S(2)}) async-start(), calls=%async_computation.19 | async-start | bytes 5898240 | tf_op jit(solution)/shard_map/all_gather | solution.py:182
  64.0 10.2 %copy-start.15 = (s32[32]{0:T(128)S(1)}, s32[32]{0:T(128)}, u32[]{:S(2)}) copy-start(s32[32]{0:T(128)} %param.14) | copy-start | bytes 388
  66.7 27.5 %all-to-all-start = ((bf16[16,64,576]{2,1,0:T(8,128)(2,1)}), bf16[16,64,576]{2,1,0:T(8,128)(2,1)S(1)}, u32[]{:S(2)}, u32[]{:S(2)}) async-start(bf16[16,64,576]{2,1,0:T(8,128)(2,1)} %reshape.361), calls=%async_computation | async-start | bytes 2621440 | tf_op jit(solution)/shard_map/all_to_all | solution.py:170
  103.8 15.6 %all-to-all-start.1 = ((bf16[16,64,192]{2,1,0:T(8,128)(2,1)}), bf16[16,64,192]{2,1,0:T(8,128)(2,1)S(1)}, u32[]{:S(2)}, u32[]{:S(2)}) async-start(bf16[16,64,192]{2,1,0:T(8,128)(2,1)} %bitcast.12), calls=%async_computation.1 | async-start | bytes 1048576 | tf_op jit(solution)/shard_map/all_to_all | solution.py:176
  108.2 376.5 %reduce-scatter.7.cloned.1.call-start = ((), (), s32[]{:S(2)}) async-start(), calls=%async_computation.13 | async-start | bytes 1474560 | tf_op jit(solution)/shard_map/reduce_scatter | solution.py:186
  199.1 10.9 %collective-permute-start = (bf16[256,768]{1,0:T(8,128)(2,1)S(1)}, bf16[256,768]{1,0:T(8,128)(2,1)S(1)}, u32[]{:S(2)}, u32[]{:S(2)}) collective-permute-start(bf16[256,768]{1,0:T(8,128)(2,1)S(1)} %fusion.73), channel_id=1, source_target_pairs={{0,64},{1,65},{2,66},{3,67},{4,68},{5,69},{6,70},{7,71},{8,72},{9,... | collective-permute-start | bytes 1179656 | tf_op jit(solution)/shard_map/ppermute | solution.py:319
  294.4 2.5 copy-start
  296.0 0.9 copy-start.3
  367.4 3.7 copy-start.4
  372.2 12.5 %collective-permute-start.1 = (bf16[256,768]{1,0:T(8,128)(2,1)}, bf16[256,768]{1,0:T(8,128)(2,1)}, u32[]{:S(2)}, u32[]{:S(2)}) collective-permute-start(bf16[256,768]{1,0:T(8,128)(2,1)} %fusion.98), channel_id=1, source_target_pairs={{64,0},{65,1},{66,2},{67,3},{68,4},{69,5},{70,6},{71,7},{72,8},{73... | collective-permute-start | bytes 1179656 | tf_op jit(solution)/shard_map/ppermute | solution.py:327
  385.9 11.6 %copy-start.5 = (bf16[256,768]{1,0:T(8,128)(2,1)}, bf16[256,768]{1,0:T(8,128)(2,1)S(1)}, u32[]{:S(2)}) copy-start(bf16[256,768]{1,0:T(8,128)(2,1)S(1)} %get-tuple-element.78) | copy-start | bytes 1179652
  392.9 4.6 copy-start.6
  397.9 0.9 copy-start.1
  400.3 110.1 %reduce-scatter.5.cloned.1.call-start = ((), (), s32[]{:S(2)}) async-start(), calls=%async_computation.12 | async-start | bytes 4423680 | tf_op jit(solution)/shard_map/reduce_scatter | solution.py:186
  472.6 91.2 %reduce-scatter.11.cloned.1.call-start = ((), (), s32[]{:S(2)}) async-start(), calls=%async_computation.15 | async-start | bytes 5898240 | tf_op jit(solution)/shard_map/reduce_scatter | solution.py:186
  479.1 138.1 %reduce-scatter.9.cloned.1.call-start = ((), (), s32[]{:S(2)}) async-start(), calls=%async_computation.14 | async-start | bytes 5898240 | tf_op jit(solution)/shard_map/reduce_scatter | solution.py:186
  484.6 467.7 %all-reduce.3.cloned.1.call-start = ((), (), s32[]{:S(2)}) async-start(), calls=%async_computation.20 | async-start | bytes 7077888 | tf_op jit(solution)/shard_map/psum | solution.py:187
  623.2 326.9 %copy-start.2 = (f32[256,768]{1,0:T(8,128)S(1)}, f32[256,768]{1,0:T(8,128)}, u32[]{:S(2)}) copy-start(f32[256,768]{1,0:T(8,128)} %copy-done.1) | copy-start | bytes 2359300
  952.3 3.1 copy-start.7
  952.3 4.7 copy-start.8
  955.4 2.9 copy-start.10
Sparse Core Ops, SparseCore 0:
  9.7 46.3 all-gather.10
  57.8 23.8 all-gather.12
  83.4 54.2 all-gather.14
  139.1 53.0 all-gather.16
  400.5 20.3 reduce-scatter.6
  472.8 37.6 reduce-scatter.4
  512.9 50.8 reduce-scatter.10
  566.2 50.8 reduce-scatter.8
  619.9 148.1 all-reduce.2

commit v2 on v1

--- a/solution.py
+++ b/solution.py
@@ -12,6 +12,7 @@
 GROUP_HEADS = HEADS // GROUPS
 WIDTH = GROUP_HEADS * HDIM
 QUERY_BLOCK = 256
+EXTRA = 16
 CTX = ("x", "yh", "core")
 
 epsilon = 1e-05
@@ -179,12 +180,33 @@
 
 
 def gather_weight(weight):
-    return lax.all_gather(weight[0], "fsdp", axis=0, tiled=True)
+    half = weight.shape[1] // 2
+    own = lax.dynamic_slice_in_dim(weight[0], lax.axis_index("core") * half, half, 0)
+    return lax.all_gather(own, ("fsdp", "core"), axis=0, tiled=True)
+
+
+def gather_small(value):
+    count = lax.axis_size("fsdp")
+    place = lax.axis_index("fsdp")
+    whole = jnp.zeros((count,) + value.shape, value.dtype)
+    for shift in range(count):
+        pairs = [(source, (source + shift) % count) for source in range(count)]
+        member = lax.ppermute(value, "fsdp", pairs) if shift else value
+        whole = lax.dynamic_update_index_in_dim(whole, member, (place - shift) % count, 0)
+    return whole
 
 
 def scatter_grad(grad):
-    share = lax.psum_scatter(grad.astype(jnp.bfloat16), "fsdp", scatter_dimension=0, tiled=True)
-    return lax.psum(share, CTX).astype(jnp.float32)[None]
+    return lax.psum_scatter(grad, ("fsdp", "core"), scatter_dimension=0, tiled=True)
+
+
+def finish_grad(share, axes):
+    total = lax.psum(share, axes)
+    other = lax.ppermute(total, "core", [(0, 1), (1, 0)])
+    first = lax.axis_index("core") == 0
+    return jnp.stack([jnp.where(first, total, other), jnp.where(first, other, total)]).astype(
+        jnp.float32
+    )
 
 
 def shards(
@@ -202,7 +224,7 @@
 ):
     shard = norm_gains.shape[2]
     small = jnp.concatenate([norm_gains[0], biases[0], mlp_bias.reshape(-1, shard)], 0)
-    small_all = lax.all_gather(small, "fsdp", axis=0).astype(jnp.float32)
+    small_all = gather_small(small).astype(jnp.float32)
     w_qkv = gather_weight(attn_in)
     w_out = gather_weight(attn_out)
     w_up = gather_weight(mlp_in)
@@ -286,6 +308,10 @@
         d_out = cross(mixed, grad_attn, "td,te->de")
         d_shift_attn = jnp.sum(grad_attn.astype(jnp.float32), 0)
         grad_mixed = cross(grad_attn, w_out, "te,de->td").astype(jnp.bfloat16)
+        d_down, d_up, d_out = (value.astype(jnp.bfloat16) for value in (d_down, d_up, d_out))
+        grad_mixed, d_down, d_up, d_out = lax.optimization_barrier(
+            (grad_mixed, d_down, d_up, d_out)
+        )
         grad_mixed_heads = to_heads(grad_mixed, micro_count, 1)
         grad_heads = attend_back(
             joined_heads, grad_mixed_heads, log_total, row_places, column_places
@@ -328,20 +354,34 @@
         grad_low = jnp.where(section_id == sections - 1, top_grad, received)
     input_grad, (d_qkv, d_out, d_up, d_down, vectors, d_up_bias) = backward(grad_low, saved)
 
-    vector_grads = jnp.concatenate([vectors, d_up_bias.reshape(-1, model_width)], 0)
-    vector_grads = lax.psum(vector_grads, CTX + ("fsdp",))
-    fsdp_id = lax.axis_index("fsdp")
-    own_vectors = lax.dynamic_slice_in_dim(vector_grads[:8], fsdp_id * shard, shard, 1)
-    up_len = mlp_bias.shape[1]
-    own_up_bias = lax.dynamic_slice_in_dim(vector_grads[8:].reshape(-1), fsdp_id * up_len, up_len, 0)
+    members = 2 * (model_width // shard)
+    owner_row = jnp.concatenate(
+        [
+            vectors.reshape(8, -1, shard).transpose(1, 0, 2).reshape(-1, 1, 8 * shard),
+            d_up_bias.reshape(-1, 1, mlp_bias.shape[1]),
+        ],
+        -1,
+    )
+    owner_row = jnp.pad(owner_row, ((0, 0), (0, 2 * EXTRA - 1), (0, 0)))
+    owner_row = owner_row.reshape(members, EXTRA, -1)
+    d_qkv = jnp.concatenate([d_qkv.reshape(members, shard // 2, -1), owner_row], 1)
+    d_qkv = d_qkv.astype(jnp.bfloat16).reshape(-1, d_qkv.shape[-1])
+    g_up = finish_grad(scatter_grad(d_up), ("yh", "x"))
+    g_down = finish_grad(scatter_grad(d_down), ("yh", "x"))
+    g_out = finish_grad(scatter_grad(d_out), ("x", "yh"))
+    g_qkv = finish_grad(scatter_grad(d_qkv), ("x", "yh"))
+    own_row = g_qkv[0, shard // 2]
+    own_vectors = own_row[: 8 * shard].reshape(8, shard)
+    own_up_bias = own_row[8 * shard :]
+    g_qkv = g_qkv[:, : shard // 2]
     out_shape = (1, micro_count, 1, local_rows, model_width)
     return (
         layer_out.reshape(out_shape),
         input_grad.reshape(out_shape),
-        scatter_grad(d_qkv),
-        scatter_grad(d_out),
-        scatter_grad(d_up),
-        scatter_grad(d_down),
+        g_qkv.reshape(1, -1, g_qkv.shape[-1]),
+        g_out.reshape(1, -1, g_out.shape[-1]),
+        g_up.reshape(1, -1, g_up.shape[-1]),
+        g_down.reshape(1, -1, g_down.shape[-1]),
         own_vectors[None, :2],
         own_vectors[None, 2:],
         own_up_bias[None],

time: 984 us -> 766 us (0.78); the launches traced: 966 us -> 758 us
  blocking collectives: 453 us -> 97.1 us
  waiting for transfers between devices: 278 us -> 390 us
  starting transfers between devices: 17.3 us -> 40.8 us
  local copies, waits for them, and re-layouts: 57.6 us -> 71.6 us
    psum x1 -> x0, blocking collectives: 319 us -> none  [shards(): vector_grads = lax.psum(vector_grads, CTX + ('fsdp',))]
    psum x1 -> x2, waiting for transfers between devices: 0.01 us -> 166 us  [finish_grad(): total = lax.psum(share, axes)]
    all_gather x4, waiting for transfers between devices: 94.7 us -> 47.2 us  [gather_weight(): return lax.all_gather(own, ('fsdp', 'core'), axis=0, tiled=True)]
    reduce_scatter x4, waiting for transfers between devices: 132 us -> 106 us  [scatter_grad(): lax.psum_scatter(grad, ('fsdp', 'core'), scatter_dimension=0, tiled=True)]
    all_to_all x3 -> x2, blocking collectives: 63.5 us -> 39.3 us  [from_heads(): lax.all_to_all(columns.reshape(members, local, parts * WIDTH), CTX, 0, 0,...]
    all_to_all x1 -> x2, waiting for transfers between devices: 10.7 us -> 29.6 us  [from_heads(): lax.all_to_all(columns.reshape(members, local, parts * WIDTH), CTX, 0, 0,...]
    ppermute x0 -> x7, starting transfers between devices: none -> 18.6 us  [the longest x4 11.4 us: finish_grad(): other = lax.ppermute(total, 'core', [(0, 1), (1, 0)])]
    all_gather x1 -> x0, blocking collectives: 11.8 us -> none  [shards(): small_all = lax.all_gather(small, 'fsdp', axis=0).astype(jnp.float32)]
  transfers between devices with their start and end apart: 13 -> 22, of which waited for: 10 -> 13; matrix products, arithmetic and copies ran while one was open for 7% -> 8% of each run, Pallas kernels for 2% -> 1%
where the time goes in v2:
time: 766 us; the launch traced here: 758 us
  waiting for transfers between devices  390 us (51%)
  blocking collectives  97.1 us (13%)
  matrix products  74.4 us (10%)
  local copies, waits for them, and re-layouts  71.6 us (9%)
  Pallas kernels  42.7 us (6%)
  starting transfers between devices  40.8 us (5%)
  between operations  23.1 us (3%)
  other arithmetic  18.7 us (2%)
    psum x2, waiting for transfers between devices, finish_grad(): total = lax.psum(share, axes)  166 us
    reduce_scatter x4, waiting for transfers between devices, scatter_grad(): lax.psum_scatter(grad, ('fsdp', 'core'), scatter_dimension=0, tiled=True)  106 us
    dot_general x18, matrix products, cross(): jnp.einsum(pattern, left_side, right_side, preferred_element_type=jnp.flo...  74.4 us
    all_to_all x3, blocking collectives, to_heads(): lax.all_to_all(split, CTX, 0, 0, tiled=True).reshape(-1, parts * WIDTH)  57.8 us
    all_gather x4, waiting for transfers between devices, gather_weight(): return lax.all_gather(own, ('fsdp', 'core'), axis=0, tiled=True)  47.2 us
    all_to_all x2, blocking collectives, from_heads(): lax.all_to_all(columns.reshape(members, local, parts * WIDTH), CTX, 0, 0,...  39.3 us
    all_to_all x2, waiting for transfers between devices, from_heads(): lax.all_to_all(columns.reshape(members, local, parts * WIDTH), CTX, 0, 0,...  29.6 us
    pallas_call x2, Pallas kernels, attend_back(): pl.pallas_call(attend_back_body, grid=(count // QUERY_BLOCK,), in_specs=[...  24.5 us
  transfers between devices with their start and end apart: 22, of which 13 were waited for; matrix products, arithmetic and copies ran while one was open for 8% of the time, Pallas kernels for 1%

profile of v2, /device:TPU:1, one launch (start us, length us, event | category | flops | bytes accessed | tf_op | source)
XLA Modules:
  0.0 758.2 jit_solution(6976134491581883624)
XLA Ops:
  13.0 4.5 collective-permute-start.1
  29.8 13.8 %all-gather.9.cloned.1.call-done = bf16[1,768,2304]{2,1,0:T(8,128)(2,1)} async-done(((bf16[1,96,2304]{2,1,0:T(8,128)(2,1)}), bf16[1,768,2304]{2,1,0:T(8,128)(2,1)}) %all-gather.9.cloned.1.call-update) | async-done | bytes 3538960 | tf_op jit(solution)/shard_map/all_gather | solution.py:185
  43.6 3.2 fusion.25
  54.2 7.0 all-to-all-start
  61.9 19.3 %all-to-all-done = bf16[16,64,576]{2,1,0:T(8,128)(2,1)S(1)} async-done(((bf16[16,64,576]{2,1,0:T(8,128)(2,1)}), bf16[16,64,576]{2,1,0:T(8,128)(2,1)S(1)}, u32[]{:S(2)}, u32[]{:S(2)}) %all-to-all-start) | async-done | bytes 1179680 | tf_op jit(solution)/shard_map/all_to_all | solution.py:171
  81.2 9.4 %shard_map.178 = (bf16[1024,192]{1,0:T(8,128)(2,1)}, f32[8,1024]{1,0:T(8,128)}) custom-call(s32[1,1024]{1,0:T(1,128)S(1)} %add.277.row_places, s32[1024,1]{1,0:T(8,128)S(1)} %add.328.column_places, bf16[1024,576]{1,0:T(8,128)(2,1)S(1)} %bitcast.204), custom_call_target="tpu_custom_call" | custom-call | flops 805306368 | bytes 1572864 | tf_op jit(solution)/shard_map/pallas_call | solution.py:55
  90.6 4.7 all-to-all-start.1
  95.8 10.6 %all-to-all-done.1 = bf16[16,64,192]{2,1,0:T(8,128)(2,1)S(1)} async-done(((bf16[16,64,192]{2,1,0:T(8,128)(2,1)}), bf16[16,64,192]{2,1,0:T(8,128)(2,1)S(1)}, u32[]{:S(2)}, u32[]{:S(2)}) %all-to-all-start.1) | async-done | bytes 393248 | tf_op jit(solution)/shard_map/all_to_all | solution.py:177
  109.5 33.3 %all-gather.15.cloned.1.call-done = bf16[1,3072,768]{2,1,0:T(8,128)(2,1)} async-done(((bf16[1,384,768]{2,1,0:T(8,128)(2,1)}), bf16[1,3072,768]{2,1,0:T(8,128)(2,1)}) %all-gather.15.cloned.1.call-update) | async-done | bytes 4718608 | tf_op jit(solution)/shard_map/all_gather | solution.py:185
  142.8 6.8 fusion.76
  152.8 8.2 %collective-permute-done.3 = bf16[256,768]{1,0:T(8,128)(2,1)S(1)} collective-permute-done((bf16[256,768]{1,0:T(8,128)(2,1)S(1)}, bf16[256,768]{1,0:T(8,128)(2,1)S(1)}, u32[]{:S(2)}, u32[]{:S(2)}) %collective-permute-start.3) | collective-permute-done | bytes 393248 | tf_op jit(solution)/shard_map/ppermute | solution.py:345
  161.5 3.2 fusion.26
  167.1 3.6 copy.90
  170.7 5.1 reshape.456
  175.8 27.6 %all_to_all.40 = bf16[16,64,576]{2,1,0:T(8,128)(2,1)S(1)} all-to-all(bf16[16,64,576]{2,1,0:T(8,128)(2,1)} %reshape.456), channel_id=1, replica_groups=mesh['section'=2,'x'=4,'yh'=2,'core'=2,'fsdp'=4] {'x','yh','core'}, dimensions={0} | all-to-all | bytes 2359296 | tf_op jit(solution)/shard_map/all_to_all | solution.py:171
  203.5 8.8 %shard_map.179 = (bf16[1024,192]{1,0:T(8,128)(2,1)S(1)}, f32[8,1024]{1,0:T(8,128)S(1)}) custom-call(s32[1,1024]{1,0:T(1,128)S(1)} %add.277.row_places, s32[1024,1]{1,0:T(8,128)S(1)} %add.328.column_places, bf16[1024,576]{1,0:T(8,128)(2,1)S(1)} %bitcast.201), custom_call_target="tpu_custom_call" | custom-call | flops 805306368 | bytes 1572864 | tf_op jit(solution)/shard_map/pallas_call | solution.py:55
  212.2 14.5 %all_to_all.41 = bf16[16,64,192]{2,1,0:T(8,128)(2,1)S(1)} all-to-all(bf16[16,64,192]{2,1,0:T(8,128)(2,1)S(1)} %bitcast.207), channel_id=1, replica_groups=mesh['section'=2,'x'=4,'yh'=2,'core'=2,'fsdp'=4] {'x','yh','core'}, dimensions={0} | all-to-all | bytes 786432 | tf_op jit(solution)/shard_map/all_to_all | solution.py:177
  230.5 5.5 fusion.22
  236.0 9.4 %fusion.144 = (f32[256]{0:T(256)S(1)}, f32[256]{0:T(256)S(1)}, f32[256,768]{1,0:T(8,128)}) fusion(f32[256]{0:T(256)S(1)} %add_rsqrt_fusion.1, f32[256,768]{1,0:T(8,128)S(1)} %get-tuple-element.113, f32[256]{0:T(256)S(1)} %broadcast_multiply_fusion.9, f32[768]{0:T(1024)S(1)} %mul.290, bf16[1,768,3072]{2,1,0:T(8,128)(2,1)} %all-gather.13.cloned.1.call-done, ...), kind=kOutput, calls=%fused_computation.207 | convolution fusion | flops 2432826880 | bytes 14556160 | tf_op jit(solution)/shard_map/tf,df->td/dot_general | solution.py:142
  252.6 15.0 %all_to_all.42 = bf16[16,64,192]{2,1,0:T(8,128)(2,1)S(1)} all-to-all(bf16[16,64,192]{2,1,0:T(8,128)(2,1)S(1)} %bitcast.223), channel_id=1, replica_groups=mesh['section'=2,'x'=4,'yh'=2,'core'=2,'fsdp'=4] {'x','yh','core'}, dimensions={0} | all-to-all | bytes 786432 | tf_op jit(solution)/shard_map/all_to_all | solution.py:171
  267.6 11.7 %shard_map.180 = bf16[1024,576]{1,0:T(8,128)(2,1)S(1)} custom-call(s32[1,1024]{1,0:T(1,128)S(1)} %add.277.row_places, s32[1024,1]{1,0:T(8,128)S(1)} %add.328.column_places, bf16[1024,576]{1,0:T(8,128)(2,1)S(1)} %bitcast.202, bf16[1024,192]{1,0:T(8,128)(2,1)S(1)} %bitcast.208, f32[8,1024]{1,0:T(8,128)S(1)} %get-tuple-element.18.log_total), custom_call_target="tpu_custom_call" | custom-call | flops 2013265920 | bytes 3145728 | tf_op jit(solution)/shard_map/pallas_call | solution.py:116
  279.3 24.8 %all_to_all.43 = bf16[16,64,576]{2,1,0:T(8,128)(2,1)} all-to-all(bf16[16,64,576]{2,1,0:T(8,128)(2,1)S(1)} %bitcast.205), channel_id=1, replica_groups=mesh['section'=2,'x'=4,'yh'=2,'core'=2,'fsdp'=4] {'x','yh','core'}, dimensions={0} | all-to-all | bytes 2359296 | tf_op jit(solution)/shard_map/all_to_all | solution.py:177
  304.2 5.3 reshape.467
  309.4 4.8 copy.72
  314.2 4.0 reshape.468
  318.2 3.7 fusion.143
  324.2 11.2 %collective-permute-done.4 = bf16[256,768]{1,0:T(8,128)(2,1)} collective-permute-done((bf16[256,768]{1,0:T(8,128)(2,1)}, bf16[256,768]{1,0:T(8,128)(2,1)}, u32[]{:S(2)}, u32[]{:S(2)}) %collective-permute-start.4) | collective-permute-done | bytes 393248 | tf_op jit(solution)/shard_map/ppermute | solution.py:353
  336.6 6.3 convolution_convert_fusion.2
  343.0 6.7 fusion.152
  350.9 3.7 convolution_convert_fusion.1
  354.6 4.5 multiply_reduce_fusion
  366.3 15.2 %all_to_all.44 = bf16[16,64,192]{2,1,0:T(8,128)(2,1)S(1)} all-to-all(bf16[16,64,192]{2,1,0:T(8,128)(2,1)S(1)} %bitcast.224), channel_id=1, replica_groups=mesh['section'=2,'x'=4,'yh'=2,'core'=2,'fsdp'=4] {'x','yh','core'}, dimensions={0} | all-to-all | bytes 786432 | tf_op jit(solution)/shard_map/all_to_all | solution.py:171
  381.5 12.8 %shard_map.181 = bf16[1024,576]{1,0:T(8,128)(2,1)} custom-call(s32[1,1024]{1,0:T(1,128)S(1)} %add.277.row_places, s32[1024,1]{1,0:T(8,128)S(1)} %add.328.column_places, bf16[1024,576]{1,0:T(8,128)(2,1)S(1)} %bitcast.203, bf16[1024,192]{1,0:T(8,128)(2,1)S(1)} %bitcast.206, f32[8,1024]{1,0:T(8,128)S(1)} %get-tuple-element.18.log_total), custom_call_target="tpu_custom_call" | custom-call | flops 2013265920 | bytes 3145728 | tf_op jit(solution)/shard_map/pallas_call | solution.py:116
  394.3 5.4 all-to-all-start.7
  401.0 19.0 %all-to-all-done.7 = bf16[16,64,576]{2,1,0:T(8,128)(2,1)} async-done(((bf16[16,64,576]{2,1,0:T(8,128)(2,1)}), bf16[16,64,576]{2,1,0:T(8,128)(2,1)}, u32[]{:S(2)}, u32[]{:S(2)}) %all-to-all-start.7) | async-done | bytes 1179680 | tf_op jit(solution)/shard_map/all_to_all | solution.py:177
  420.0 4.3 reshape.473
  424.3 3.2 copy.75
  427.5 4.0 reshape.487
  431.4 4.0 reshape.474
  435.4 3.5 fusion.27
  449.9 30.3 %reduce-scatter.5.cloned.1.call-done = bf16[112,2304]{1,0:T(8,128)(2,1)} async-done(((bf16[896,2304]{1,0:T(8,128)(2,1)}), bf16[112,2304]{1,0:T(8,128)(2,1)}) %reduce-scatter.5.cloned.1.call-update) | async-done | bytes 516112 | tf_op jit(solution)/shard_map/reduce_scatter | solution.py:200
  480.3 6.1 fusion.73
  486.4 34.6 %reduce-scatter.9.cloned.1.call-done = bf16[96,3072]{1,0:T(8,128)(2,1)} async-done(((bf16[768,3072]{1,0:T(8,128)(2,1)}), bf16[96,3072]{1,0:T(8,128)(2,1)}) %reduce-scatter.9.cloned.1.call-update) | async-done | bytes 589840 | tf_op jit(solution)/shard_map/reduce_scatter | solution.py:200
  521.0 40.8 %reduce-scatter.11.cloned.1.call-done = bf16[384,768]{1,0:T(8,128)(2,1)} async-done(((bf16[3072,768]{1,0:T(8,128)(2,1)}), bf16[384,768]{1,0:T(8,128)(2,1)}) %reduce-scatter.11.cloned.1.call-update) | async-done | bytes 589840 | tf_op jit(solution)/shard_map/reduce_scatter | solution.py:200
  561.8 86.1 %all-reduce.6.cloned.1.call-done = (bf16[112,2304]{1,0:T(8,128)(2,1)}, bf16[96,768]{1,0:T(8,128)(2,1)}) async-done(((bf16[112,2304]{1,0:T(8,128)(2,1)}, bf16[96,768]{1,0:T(8,128)(2,1)}), (bf16[112,2304]{1,0:T(8,128)(2,1)}, bf16[96,768]{1,0:T(8,128)(2,1)})) %all-reduce.6.cloned.1.call-update) | async-done | bytes 663568 | tf_op jit(solution)/shard_map/psum | solution.py:204
  647.9 5.9 collective-permute-start.6
  656.9 80.2 %all-reduce.8.cloned.1.call-done = (bf16[96,3072]{1,0:T(8,128)(2,1)}, bf16[384,768]{1,0:T(8,128)(2,1)}) async-done(((bf16[96,3072]{1,0:T(8,128)(2,1)}, bf16[384,768]{1,0:T(8,128)(2,1)}), (bf16[96,3072]{1,0:T(8,128)(2,1)}, bf16[384,768]{1,0:T(8,128)(2,1)})) %all-reduce.8.cloned.1.call-update) | async-done | bytes 1179664 | tf_op jit(solution)/shard_map/psum | solution.py:204
  737.1 5.6 collective-permute-start.7
  (205 shorter events, 73.8 us)
Async XLA Ops:
  7.2 3.8 copy-start
  7.2 4.8 copy-start.20
  7.2 5.6 copy-start.26
  7.2 5.8 copy-start.21
  7.2 5.8 copy-start.25
  7.2 12.9 %copy-start.22 = (s32[4]{0:T(128)S(1)}, s32[4]{0:T(128)}, u32[]{:S(2)}) copy-start(s32[4]{0:T(128)} %param.13) | copy-start | bytes 52
  7.2 21.3 %copy-start.19 = (bf16[4,1,64,768]{3,2,1,0:T(8,128)(2,1)S(1)}, bf16[4,1,64,768]{3,2,1,0:T(8,128)(2,1)}, u32[]{:S(2)}) copy-start(bf16[4,1,64,768]{3,2,1,0:T(8,128)(2,1)} %param.11) | copy-start | bytes 1179652
  7.3 36.4 %all-gather.9.cloned.1.call-start = ((), (), s32[]{:S(2)}) async-start(), calls=%async_computation.16 | async-start | bytes 3981312 | tf_op jit(solution)/shard_map/all_gather | solution.py:185
  9.3 98.0 %all-gather.11.cloned.1.call-start = ((), (), s32[]{:S(2)}) async-start(), calls=%async_computation.17 | async-start | bytes 1327104 | tf_op jit(solution)/shard_map/all_gather | solution.py:185
  11.0 98.5 %all-gather.13.cloned.1.call-start = ((), (), s32[]{:S(2)}) async-start(), calls=%async_computation.18 | async-start | bytes 5308416 | tf_op jit(solution)/shard_map/all_gather | solution.py:185
  11.9 130.9 %all-gather.15.cloned.1.call-start = ((), (), s32[]{:S(2)}) async-start(), calls=%async_computation.19 | async-start | bytes 5308416 | tf_op jit(solution)/shard_map/all_gather | solution.py:185
  13.0 16.3 %collective-permute-start.1 = (bf16[12,192]{1,0:T(8,128)(2,1)S(1)}, bf16[12,192]{1,0:T(8,128)(2,1)S(1)}, u32[]{:S(2)}, u32[]{:S(2)}) collective-permute-start(bf16[12,192]{1,0:T(8,128)(2,1)S(1)} %pad_maximum_fusion.7), channel_id=1, source_target_pairs={{0,2},{1,3},{2,0},{3,1},{4,6},{5,7},{6,4},{7,5},{8,10},{9,11},{10,... | collective-permute-start | bytes 13832 | tf_op jit(solution)/shard_map/ppermute | solution.py:194
  17.5 11.8 %collective-permute-start = (bf16[12,192]{1,0:T(8,128)(2,1)S(1)}, bf16[12,192]{1,0:T(8,128)(2,1)S(1)}, u32[]{:S(2)}, u32[]{:S(2)}) collective-permute-start(bf16[12,192]{1,0:T(8,128)(2,1)S(1)} %pad_maximum_fusion.7), channel_id=1, source_target_pairs={{0,1},{1,2},{2,3},{3,0},{4,5},{5,6},{6,7},{7,4},{8,9},{9,10},{10,1... | collective-permute-start | bytes 13832 | tf_op jit(solution)/shard_map/ppermute | solution.py:194
  18.2 11.1 %collective-permute-start.2 = (bf16[12,192]{1,0:T(8,128)(2,1)S(1)}, bf16[12,192]{1,0:T(8,128)(2,1)S(1)}, u32[]{:S(2)}, u32[]{:S(2)}) collective-permute-start(bf16[12,192]{1,0:T(8,128)(2,1)S(1)} %pad_maximum_fusion.7), channel_id=1, source_target_pairs={{0,3},{1,0},{2,1},{3,2},{4,7},{5,4},{6,5},{7,6},{8,11},{9,8},{10,9... | collective-permute-start | bytes 13832 | tf_op jit(solution)/shard_map/ppermute | solution.py:194
  28.7 18.1 %copy-start.9 = (bf16[4,1,64,768]{3,2,1,0:T(8,128)(2,1)}, bf16[4,1,64,768]{3,2,1,0:T(8,128)(2,1)S(1)}, u32[]{:S(2)}) copy-start(bf16[4,1,64,768]{3,2,1,0:T(8,128)(2,1)S(1)} %get-tuple-element.90) | copy-start | bytes 1179652
  51.5 9.6 %copy-start.27 = (s32[32]{0:T(128)S(1)}, s32[32]{0:T(128)}, u32[]{:S(2)}) copy-start(s32[32]{0:T(128)} %param.14) | copy-start | bytes 388
  54.2 27.0 %all-to-all-start = ((bf16[16,64,576]{2,1,0:T(8,128)(2,1)}), bf16[16,64,576]{2,1,0:T(8,128)(2,1)S(1)}, u32[]{:S(2)}, u32[]{:S(2)}) async-start(bf16[16,64,576]{2,1,0:T(8,128)(2,1)} %reshape.450), calls=%async_computation | async-start | bytes 2621440 | tf_op jit(solution)/shard_map/all_to_all | solution.py:171
  81.2 26.1 %copy-start.10 = (bf16[4,1,64,768]{3,2,1,0:T(8,128)(2,1)S(1)}, bf16[4,1,64,768]{3,2,1,0:T(8,128)(2,1)}, u32[]{:S(2)}) copy-start(bf16[4,1,64,768]{3,2,1,0:T(8,128)(2,1)} %copy-done.9) | copy-start | bytes 1179652
  90.6 15.8 %all-to-all-start.1 = ((bf16[16,64,192]{2,1,0:T(8,128)(2,1)}), bf16[16,64,192]{2,1,0:T(8,128)(2,1)S(1)}, u32[]{:S(2)}, u32[]{:S(2)}) async-start(bf16[16,64,192]{2,1,0:T(8,128)(2,1)} %bitcast.15), calls=%async_computation.1 | async-start | bytes 1048576 | tf_op jit(solution)/shard_map/all_to_all | solution.py:177
  95.7 53.9 %copy-start.23 = (f32[768]{0:T(1024)}, f32[768]{0:T(1024)S(1)}, u32[]{:S(2)}) copy-start(f32[768]{0:T(1024)S(1)} %add.308) | copy-start | bytes 9220
  109.4 51.6 %copy-start.11 = (bf16[4,1,64,768]{3,2,1,0:T(8,128)(2,1)S(1)}, bf16[4,1,64,768]{3,2,1,0:T(8,128)(2,1)}, u32[]{:S(2)}) copy-start(bf16[4,1,64,768]{3,2,1,0:T(8,128)(2,1)} %copy-done.9) | copy-start | bytes 1179652
  149.6 11.4 %collective-permute-start.3 = (bf16[256,768]{1,0:T(8,128)(2,1)S(1)}, bf16[256,768]{1,0:T(8,128)(2,1)S(1)}, u32[]{:S(2)}, u32[]{:S(2)}) collective-permute-start(bf16[256,768]{1,0:T(8,128)(2,1)S(1)} %fusion.76), channel_id=1, source_target_pairs={{0,64},{1,65},{2,66},{3,67},{4,68},{5,69},{6,70},{7,71},{8,72},{9,... | collective-permute-start | bytes 1179656 | tf_op jit(solution)/shard_map/ppermute | solution.py:345
  161.2 160.7 %copy-start.3 = (bf16[256,768]{1,0:T(8,128)(2,1)}, bf16[256,768]{1,0:T(8,128)(2,1)S(1)}, u32[]{:S(2)}) copy-start(bf16[256,768]{1,0:T(8,128)(2,1)S(1)} %get-tuple-element.88) | copy-start | bytes 1179652
  245.4 2.5 copy-start.2
  318.1 3.7 copy-start.8
  322.9 12.5 %collective-permute-start.4 = (bf16[256,768]{1,0:T(8,128)(2,1)}, bf16[256,768]{1,0:T(8,128)(2,1)}, u32[]{:S(2)}, u32[]{:S(2)}) collective-permute-start(bf16[256,768]{1,0:T(8,128)(2,1)} %fusion.101), channel_id=1, source_target_pairs={{64,0},{65,1},{66,2},{67,3},{68,4},{69,5},{70,6},{71,7},{72,8},{73... | collective-permute-start | bytes 1179656 | tf_op jit(solution)/shard_map/ppermute | solution.py:353
  349.7 1.1 copy-start.15
  354.6 5.8 copy-start.12
  359.5 0.9 copy-start.5
  394.3 25.7 %all-to-all-start.7 = ((bf16[16,64,576]{2,1,0:T(8,128)(2,1)}), bf16[16,64,576]{2,1,0:T(8,128)(2,1)}, u32[]{:S(2)}, u32[]{:S(2)}) async-start(bf16[16,64,576]{2,1,0:T(8,128)(2,1)} %bitcast.38), calls=%async_computation.7 | async-start | bytes 2621440 | tf_op jit(solution)/shard_map/all_to_all | solution.py:177
  399.8 50.1 %reduce-scatter.7.cloned.1.call-start = ((), (), s32[]{:S(2)}) async-start(), calls=%async_computation.13 | async-start | bytes 1327104 | tf_op jit(solution)/shard_map/reduce_scatter | solution.py:200
  400.3 79.9 %reduce-scatter.5.cloned.1.call-start = ((), (), s32[]{:S(2)}) async-start(), calls=%async_computation.12 | async-start | bytes 4644864 | tf_op jit(solution)/shard_map/reduce_scatter | solution.py:200
  435.4 4.4 copy-start.4
  448.3 72.7 %reduce-scatter.9.cloned.1.call-start = ((), (), s32[]{:S(2)}) async-start(), calls=%async_computation.14 | async-start | bytes 5308416 | tf_op jit(solution)/shard_map/reduce_scatter | solution.py:200
  449.1 31.2 %copy-start.24 = (f32[768]{0:T(1024)S(1)}, f32[768]{0:T(1024)}, u32[]{:S(2)}) copy-start(f32[768]{0:T(1024)} %copy-done.23) | copy-start | bytes 9220
  449.1 112.7 %reduce-scatter.11.cloned.1.call-start = ((), (), s32[]{:S(2)}) async-start(), calls=%async_computation.15 | async-start | bytes 5308416 | tf_op jit(solution)/shard_map/reduce_scatter | solution.py:200
  449.8 198.1 %all-reduce.6.cloned.1.call-start = ((), (), s32[]{:S(2)}) async-start(), calls=%async_computation.20 | async-start | bytes 1327104 | tf_op jit(solution)/shard_map/psum | solution.py:204
  480.2 173.6 %copy-start.6 = (f32[256,768]{1,0:T(8,128)S(1)}, f32[256,768]{1,0:T(8,128)}, u32[]{:S(2)}) copy-start(f32[256,768]{1,0:T(8,128)} %copy-done.5) | copy-start | bytes 2359300
  480.2 173.6 %copy-start.14 = (f32[256,768]{1,0:T(8,128)S(1)}, f32[256,768]{1,0:T(8,128)}, u32[]{:S(2)}) copy-start(f32[256,768]{1,0:T(8,128)} %copy-done.13) | copy-start | bytes 2359300
  480.3 256.9 %all-reduce.8.cloned.1.call-start = ((), (), s32[]{:S(2)}) async-start(), calls=%async_computation.21 | async-start | bytes 2359296 | tf_op jit(solution)/shard_map/psum | solution.py:204
  647.9 94.7 %copy-start.18 = (bf16[112,2304]{1,0:T(8,128)(2,1)S(1)}, bf16[112,2304]{1,0:T(8,128)(2,1)}, u32[]{:S(2)}) copy-start(bf16[112,2304]{1,0:T(8,128)(2,1)} %get-tuple-element.79) | copy-start | bytes 1548292
  647.9 7.1 collective-permute-start.6
  654.9 87.8 %collective-permute-start.5 = (bf16[112,2304]{1,0:T(8,128)(2,1)}, bf16[112,2304]{1,0:T(8,128)(2,1)}, u32[]{:S(2)}, u32[]{:S(2)}) collective-permute-start(bf16[112,2304]{1,0:T(8,128)(2,1)} %get-tuple-element.79), channel_id=1, source_target_pairs={{0,4},{4,0},{1,5},{5,1},{2,6},{6,2},{3,7},{7,3},{8,12},{12,8},{9,1... | collective-permute-start | bytes 1548296 | tf_op jit(solution)/shard_map/ppermute | solution.py:205
  737.1 12.0 %collective-permute-start.7 = (bf16[96,3072]{1,0:T(8,128)(2,1)}, bf16[96,3072]{1,0:T(8,128)(2,1)S(1)}, u32[]{:S(2)}, u32[]{:S(2)}) collective-permute-start(bf16[96,3072]{1,0:T(8,128)(2,1)} %get-tuple-element.81), channel_id=1, source_target_pairs={{0,4},{4,0},{1,5},{5,1},{2,6},{6,2},{3,7},{7,3},{8,12},{12,8},{9,1... | collective-permute-start | bytes 1769480 | tf_op jit(solution)/shard_map/ppermute | solution.py:205
  742.7 4.6 collective-permute-start.8
  745.2 2.0 copy-start.17
  747.4 1.7 copy-start.16
  749.1 1.9 copy-start.1
  (2 other events, 1.8 us)
Sparse Core Ops, SparseCore 0:
  10.4 33.2 all-gather.8
  45.9 23.5 all-gather.10
  71.8 34.4 all-gather.12
  108.4 34.3 all-gather.14
  402.7 29.2 reduce-scatter.6
  448.4 31.7 reduce-scatter.4
  482.7 38.2 reduce-scatter.8
  523.5 38.1 reduce-scatter.10
  564.5 83.3 all-reduce.5
  650.5 86.5 all-reduce.7

commit v3 on v1

v3 whole, which is shorter than its diff:
```python
import jax
import jax.numpy as jnp
from jax import lax
from jax.experimental import pallas as pl
from jax.experimental.pallas import tpu as pltpu
from jax.sharding import Mesh
from jax.sharding import PartitionSpec as P

HEADS = 12
HDIM = 64
GROUPS = 4
GROUP_HEADS = HEADS // GROUPS
WIDTH = GROUP_HEADS * HDIM
QUERY_BLOCK = 256
EXTRA = 32
CTX = ("x", "yh", "core")

epsilon = 1e-05
neg_fill = -1e30


def dot(left_side, right_side, left_dim, right_dim):
    return lax.dot_general(
        left_side,
        right_side,
        (((left_dim,), (right_dim,)), ((), ())),
        preferred_element_type=jnp.float32,
    )


def head_columns(part, head):
    start = part * WIDTH + head * HDIM
    return slice(start, start + HDIM)


def attend_body(
    row_places, column_places, own, other, weight, bias, joined, mixed, log_total
):
    step = pl.program_id(0)
    half = own.shape[1]

    @pl.when(step == 0)
    def _():
        product = dot(own[...], weight[:half, :], 1, 0) + dot(other[...], weight[half:, :], 1, 0)
        joined[...] = (product + bias[...]).astype(jnp.bfloat16)

    rows = pl.ds(pl.multiple_of(step * QUERY_BLOCK, QUERY_BLOCK), QUERY_BLOCK)
    hidden = jnp.where(column_places[...] <= row_places[...], 0.0, neg_fill)
    parts = []
    for head in range(GROUP_HEADS):
        queries = joined[rows, head_columns(0, head)] * jnp.bfloat16(HDIM ** (-0.5))
        keys = joined[:, head_columns(1, head)]
        values = joined[:, head_columns(2, head)]
        scores = dot(keys, queries, 1, 1) + hidden
        top = jnp.max(scores, 0, keepdims=True)
        powers = jnp.exp(scores - top)
        total = jnp.sum(powers, 0, keepdims=True)
        parts.append(dot(values, powers.astype(jnp.bfloat16), 0, 0) / total)
        log_total[head : head + 1, :] = top + jnp.log(total)
    mixed[...] = jnp.concatenate(parts, 0).T.astype(jnp.bfloat16)


def whole(*shape):
    return pl.BlockSpec(shape, lambda i: (0,) * len(shape))


def attend(own, other, weight, bias, row_places, column_places):
    count, half = own.shape
    return pl.pallas_call(
        attend_body,
        grid=(count // QUERY_BLOCK,),
        in_specs=[
            pl.BlockSpec((1, QUERY_BLOCK), lambda i: (0, i)),
            whole(count, 1),
            whole(count, half),
            whole(count, half),
            whole(2 * half, 3 * WIDTH),
            whole(1, 3 * WIDTH),
        ],
        out_specs=[
            whole(count, 3 * WIDTH),
            pl.BlockSpec((QUERY_BLOCK, WIDTH), lambda i: (i, 0)),
            pl.BlockSpec((8, QUERY_BLOCK), lambda i: (0, i)),
        ],
        out_shape=[
            jax.ShapeDtypeStruct((count, 3 * WIDTH), jnp.bfloat16),
            jax.ShapeDtypeStruct((count, WIDTH), jnp.bfloat16),
            jax.ShapeDtypeStruct((8, count), jnp.float32),
        ],
        compiler_params=pltpu.CompilerParams(vmem_limit_bytes=48 << 20),
        cost_estimate=pl.CostEstimate(
            flops=4 * count * count * WIDTH,
            bytes_accessed=8 * count * WIDTH,
            transcendentals=count * count * GROUP_HEADS,
        ),
    )(row_places, column_places, own, other, weight, bias)


def attend_back_body(
    row_places,
    column_places,
    joined,
    grad_mixed,
    log_total,
    weight,
    grad_joined,
    grad_own,
    grad_other,
    key_sums,
    value_sums,
):
    step = pl.program_id(0)
    rows = pl.ds(pl.multiple_of(step * QUERY_BLOCK, QUERY_BLOCK), QUERY_BLOCK)

    @pl.when(step == 0)
    def _():
        key_sums[...] = jnp.zeros_like(key_sums)
        value_sums[...] = jnp.zeros_like(value_sums)

    hidden = jnp.where(column_places[...] <= row_places[...], 0.0, neg_fill)
    parts = []
    for head in range(GROUP_HEADS):
        queries = joined[rows, head_columns(0, head)] * jnp.bfloat16(HDIM ** (-0.5))
        keys = joined[:, head_columns(1, head)]
        values = joined[:, head_columns(2, head)]
        grads = grad_mixed[:, head_columns(0, head)]
        weights = jnp.exp(dot(keys, queries, 1, 1) + hidden - log_total[head : head + 1, :])
        grad_weights = dot(values, grads, 1, 1)
        inner_sum = jnp.sum(weights * grad_weights, 0, keepdims=True)
        grad_scores = (weights * (grad_weights - inner_sum)).astype(jnp.bfloat16)
        value_sums[head] += dot(weights.astype(jnp.bfloat16), grads, 1, 0)
        key_sums[head] += dot(grad_scores, queries, 1, 0)
        parts.append(dot(keys, grad_scores, 0, 0) * (HDIM ** (-0.5)))
    grad_joined[rows, :WIDTH] = jnp.concatenate(parts, 0).T.astype(jnp.bfloat16)

    @pl.when(step == pl.num_programs(0) - 1)
    def _():
        for head in range(GROUP_HEADS):
            grad_joined[:, head_columns(1, head)] = key_sums[head].astype(jnp.bfloat16)
            grad_joined[:, head_columns(2, head)] = value_sums[head].astype(jnp.bfloat16)
        half = grad_own.shape[1]
        grad_own[...] = dot(grad_joined[...], weight[:half, :], 1, 1).astype(jnp.bfloat16)
        grad_other[...] = dot(grad_joined[...], weight[half:, :], 1, 1).astype(jnp.bfloat16)


def attend_back(joined, grad_mixed, log_total, weight, row_places, column_places):
    count = joined.shape[0]
    half = weight.shape[0] // 2
    return pl.pallas_call(
        attend_back_body,
        grid=(count // QUERY_BLOCK,),
        in_specs=[
            pl.BlockSpec((1, QUERY_BLOCK), lambda i: (0, i)),
            whole(count, 1),
            whole(count, 3 * WIDTH),
            pl.BlockSpec((QUERY_BLOCK, WIDTH), lambda i: (i, 0)),
            pl.BlockSpec((8, QUERY_BLOCK), lambda i: (0, i)),
            whole(2 * half, 3 * WIDTH),
        ],
        out_specs=[whole(count, 3 * WIDTH), whole(count, half), whole(count, half)],
        out_shape=[
            jax.ShapeDtypeStruct((count, 3 * WIDTH), jnp.bfloat16),
            jax.ShapeDtypeStruct((count, half), jnp.bfloat16),
            jax.ShapeDtypeStruct((count, half), jnp.bfloat16),
        ],
        scratch_shapes=[
            pltpu.VMEM((GROUP_HEADS, count, HDIM), jnp.float32),
            pltpu.VMEM((GROUP_HEADS, count, HDIM), jnp.float32),
        ],
        compiler_params=pltpu.CompilerParams(vmem_limit_bytes=48 << 20),
        cost_estimate=pl.CostEstimate(
            flops=10 * count * count * WIDTH,
            bytes_accessed=16 * count * WIDTH,
            transcendentals=count * count * GROUP_HEADS,
        ),
    )(row_places, column_places, joined, grad_mixed, log_total, weight)


def cross(left_side, right_side, pattern):
    return jnp.einsum(pattern, left_side, right_side, preferred_element_type=jnp.float32)


def normalize(values, gain_row, shift_row):
    center = values - jnp.mean(values, -1, keepdims=True)
    spread = lax.rsqrt(jnp.mean(center * center, -1, keepdims=True) + epsilon)
    unit_rows = center * spread
    return (unit_rows * gain_row + shift_row, unit_rows, spread)


def normalize_back(grad_out, unit_rows, spread, gain_row):
    grad_unit = grad_out * gain_row
    grad_in = spread * (
        grad_unit
        - jnp.mean(grad_unit, -1, keepdims=True)
        - unit_rows * jnp.mean(grad_unit * unit_rows, -1, keepdims=True)
    )
    return (grad_in, jnp.sum(grad_out * unit_rows, 0), jnp.sum(grad_out, 0))


def positions(block_table, block_len):
    offsets = jnp.arange(block_len, dtype=jnp.int32)
    return (block_table[:, None] * block_len + offsets[None, :]).reshape(-1)


def exchange(value, axes):
    return lax.all_to_all(value, axes, 0, 0, tiled=True)


def swap(value):
    return lax.ppermute(value, "core", [(0, 1), (1, 0)])


def in_order(own, other):
    first = lax.axis_index("core") == 0
    return jnp.where(first, own, other), jnp.where(first, other, own)


def gather_weight(weight):
    half = weight.shape[1] // 2
    own = lax.dynamic_slice_in_dim(weight[0], lax.axis_index("core") * half, half, 0)
    return lax.all_gather(own, ("fsdp", "core"), axis=0, tiled=True)


def gather_small(value):
    count = lax.axis_size("fsdp")
    place = lax.axis_index("fsdp")
    gathered = jnp.zeros((count,) + value.shape, value.dtype)
    for shift in range(count):
        pairs = [(source, (source + shift) % count) for source in range(count)]
        member = lax.ppermute(value, "fsdp", pairs) if shift else value
        gathered = lax.dynamic_update_index_in_dim(gathered, member, (place - shift) % count, 0)
    return gathered


def sum_low(value):
    return jnp.sum(value.astype(jnp.float32), 0).astype(jnp.bfloat16)


def spread(value, axes):
    count = lax.axis_size(axes)
    return exchange(jnp.broadcast_to(value[None], (count,) + value.shape), axes)


def shards(
    inputs,
    cotangent,
    plan,
    block_table,
    attn_in,
    attn_out,
    mlp_in,
    mlp_out,
    norm_gains,
    biases,
    mlp_bias,
):
    shard = norm_gains.shape[2]
    core_id = lax.axis_index("core")
    group_id = lax.axis_index("yh") * 2 + core_id
    fsdp_id = lax.axis_index("fsdp")
    section_id = lax.axis_index("section")
    sections = lax.axis_size("section")
    fsdp_count = lax.axis_size("fsdp")

    small = jnp.concatenate([norm_gains[0], biases[0], mlp_bias.reshape(-1, shard)], 0)
    own_columns = lax.dynamic_index_in_dim(
        attn_in[0].reshape(shard, 3, GROUPS, WIDTH), group_id, 2, keepdims=False
    ).reshape(shard, 3 * WIDTH)
    w_group = gather_small(own_columns).reshape(-1, 3 * WIDTH)
    small_all = gather_small(small).astype(jnp.float32)
    w_out = gather_weight(attn_out)
    w_up = gather_weight(mlp_in)
    w_down = gather_weight(mlp_out)
    model_width = w_out.shape[0]
    half = model_width // 2
    w_group = jnp.concatenate(in_order(w_group[:half], w_group[half:]), 0)
    w_out_groups = w_out.reshape(GROUPS, WIDTH, model_width)
    vector_rows = small_all[:, :8].transpose(1, 0, 2).reshape(8, model_width)
    gain_rows, bias_rows = vector_rows[:2], vector_rows[2:]
    up_bias = small_all[:, 8:].reshape(-1)
    own_bias = lax.dynamic_index_in_dim(small_all, group_id, 0, keepdims=False)
    group_bias = jnp.concatenate([own_bias[3], jnp.zeros_like(own_bias[3]), own_bias[4]])[None]

    micro_count, _, local_rows, _ = inputs.shape
    rows = micro_count * local_rows
    places = positions(block_table, local_rows // 2)
    row_places, column_places = places[None, :], places[:, None]
    fresh = jnp.stack(
        [lax.dynamic_index_in_dim(inputs, plan[step], 0, keepdims=False) for step in range(micro_count)]
    ).reshape(rows, model_width)
    top_grad = cotangent.reshape(rows, model_width)
    head_shape = (micro_count, GROUPS, local_rows, WIDTH)

    def forward(entering):
        stream = entering.astype(jnp.float32)
        normed, unit_one, spread_one = normalize(stream, gain_rows[0], bias_rows[0])
        halves = normed.astype(jnp.bfloat16).reshape(micro_count, 1, local_rows, 2, half)
        halves = jnp.broadcast_to(
            halves.transpose(0, 1, 3, 2, 4), (micro_count, 2, 2, local_rows, half)
        )
        own = exchange(halves.reshape(-1, local_rows, half), CTX).reshape(-1, half)
        other = swap(own)
        joined, mixed_heads, log_total = attend(
            own, other, w_group, group_bias, row_places, column_places
        )
        mixed = exchange(mixed_heads.reshape(-1, local_rows, WIDTH), CTX).reshape(head_shape)
        attended = cross(mixed, w_out_groups, "mgtd,gde->mte").reshape(rows, model_width)
        middle = stream + (attended + bias_rows[3])
        normed_two, unit_two, spread_two = normalize(middle, gain_rows[1], bias_rows[4])
        normed_two_low = normed_two.astype(jnp.bfloat16)
        hidden_pre = cross(normed_two_low, w_up, "td,df->tf") + up_bias
        active_low = jax.nn.gelu(hidden_pre).astype(jnp.bfloat16)
        result = (middle + (cross(active_low, w_down, "tf,fd->td") + bias_rows[5])).astype(
            jnp.bfloat16
        )
        saved = (
            unit_one,
            spread_one,
            own,
            other,
            joined,
            log_total,
            mixed,
            unit_two,
            spread_two,
            normed_two_low,
            hidden_pre,
            active_low,
        )
        return result, saved

    def backward(grad_low, saved, last):
        (
            unit_one,
            spread_one,
            own,
            other,
            joined,
            log_total,
            mixed,
            unit_two,
            spread_two,
            normed_two_low,
            hidden_pre,
            active_low,
        ) = saved
        grad_top = grad_low.astype(jnp.float32)
        grad_active = cross(grad_low, w_down, "td,fd->tf")
        _, gelu_pull = jax.vjp(jax.nn.gelu, hidden_pre)
        grad_hidden = gelu_pull(grad_active)[0].astype(jnp.bfloat16)
        grad_normed_two = cross(grad_hidden, w_up, "tf,df->td")
        grad_norm_two, d_gain_two, d_shift_two = normalize_back(
            grad_normed_two, unit_two, spread_two, gain_rows[1]
        )
        grad_middle = grad_top + grad_norm_two
        grad_attn = grad_middle.astype(jnp.bfloat16)
        attn_parts = grad_attn.reshape(micro_count, local_rows, model_width)
        grad_mixed = cross(attn_parts, w_out_groups, "mte,gde->mgtd").astype(jnp.bfloat16)
        share = None
        if last:
            members = 2 * fsdp_count
            d_down = cross(active_low, grad_low, "tf,td->fd").astype(jnp.bfloat16)
            d_up = cross(normed_two_low, grad_hidden, "td,tf->df").astype(jnp.bfloat16)
            d_out = cross(mixed, attn_parts, "mgtd,mte->gde").astype(jnp.bfloat16)
            d_up = d_up.reshape(members, shard // 2, -1, model_width).transpose(0, 2, 1, 3)
            parts = [
                d_down.reshape(members, -1, model_width),
                d_up.reshape(members, -1, model_width),
                d_out.reshape(members, -1, model_width),
            ]
            parts.append(jnp.zeros((members, EXTRA, model_width), jnp.bfloat16))
            joint = jnp.concatenate(parts, 1)
            grad_mixed, joint = lax.optimization_barrier((grad_mixed, joint))
            share = lax.psum_scatter(
                joint.reshape(-1, model_width),
                ("fsdp", "core"),
                scatter_dimension=0,
                tiled=True,
            )
        grad_heads = exchange(grad_mixed.reshape(-1, local_rows, WIDTH), CTX).reshape(-1, WIDTH)
        grad_joined, grad_own, grad_other = attend_back(
            joined, grad_heads, log_total, w_group, row_places, column_places
        )
        received = swap(grad_other)
        summed = (grad_own.astype(jnp.float32) + received.astype(jnp.float32)).astype(jnp.bfloat16)
        returned = exchange(summed.reshape(-1, local_rows, half), CTX)
        returned = returned.reshape(micro_count, 2, 2, local_rows, half).astype(jnp.float32)
        grad_normed = (returned[:, 0] + returned[:, 1]).transpose(0, 2, 1, 3)
        grad_normed = grad_normed.reshape(rows, model_width)
        if last:
            grad_normed, share = lax.optimization_barrier((grad_normed, share))
        grad_norm_one, d_gain_one, d_shift_one = normalize_back(
            grad_normed, unit_one, spread_one, gain_rows[0]
        )
        grad_in = (grad_middle + grad_norm_one).astype(jnp.bfloat16)
        if not last:
            return grad_in
        d_qkv = jnp.concatenate(
            in_order(
                cross(own, grad_joined, "td,te->de").astype(jnp.bfloat16),
                cross(other, grad_joined, "td,te->de").astype(jnp.bfloat16),
            ),
            0,
        )
        joined_sums = jnp.sum(grad_joined.astype(jnp.float32), 0)
        vectors = jnp.stack(
            [
                d_gain_one,
                d_gain_two,
                d_shift_one,
                jnp.sum(grad_attn.astype(jnp.float32), 0),
                d_shift_two,
                jnp.sum(grad_top, 0),
            ]
        )
        d_up_bias = jnp.sum(grad_hidden.astype(jnp.float32), 0)
        return grad_in, share, d_qkv, joined_sums, vectors, d_up_bias

    forward_pairs = [(i, i + 1) for i in range(sections - 1)]
    entering = fresh
    for _ in range(sections - 1):
        result, _ = forward(entering)
        received = lax.ppermute(result, "section", forward_pairs)
        entering = jnp.where(section_id == 0, fresh, received)
    layer_out, saved = forward(entering)

    back_pairs = [(i + 1, i) for i in range(sections - 1)]
    grad_low = top_grad
    for _ in range(sections - 1):
        result = backward(grad_low, saved, False)
        received = lax.ppermute(result, "section", back_pairs)
        grad_low = jnp.where(section_id == sections - 1, top_grad, received)
    input_grad, share, d_qkv, joined_sums, vectors, d_up_bias = backward(grad_low, saved, True)

    pieces = 4 * fsdp_count
    qkv_piece = sum_low(exchange(d_qkv.reshape(pieces, -1, 3 * WIDTH), ("fsdp", "x")))
    qkv_all = spread(qkv_piece, CTX).reshape(4, GROUPS, -1, 3, WIDTH).transpose(0, 2, 3, 1, 4)
    g_qkv = qkv_all.reshape(1, shard, -1).astype(jnp.float32)

    joint_piece = sum_low(exchange(share.reshape(8, -1, model_width), ("x", "yh")))
    joint_all = spread(joint_piece, ("x", "yh")).reshape(-1, model_width)
    both = jnp.stack(in_order(joint_all, swap(joint_all))).astype(jnp.float32)
    down_rows = mlp_out.shape[1] // 2
    g_down = both[:, :down_rows].reshape(1, -1, model_width)
    g_up = both[:, down_rows : 2 * down_rows].reshape(2, -1, shard // 2, model_width)
    g_up = g_up.transpose(0, 2, 1, 3).reshape(1, shard, -1)
    g_out = both[:, 2 * down_rows : 2 * down_rows + shard // 2].reshape(1, shard, model_width)

    ours = jnp.arange(fsdp_count)[:, None] == group_id
    vector_parts = jnp.concatenate(
        [
            vectors.reshape(6, -1, shard).transpose(1, 0, 2).reshape(-1, 6 * shard),
            jnp.where(ours, joined_sums[None, :WIDTH], 0.0),
            jnp.where(ours, joined_sums[None, 2 * WIDTH :], 0.0),
            d_up_bias.reshape(fsdp_count, -1),
        ],
        1,
    )
    vector_sum = jnp.sum(exchange(vector_parts, "fsdp"), 0)
    vector_sum = jnp.sum(spread(vector_sum, CTX), 0)
    own_vectors = vector_sum[: 8 * shard].reshape(8, shard)
    own_up_bias = vector_sum[8 * shard :]
    order = (2, 6, 7, 3, 4, 5)
    g_biases = jnp.stack([own_vectors[place] for place in order])
    out_shape = (1, micro_count, 1, local_rows, model_width)
    return (
        layer_out.reshape(out_shape),
        input_grad.reshape(out_shape),
        g_qkv,
        g_out,
        g_up,
        g_down,
        own_vectors[None, :2],
        g_biases[None],
        own_up_bias[None],
    )


def solution(mesh):
    fine = Mesh(
        mesh.devices.reshape(2, 4, 2, 2, 4), ("section", "x", "yh", "core", "fsdp")
    )
    rows = P(None, "fsdp", CTX, None)
    weight = P("section", "fsdp", None)
    vector = P("section", None, "fsdp")
    row = P("section", "fsdp")
    out_rows = P("section", None, "fsdp", CTX, None)
    return jax.shard_map(
        shards,
        mesh=fine,
        in_specs=(rows, rows, P(), P(), weight, weight, weight, weight, vector, vector, row),
        out_specs=(out_rows, out_rows, weight, weight, weight, weight, vector, vector, row),
        check_vma=False,
    )
```

time: 984 us -> 534 us (0.54)
  blocking collectives: 453 us -> 101 us
  waiting for transfers between devices: 278 us -> 135 us
  starting transfers between devices: 17.3 us -> 70 us
  matrix products: 79.3 us -> 49.6 us
  other arithmetic: 15.7 us -> 29.6 us
    psum x1 -> x0, blocking collectives: 319 us -> none  [shards(): vector_grads = lax.psum(vector_grads, CTX + ('fsdp',))]
    reduce_scatter x4 -> x1, waiting for transfers between devices: 132 us -> 7.29 us  [backward(): lax.psum_scatter(joint.reshape(-1, model_width), ('fsdp', 'core'), scatte...]
    all_gather x4 -> x3, waiting for transfers between devices: 94.7 us -> 11.9 us  [gather_weight(): return lax.all_gather(own, ('fsdp', 'core'), axis=0, tiled=True)]
    all_to_all x2 -> x8, waiting for transfers between devices: 30 us -> 84.2 us  [exchange(): return lax.all_to_all(value, axes, 0, 0, tiled=True)]
    all_to_all x2 -> x8, starting transfers between devices: 12 us -> 51.4 us  [exchange(): return lax.all_to_all(value, axes, 0, 0, tiled=True)]
    dot_general x18 -> x15, matrix products: 79.3 us -> 49.6 us  [cross(): jnp.einsum(pattern, left_side, right_side, preferred_element_type=jnp.flo...]
    reshape x16 -> x6, local copies, waits for them, and re-layouts: 40.2 us -> 14.3 us  [the longest x1 9.74 us: backward(): d_up.reshape(members, shard // 2, -1, model_width).transpose(0, 2, 1, 3)]
    all_to_all x6, blocking collectives: 122 us -> 101 us  [exchange(): return lax.all_to_all(value, axes, 0, 0, tiled=True)]
  transfers between devices with their start and end apart: 13 -> 25, of which waited for: 10 -> 16; matrix products, arithmetic and copies ran while one was open for 7% -> 11% of each run, Pallas kernels for 2% -> 5%
where the time goes in v3:
time: 534 us; the launch traced here: 526 us
  waiting for transfers between devices  135 us (25%)
  blocking collectives  101 us (19%)
  starting transfers between devices  70 us (13%)
  local copies, waits for them, and re-layouts  65 us (12%)
  Pallas kernels  51.5 us (10%)
  matrix products  49.6 us (9%)
  other arithmetic  29.6 us (6%)
  between operations  23.1 us (4%)
    all_to_all x6, blocking collectives, exchange(): return lax.all_to_all(value, axes, 0, 0, tiled=True)  101 us
    all_to_all x8, waiting for transfers between devices, exchange(): return lax.all_to_all(value, axes, 0, 0, tiled=True)  84.2 us
    all_to_all x8, starting transfers between devices, exchange(): return lax.all_to_all(value, axes, 0, 0, tiled=True)  51.4 us
    dot_general x15, matrix products, cross(): jnp.einsum(pattern, left_side, right_side, preferred_element_type=jnp.flo...  49.6 us
    pallas_call x2, Pallas kernels, attend_back(): pl.pallas_call(attend_back_body, grid=(count // QUERY_BLOCK,), in_specs=[...  29.9 us
    pallas_call x2, Pallas kernels, attend(): pl.pallas_call(attend_body, grid=(count // QUERY_BLOCK,), in_specs=[pl.Bl...  21.6 us
    all_gather x3, waiting for transfers between devices, gather_weight(): return lax.all_gather(own, ('fsdp', 'core'), axis=0, tiled=True)  11.9 us
    ppermute x1, waiting for transfers between devices, shards(): received = lax.ppermute(result, 'section', back_pairs)  10.9 us
  transfers between devices with their start and end apart: 25, of which 16 were waited for; matrix products, arithmetic and copies ran while one was open for 11% of the time, Pallas kernels for 5%

profile of v3, /device:TPU:1, one launch (start us, length us, event | category | flops | bytes accessed | tf_op | source)
XLA Modules:
  0.0 525.6 jit_solution(9196468918436480257)
XLA Ops:
  12.1 4.5 collective-permute-start.1
  28.7 2.9 reshape_squeeze.3
  34.3 8.5 %all-to-all-start = ((bf16[16,64,384]{2,1,0:T(8,128)(2,1)}), bf16[16,64,384]{2,1,0:T(8,128)(2,1)S(1)}, u32[]{:S(2)}, u32[]{:S(2)}) async-start(bf16[16,64,384]{2,1,0:T(8,128)(2,1)} %bitcast.14), calls=%async_computation | async-start | bytes 1572864 | tf_op jit(solution)/shard_map/all_to_all | solution.py:206
  48.6 8.3 %all-to-all-done = bf16[16,64,384]{2,1,0:T(8,128)(2,1)S(1)} async-done(((bf16[16,64,384]{2,1,0:T(8,128)(2,1)}), bf16[16,64,384]{2,1,0:T(8,128)(2,1)S(1)}, u32[]{:S(2)}, u32[]{:S(2)}) %all-to-all-start) | async-done | bytes 786464 | tf_op jit(solution)/shard_map/all_to_all | solution.py:206
  61.3 6.9 %collective-permute-done.4 = bf16[192,576]{0,1:T(8,128)(2,1)} collective-permute-done((bf16[192,576]{0,1:T(8,128)(2,1)}, bf16[192,576]{0,1:T(8,128)(2,1)}, u32[]{:S(2)}, u32[]{:S(2)}) %collective-permute-start.4) | collective-permute-done | bytes 221216 | tf_op jit(solution)/shard_map/ppermute | solution.py:230
  72.3 11.2 %shard_map.178 = (bf16[1024,576]{1,0:T(8,128)(2,1)}, bf16[1024,192]{1,0:T(8,128)(2,1)}, f32[8,1024]{1,0:T(8,128)}) custom-call(s32[1,1024]{1,0:T(1,128)S(1)} %add.292.row_places, s32[1024,1]{1,0:T(8,128)S(1)} %add.350.column_places, bf16[1024,384]{1,0:T(8,128)(2,1)S(1)} %bitcast.236, bf16[1024,384]{1,0:T(8,128)(2,1)S(1)} %collective-permute-done.3.other, ...), custom_call_target="tpu_custom_call" | custom-call | flops 805306368 | bytes 1572864 | tf_op jit(solution)/shard_map/pallas_call | solution.py:69
  83.4 9.6 %all-to-all-start.1 = ((bf16[16,64,192]{2,1,0:T(8,128)(2,1)}), bf16[16,64,192]{2,1,0:T(8,128)(2,1)S(1)}, u32[]{:S(2)}, u32[]{:S(2)}) async-start(bf16[16,64,192]{2,1,0:T(8,128)(2,1)} %bitcast.25), calls=%async_computation.1 | async-start | bytes 1048576 | tf_op jit(solution)/shard_map/all_to_all | solution.py:206
  93.5 10.7 %all-to-all-done.1 = bf16[16,64,192]{2,1,0:T(8,128)(2,1)S(1)} async-done(((bf16[16,64,192]{2,1,0:T(8,128)(2,1)}), bf16[16,64,192]{2,1,0:T(8,128)(2,1)S(1)}, u32[]{:S(2)}, u32[]{:S(2)}) %all-to-all-start.1) | async-done | bytes 393248 | tf_op jit(solution)/shard_map/all_to_all | solution.py:206
  107.5 11.9 %all-gather.11.cloned.1.call-done = bf16[1,3072,768]{2,1,0:T(8,128)(2,1)} async-done(((bf16[1,384,768]{2,1,0:T(8,128)(2,1)}), bf16[1,3072,768]{2,1,0:T(8,128)(2,1)}) %all-gather.11.cloned.1.call-update) | async-done | bytes 4718608 | tf_op jit(solution)/shard_map/all_gather | solution.py:221
  119.4 7.6 %fusion.67 = bf16[256,768]{1,0:T(8,128)(2,1)} fusion(f32[256,768]{1,0:T(8,128)S(1)} %get-tuple-element.151, bf16[1,3072,768]{2,1,0:T(8,128)(2,1)} %all-gather.11.cloned.1.call-done, bf16[1,768,3072]{2,1,0:T(8,128)(2,1)} %all-gather.9.cloned.1.call-done, f32[3072]{0:T(1024)S(1)} %add.317, f32[768]{0:T(1024)S(1)} %add.323, f32[768]{0:T(1024)S(1)} %add.314, ...), kind=kOutput, calls=%fused_computation.66 | convolution fusion | flops 2425356288 | bytes 10640384 | tf_op jit(solution)/shard_map/tf,fd->td/dot_general | solution.py:180
  127.0 3.1 collective-permute-start.7
  130.3 8.4 %collective-permute-done.7 = bf16[256,768]{1,0:T(8,128)(2,1)S(1)} collective-permute-done((bf16[256,768]{1,0:T(8,128)(2,1)}, bf16[256,768]{1,0:T(8,128)(2,1)S(1)}, u32[]{:S(2)}, u32[]{:S(2)}) %collective-permute-start.7) | collective-permute-done | bytes 393248 | tf_op jit(solution)/shard_map/ppermute | solution.py:423
  139.7 22.1 %all_to_all.75 = bf16[16,64,384]{2,1,0:T(8,128)(2,1)S(1)} all-to-all(bf16[16,64,384]{2,1,0:T(8,128)(2,1)S(1)} %bitcast.256), channel_id=1, replica_groups=mesh['section'=2,'x'=4,'yh'=2,'core'=2,'fsdp'=4] {'x','yh','core'}, dimensions={0} | all-to-all | bytes 1572864 | tf_op jit(solution)/shard_map/all_to_all | solution.py:206
  164.3 10.4 %shard_map.179 = (bf16[1024,576]{1,0:T(8,128)(2,1)S(1)}, bf16[1024,192]{1,0:T(8,128)(2,1)S(1)}, f32[8,1024]{1,0:T(8,128)S(1)}) custom-call(s32[1,1024]{1,0:T(1,128)S(1)} %add.292.row_places, s32[1024,1]{1,0:T(8,128)S(1)} %add.350.column_places, bf16[1024,384]{1,0:T(8,128)(2,1)S(1)} %bitcast.233, bf16[1024,384]{1,0:T(8,128)(2,1)S(1)} %collective-permute-done.8.other, ...), custom_call_target="tpu_custom_call" | custom-call | flops 805306368 | bytes 1572864 | tf_op jit(solution)/shard_map/pallas_call | solution.py:69
  174.8 14.0 %all_to_all.76 = bf16[16,64,192]{2,1,0:T(8,128)(2,1)S(1)} all-to-all(bf16[16,64,192]{2,1,0:T(8,128)(2,1)S(1)} %bitcast.239), channel_id=1, replica_groups=mesh['section'=2,'x'=4,'yh'=2,'core'=2,'fsdp'=4] {'x','yh','core'}, dimensions={0} | all-to-all | bytes 786432 | tf_op jit(solution)/shard_map/all_to_all | solution.py:206
  189.7 3.2 fusion.22
  192.9 9.5 %fusion.119 = (f32[256]{0:T(256)S(1)}, f32[256]{0:T(256)S(1)}, f32[256,768]{1,0:T(8,128)}) fusion(f32[256]{0:T(256)S(1)} %add_rsqrt_fusion.1, f32[256,768]{1,0:T(8,128)} %copy-done.9, f32[256]{0:T(256)S(1)} %broadcast_multiply_fusion.9, f32[768]{0:T(1024)S(1)} %mul.316, bf16[1,768,3072]{2,1,0:T(8,128)(2,1)} %all-gather.9.cloned.1.call-done, ...), kind=kOutput, calls=%fused_computation.190 | convolution fusion | flops 2432826880 | bytes 14556160 | tf_op jit(solution)/shard_map/tf,df->td/dot_general | solution.py:180
  202.4 2.8 fusion.120
  205.8 15.4 %all_to_all.77 = bf16[16,64,192]{2,1,0:T(8,128)(2,1)S(1)} all-to-all(bf16[16,64,192]{2,1,0:T(8,128)(2,1)S(1)} %bitcast.265), channel_id=1, replica_groups=mesh['section'=2,'x'=4,'yh'=2,'core'=2,'fsdp'=4] {'x','yh','core'}, dimensions={0} | all-to-all | bytes 786432 | tf_op jit(solution)/shard_map/all_to_all | solution.py:206
  221.2 15.5 %shard_map.180 = (bf16[1024,576]{1,0:T(8,128)(2,1)}, bf16[1024,384]{1,0:T(8,128)(2,1)S(1)}, bf16[1024,384]{1,0:T(8,128)(2,1)S(1)}) custom-call(s32[1,1024]{1,0:T(1,128)S(1)} %add.292.row_places, s32[1024,1]{1,0:T(8,128)S(1)} %add.350.column_places, bf16[1024,576]{1,0:T(8,128)(2,1)} %copy-done.6, bf16[1024,192]{1,0:T(8,128)(2,1)S(1)} %bitcast.238, ...), custom_call_target="tpu_custom_call" | custom-call | flops 2013265920 | bytes 3145728 | tf_op jit(solution)/shard_map/pallas_call | solution.py:149
  240.2 17.4 %all_to_all.78 = bf16[16,64,384]{2,1,0:T(8,128)(2,1)S(1)} all-to-all(bf16[16,64,384]{2,1,0:T(8,128)(2,1)S(1)} %bitcast.258), channel_id=1, replica_groups=mesh['section'=2,'x'=4,'yh'=2,'core'=2,'fsdp'=4] {'x','yh','core'}, dimensions={0} | all-to-all | bytes 1572864 | tf_op jit(solution)/shard_map/all_to_all | solution.py:206
  265.2 10.9 %collective-permute-done.10 = bf16[256,768]{1,0:T(8,128)(2,1)} collective-permute-done((bf16[256,768]{1,0:T(8,128)(2,1)}, bf16[256,768]{1,0:T(8,128)(2,1)}, u32[]{:S(2)}, u32[]{:S(2)}) %collective-permute-start.10) | collective-permute-done | bytes 393248 | tf_op jit(solution)/shard_map/ppermute | solution.py:431
  277.3 6.5 %convolution_convert_fusion.1 = bf16[3072,768]{1,0:T(8,128)(2,1)} fusion(bf16[256,768]{1,0:T(8,128)(2,1)S(1)} %get-tuple-element.106, f32[256,3072]{1,0:T(8,128)} %fusion.22), kind=kOutput, calls=%fused_computation.2 | convolution fusion | flops 1217396736 | bytes 8257536 | tf_op jit(solution)/shard_map/tf,td->fd/dot_general | solution.py:180
  283.8 5.3 %convert_reduce_fusion = (f32[3072]{0:T(1024)S(1)}, bf16[256,3072]{1,0:T(8,128)(2,1)S(1)}) fusion(f32[256,3072]{1,0:T(8,128)S(1)} %copy-done.37, bf16[256,768]{1,0:T(8,128)(2,1)S(1)} %get-tuple-element.106, bf16[1,3072,768]{2,1,0:T(8,128)(2,1)} %all-gather.11.cloned.1.call-done), kind=kOutput, calls=%fused_computation.37 | convolution fusion | flops 1225257984 | bytes 9842688 | tf_op jit(solution)/shard_map/td,fd->tf/dot_general | solution.py:180
  289.1 3.7 convolution_convert_fusion
  297.1 9.7 %reshape.545 = bf16[8,96,4,768]{3,2,1,0:T(4,128)(2,1)} reshape(bf16[768,3072]{1,0:T(8,128)(2,1)} %convolution_convert_fusion) | data formatting | bytes 9437184 | tf_op jit(solution)/shard_map/reshape | solution.py:365
  306.9 3.4 copy.164
  310.8 5.8 %maximum_maximum_fusion = bf16[8,896,768]{2,1,0:T(8,128)(2,1)} fusion(bf16[8,96,768]{2,1,0:T(8,128)(2,1)S(1)} %bitcast.272, bf16[8,384,768]{2,1,0:T(8,128)(2,1)S(1)} %bitcast.242, bf16[8,384,768]{2,1,0:T(8,128)(2,1)S(1)} %bitcast.255, bf16[896]{0:T(1024)(128)(2,1)S(1)} %pad.7.clone), kind=kLoop, calls=%fused_computation | loop fusion | flops 44040192 | bytes 21628672 | tf_op jit(solution)/shard_map/concatenate | solution.py:372
  316.7 15.2 %all_to_all.79 = bf16[16,64,192]{2,1,0:T(8,128)(2,1)S(1)} all-to-all(bf16[16,64,192]{2,1,0:T(8,128)(2,1)S(1)} %bitcast.266), channel_id=1, replica_groups=mesh['section'=2,'x'=4,'yh'=2,'core'=2,'fsdp'=4] {'x','yh','core'}, dimensions={0} | all-to-all | bytes 786432 | tf_op jit(solution)/shard_map/all_to_all | solution.py:206
  333.0 14.5 %shard_map.181 = (bf16[1024,576]{1,0:T(8,128)(2,1)S(1)}, bf16[1024,384]{1,0:T(8,128)(2,1)S(1)}, bf16[1024,384]{1,0:T(8,128)(2,1)S(1)}) custom-call(s32[1,1024]{1,0:T(1,128)S(1)} %add.292.row_places, s32[1024,1]{1,0:T(8,128)S(1)} %copy-done.3, bf16[1024,576]{1,0:T(8,128)(2,1)} %copy-done.6, bf16[1024,192]{1,0:T(8,128)(2,1)S(1)} %bitcast.237, ...), custom_call_target="tpu_custom_call" | custom-call | flops 2013265920 | bytes 3145728 | tf_op jit(solution)/shard_map/pallas_call | solution.py:149
  351.0 17.4 %all_to_all.80 = bf16[16,64,384]{2,1,0:T(8,128)(2,1)S(1)} all-to-all(bf16[16,64,384]{2,1,0:T(8,128)(2,1)S(1)} %bitcast.259), channel_id=1, replica_groups=mesh['section'=2,'x'=4,'yh'=2,'core'=2,'fsdp'=4] {'x','yh','core'}, dimensions={0} | all-to-all | bytes 1572864 | tf_op jit(solution)/shard_map/all_to_all | solution.py:206
  370.5 7.3 %reduce-scatter.2.cloned.1.call-done = bf16[896,768]{1,0:T(8,128)(2,1)} async-done(((bf16[7168,768]{1,0:T(8,128)(2,1)}), bf16[896,768]{1,0:T(8,128)(2,1)}) %reduce-scatter.2.cloned.1.call-update) | async-done | bytes 1376272 | tf_op jit(solution)/shard_map/reduce_scatter | solution.py:374
  377.8 6.4 %all-to-all-start.10 = ((bf16[8,112,768]{2,1,0:T(8,128)(2,1)}), bf16[8,112,768]{2,1,0:T(8,128)(2,1)}, u32[]{:S(2)}, u32[]{:S(2)}) async-start(bf16[8,112,768]{2,1,0:T(8,128)(2,1)} %bitcast.271), calls=%async_computation.11 | async-start | bytes 2752512 | tf_op jit(solution)/shard_map/all_to_all | solution.py:206
  387.3 16.0 %all-to-all-done.10 = bf16[8,112,768]{2,1,0:T(8,128)(2,1)} async-done(((bf16[8,112,768]{2,1,0:T(8,128)(2,1)}), bf16[8,112,768]{2,1,0:T(8,128)(2,1)}, u32[]{:S(2)}, u32[]{:S(2)}) %all-to-all-start.10) | async-done | bytes 1376288 | tf_op jit(solution)/shard_map/all_to_all | solution.py:206
  403.3 8.0 %all-to-all-start.8 = ((bf16[16,48,576]{2,1,0:T(8,128)(2,1)}), bf16[16,48,576]{2,1,0:T(8,128)(2,1)S(1)}, u32[]{:S(2)}, u32[]{:S(2)}) async-start(bf16[16,48,576]{2,1,0:T(8,128)(2,1)} %bitcast.81), calls=%async_computation.9 | async-start | bytes 1966080 | tf_op jit(solution)/shard_map/all_to_all | solution.py:206
  412.8 14.1 %all-to-all-done.8 = bf16[16,48,576]{2,1,0:T(8,128)(2,1)S(1)} async-done(((bf16[16,48,576]{2,1,0:T(8,128)(2,1)}), bf16[16,48,576]{2,1,0:T(8,128)(2,1)S(1)}, u32[]{:S(2)}, u32[]{:S(2)}) %all-to-all-start.8) | async-done | bytes 884768 | tf_op jit(solution)/shard_map/all_to_all | solution.py:206
  428.1 4.6 all-to-all-start.11
  432.8 18.7 %all-to-all-done.11 = bf16[8,112,768]{2,1,0:T(8,128)(2,1)} async-done(((bf16[8,112,768]{2,1,0:T(8,128)(2,1)}), bf16[8,112,768]{2,1,0:T(8,128)(2,1)}, u32[]{:S(2)}, u32[]{:S(2)}) %all-to-all-start.11) | async-done | bytes 1376288 | tf_op jit(solution)/shard_map/all_to_all | solution.py:206
  452.5 5.7 %all-to-all-start.9 = ((bf16[16,48,576]{2,1,0:T(8,128)(2,1)}), bf16[16,48,576]{2,1,0:T(8,128)(2,1)S(1)}, u32[]{:S(2)}, u32[]{:S(2)}) async-start(bf16[16,48,576]{2,1,0:T(8,128)(2,1)} %broadcast_in_dim.147), calls=%async_computation.10 | async-start | bytes 1966080 | tf_op jit(solution)/shard_map/all_to_all | solution.py:206
  458.2 6.0 %fusion.64 = bf16[256,768]{1,0:T(8,128)(2,1)} fusion(f32[256,768]{1,0:T(8,128)S(1)} %copy-done.11, bf16[1,3072,768]{2,1,0:T(8,128)(2,1)} %all-gather.11.cloned.1.call-done, f32[768]{0:T(1024)S(1)} %add.323, f32[256,3072]{1,0:T(8,128)} %fusion.22), kind=kOutput, calls=%fused_computation.65 | convolution fusion | flops 1215627264 | bytes 9047040 | tf_op jit(solution)/shard_map/tf,fd->td/dot_general | solution.py:180
  468.3 6.4 %all-to-all-done.9 = bf16[16,48,576]{2,1,0:T(8,128)(2,1)S(1)} async-done(((bf16[16,48,576]{2,1,0:T(8,128)(2,1)}), bf16[16,48,576]{2,1,0:T(8,128)(2,1)S(1)}, u32[]{:S(2)}, u32[]{:S(2)}) %all-to-all-start.9) | async-done | bytes 884768 | tf_op jit(solution)/shard_map/all_to_all | solution.py:206
  474.7 2.9 reshape.567
  477.6 3.4 copy.170
  481.1 2.8 reshape.566
  486.7 3.3 all-to-all-start.12
  490.0 4.3 all-to-all-done.12
  495.1 5.3 %all-to-all-start.13 = ((f32[16,1,2304]{2,1,0:T(1,128)}), f32[16,1,2304]{2,1,0:T(1,128)S(1)}, u32[]{:S(2)}, u32[]{:S(2)}) async-start(f32[16,1,2304]{2,1,0:T(1,128)} %broadcast_in_dim.153), calls=%async_computation.14 | async-start | bytes 294912 | tf_op jit(solution)/shard_map/all_to_all | solution.py:206
  502.6 5.7 %all-to-all-done.13 = f32[16,1,2304]{2,1,0:T(1,128)S(1)} async-done(((f32[16,1,2304]{2,1,0:T(1,128)}), f32[16,1,2304]{2,1,0:T(1,128)S(1)}, u32[]{:S(2)}, u32[]{:S(2)}) %all-to-all-start.13) | async-done | bytes 147488 | tf_op jit(solution)/shard_map/all_to_all | solution.py:206
  (263 shorter events, 85.6 us)
Async XLA Ops:
  7.2 20.4 %copy-start.18 = (bf16[4,1,64,768]{3,2,1,0:T(8,128)(2,1)S(1)}, bf16[4,1,64,768]{3,2,1,0:T(8,128)(2,1)}, u32[]{:S(2)}) copy-start(bf16[4,1,64,768]{3,2,1,0:T(8,128)(2,1)} %param.11) | copy-start | bytes 1179652
  7.2 97.8 %all-gather.7.cloned.1.call-start = ((), (), s32[]{:S(2)}) async-start(), calls=%async_computation.16 | async-start | bytes 1327104 | tf_op jit(solution)/shard_map/all_gather | solution.py:221
  9.0 98.5 %all-gather.9.cloned.1.call-start = ((), (), s32[]{:S(2)}) async-start(), calls=%async_computation.17 | async-start | bytes 5308416 | tf_op jit(solution)/shard_map/all_gather | solution.py:221
  10.0 109.4 %all-gather.11.cloned.1.call-start = ((), (), s32[]{:S(2)}) async-start(), calls=%async_computation.18 | async-start | bytes 5308416 | tf_op jit(solution)/shard_map/all_gather | solution.py:221
  12.1 19.5 %collective-permute-start.1 = (bf16[12,192]{1,0:T(8,128)(2,1)S(1)}, bf16[12,192]{1,0:T(8,128)(2,1)S(1)}, u32[]{:S(2)}, u32[]{:S(2)}) collective-permute-start(bf16[12,192]{1,0:T(8,128)(2,1)S(1)} %pad_maximum_fusion.4), channel_id=1, source_target_pairs={{0,2},{1,3},{2,0},{3,1},{4,6},{5,7},{6,4},{7,5},{8,10},{9,11},{10,... | collective-permute-start | bytes 13832 | tf_op jit(solution)/shard_map/ppermute | solution.py:230
  16.6 15.0 %collective-permute-start = (bf16[12,192]{1,0:T(8,128)(2,1)S(1)}, bf16[12,192]{1,0:T(8,128)(2,1)S(1)}, u32[]{:S(2)}, u32[]{:S(2)}) collective-permute-start(bf16[12,192]{1,0:T(8,128)(2,1)S(1)} %pad_maximum_fusion.4), channel_id=1, source_target_pairs={{0,1},{1,2},{2,3},{3,0},{4,5},{5,6},{6,7},{7,4},{8,9},{9,10},{10,1... | collective-permute-start | bytes 13832 | tf_op jit(solution)/shard_map/ppermute | solution.py:230
  17.4 14.3 %collective-permute-start.2 = (bf16[12,192]{1,0:T(8,128)(2,1)S(1)}, bf16[12,192]{1,0:T(8,128)(2,1)S(1)}, u32[]{:S(2)}, u32[]{:S(2)}) collective-permute-start(bf16[12,192]{1,0:T(8,128)(2,1)S(1)} %pad_maximum_fusion.4), channel_id=1, source_target_pairs={{0,3},{1,0},{2,1},{3,2},{4,7},{5,4},{6,5},{7,6},{8,11},{9,8},{10,9... | collective-permute-start | bytes 13832 | tf_op jit(solution)/shard_map/ppermute | solution.py:230
  32.3 12.5 %copy-start.19 = (f32[4,192]{1,0:T(4,128)}, f32[4,192]{1,0:T(4,128)S(1)}, u32[]{:S(2)}) copy-start(f32[4,192]{1,0:T(4,128)S(1)} %get-tuple-element.103) | copy-start | bytes 9220
  32.3 12.5 %copy-start.21 = (f32[4,192]{1,0:T(4,128)}, f32[4,192]{1,0:T(4,128)S(1)}, u32[]{:S(2)}) copy-start(f32[4,192]{1,0:T(4,128)S(1)} %get-tuple-element.104) | copy-start | bytes 9220
  32.5 13.9 %copy-start.36 = (s32[32]{0:T(128)S(1)}, s32[32]{0:T(128)}, u32[]{:S(2)}) copy-start(s32[32]{0:T(128)} %param.14) | copy-start | bytes 388
  34.3 22.6 %all-to-all-start = ((bf16[16,64,384]{2,1,0:T(8,128)(2,1)}), bf16[16,64,384]{2,1,0:T(8,128)(2,1)S(1)}, u32[]{:S(2)}, u32[]{:S(2)}) async-start(bf16[16,64,384]{2,1,0:T(8,128)(2,1)} %bitcast.14), calls=%async_computation | async-start | bytes 1572864 | tf_op jit(solution)/shard_map/all_to_all | solution.py:206
  44.8 13.5 %collective-permute-start.6 = (bf16[192,576]{0,1:T(8,128)(2,1)}, bf16[192,576]{0,1:T(8,128)(2,1)}, u32[]{:S(2)}, u32[]{:S(2)}) collective-permute-start(bf16[192,576]{0,1:T(8,128)(2,1)} %bitcast.17), channel_id=1, source_target_pairs={{0,3},{1,0},{2,1},{3,2},{4,7},{5,4},{6,5},{7,6},{8,11},{9,8},{10,9... | collective-permute-start | bytes 663560 | tf_op jit(solution)/shard_map/ppermute | solution.py:230
  44.9 14.6 %collective-permute-start.5 = (bf16[192,576]{0,1:T(8,128)(2,1)}, bf16[192,576]{0,1:T(8,128)(2,1)}, u32[]{:S(2)}, u32[]{:S(2)}) collective-permute-start(bf16[192,576]{0,1:T(8,128)(2,1)} %bitcast.17), channel_id=1, source_target_pairs={{0,2},{1,3},{2,0},{3,1},{4,6},{5,7},{6,4},{7,5},{8,10},{9,11},{10,... | collective-permute-start | bytes 663560 | tf_op jit(solution)/shard_map/ppermute | solution.py:230
  46.2 22.0 %collective-permute-start.4 = (bf16[192,576]{0,1:T(8,128)(2,1)}, bf16[192,576]{0,1:T(8,128)(2,1)}, u32[]{:S(2)}, u32[]{:S(2)}) collective-permute-start(bf16[192,576]{0,1:T(8,128)(2,1)} %bitcast.17), channel_id=1, source_target_pairs={{0,1},{1,2},{2,3},{3,0},{4,5},{5,6},{6,7},{7,4},{8,9},{9,10},{10,1... | collective-permute-start | bytes 663560 | tf_op jit(solution)/shard_map/ppermute | solution.py:230
  47.1 174.2 %copy-start.2 = (s32[1024,1]{1,0:T(8,128)}, s32[1024,1]{1,0:T(8,128)S(1)}, u32[]{:S(2)}) copy-start(s32[1024,1]{1,0:T(8,128)S(1)} %add.350.column_places) | copy-start | bytes 12292
  56.9 15.3 %collective-permute-start.3 = (bf16[1024,384]{1,0:T(8,128)(2,1)S(1)}, bf16[1024,384]{1,0:T(8,128)(2,1)S(1)}, u32[]{:S(2)}, u32[]{:S(2)}) collective-permute-start(bf16[1024,384]{1,0:T(8,128)(2,1)S(1)} %bitcast.235), channel_id=1, source_target_pairs={{0,4},{4,0},{1,5},{5,1},{2,6},{6,2},{3,7},{7,3},{8,12},{12,8},{9,1... | collective-permute-start | bytes 2359304 | tf_op jit(solution)/shard_map/ppermute | solution.py:210
  72.2 21.0 %copy-start.28 = (f32[4,192]{1,0:T(4,128)S(1)}, f32[4,192]{1,0:T(4,128)}, u32[]{:S(2)}) copy-start(f32[4,192]{1,0:T(4,128)} %get-tuple-element.99) | copy-start | bytes 9220
  72.2 21.0 %copy-start.27 = (f32[4,192]{1,0:T(4,128)S(1)}, f32[4,192]{1,0:T(4,128)}, u32[]{:S(2)}) copy-start(f32[4,192]{1,0:T(4,128)} %get-tuple-element.101) | copy-start | bytes 9220
  72.2 21.1 %copy-start.26 = (f32[4,192]{1,0:T(4,128)S(1)}, f32[4,192]{1,0:T(4,128)}, u32[]{:S(2)}) copy-start(f32[4,192]{1,0:T(4,128)} %get-tuple-element.100) | copy-start | bytes 9220
  72.2 21.2 %copy-start.25 = (f32[4,192]{1,0:T(4,128)S(1)}, f32[4,192]{1,0:T(4,128)}, u32[]{:S(2)}) copy-start(f32[4,192]{1,0:T(4,128)} %get-tuple-element.102) | copy-start | bytes 9220
  83.4 20.8 %all-to-all-start.1 = ((bf16[16,64,192]{2,1,0:T(8,128)(2,1)}), bf16[16,64,192]{2,1,0:T(8,128)(2,1)S(1)}, u32[]{:S(2)}, u32[]{:S(2)}) async-start(bf16[16,64,192]{2,1,0:T(8,128)(2,1)} %bitcast.25), calls=%async_computation.1 | async-start | bytes 1048576 | tf_op jit(solution)/shard_map/all_to_all | solution.py:206
  93.0 284.7 %reduce-scatter.2.cloned.1.call-start = ((), (), s32[]{:S(2)}) async-start(), calls=%async_computation.15 | async-start | bytes 12386304 | tf_op jit(solution)/shard_map/reduce_scatter | solution.py:374
  107.5 22.7 %copy-start.22 = (f32[4,192]{1,0:T(4,128)S(1)}, f32[4,192]{1,0:T(4,128)}, u32[]{:S(2)}) copy-start(f32[4,192]{1,0:T(4,128)} %copy-done.21) | copy-start | bytes 9220
  107.5 22.8 %copy-start.20 = (f32[4,192]{1,0:T(4,128)S(1)}, f32[4,192]{1,0:T(4,128)}, u32[]{:S(2)}) copy-start(f32[4,192]{1,0:T(4,128)} %copy-done.19) | copy-start | bytes 9220
  107.5 31.2 %copy-start.14 = (bf16[4,1,64,768]{3,2,1,0:T(8,128)(2,1)S(1)}, bf16[4,1,64,768]{3,2,1,0:T(8,128)(2,1)}, u32[]{:S(2)}) copy-start(bf16[4,1,64,768]{3,2,1,0:T(8,128)(2,1)} %copy-done.13) | copy-start | bytes 1179652
  127.0 11.7 %collective-permute-start.7 = (bf16[256,768]{1,0:T(8,128)(2,1)}, bf16[256,768]{1,0:T(8,128)(2,1)S(1)}, u32[]{:S(2)}, u32[]{:S(2)}) collective-permute-start(bf16[256,768]{1,0:T(8,128)(2,1)} %fusion.67), channel_id=1, source_target_pairs={{0,64},{1,65},{2,66},{3,67},{4,68},{5,69},{6,70},{7,71},{8,72},{9,... | collective-permute-start | bytes 1179656 | tf_op jit(solution)/shard_map/ppermute | solution.py:423
  138.9 122.6 %copy-start.7 = (bf16[256,768]{1,0:T(8,128)(2,1)}, bf16[256,768]{1,0:T(8,128)(2,1)S(1)}, u32[]{:S(2)}) copy-start(bf16[256,768]{1,0:T(8,128)(2,1)S(1)} %get-tuple-element.115) | copy-start | bytes 1179652
  139.7 50.0 %slice-start.2 = ((s8[4718592]{0:T(1024)(128)(4,1)}), s8[4194304]{0:T(1024)(128)(4,1)S(1)}, s32[]{:S(2)}) async-start(s8[4718592]{0:T(1024)(128)(4,1)} %bitcast.294), calls=%async_computation.21 | async-start | bytes 8388608
  161.8 27.1 %copy-start.33 = (bf16[1,768,768]{2,1,0:T(8,128)(2,1)S(1)}, bf16[1,768,768]{2,1,0:T(8,128)(2,1)}, u32[]{:S(2)}) copy-start(bf16[1,768,768]{2,1,0:T(8,128)(2,1)} %all-gather.7.cloned.1.call-done) | copy-start | bytes 3538948
  161.8 27.9 %slice-start.3 = ((s8[4718592]{0:T(1024)(128)(4,1)}), s8[524288]{0:T(1024)(128)(4,1)S(1)}, s32[]{:S(2)}) async-start(s8[4718592]{0:T(1024)(128)(4,1)} %bitcast.294), calls=%async_computation.22 | async-start | bytes 1048576
  161.8 2.5 collective-permute-start.8
  164.3 24.5 %copy-start.4 = (bf16[1024,384]{1,0:T(8,128)(2,1)}, bf16[1024,384]{1,0:T(8,128)(2,1)S(1)}, u32[]{:S(2)}) copy-start(bf16[1024,384]{1,0:T(8,128)(2,1)S(1)} %collective-permute-done.8.other) | copy-start | bytes 2359300
  174.8 18.1 %copy-start.6 = (bf16[1024,576]{1,0:T(8,128)(2,1)}, bf16[1024,576]{1,0:T(8,128)(2,1)S(1)}, u32[]{:S(2)}) copy-start(bf16[1024,576]{1,0:T(8,128)(2,1)S(1)} %get-tuple-element.24.joined) | copy-start | bytes 3538948
  236.7 3.3 collective-permute-start.9
  240.0 17.7 %copy-start.24 = (f32[2,384]{1,0:T(2,128)S(1)}, f32[2,384]{1,0:T(2,128)}, u32[]{:S(2)}) copy-start(f32[2,384]{1,0:T(2,128)} %copy-done.23) | copy-start | bytes 9220
  259.9 16.3 %copy-start.15 = (bf16[4,1,64,768]{3,2,1,0:T(8,128)(2,1)S(1)}, bf16[4,1,64,768]{3,2,1,0:T(8,128)(2,1)}, u32[]{:S(2)}) copy-start(bf16[4,1,64,768]{3,2,1,0:T(8,128)(2,1)} %param.12) | copy-start | bytes 1179652
  263.7 12.5 %collective-permute-start.10 = (bf16[256,768]{1,0:T(8,128)(2,1)}, bf16[256,768]{1,0:T(8,128)(2,1)}, u32[]{:S(2)}, u32[]{:S(2)}) collective-permute-start(bf16[256,768]{1,0:T(8,128)(2,1)} %fusion.91), channel_id=1, source_target_pairs={{64,0},{65,1},{66,2},{67,3},{68,4},{69,5},{70,6},{71,7},{72,8},{73... | collective-permute-start | bytes 1179656 | tf_op jit(solution)/shard_map/ppermute | solution.py:431
  277.3 15.5 %slice-start.4 = ((s8[4718592]{0:T(1024)(128)(4,1)}), s8[4194304]{0:T(1024)(128)(4,1)S(1)}, s32[]{:S(2)}) async-start(s8[4718592]{0:T(1024)(128)(4,1)} %bitcast.296), calls=%async_computation.23 | async-start | bytes 8388608
  347.4 3.3 collective-permute-start.11
  368.5 15.7 %copy-start.5 = (bf16[1024,384]{1,0:T(8,128)(2,1)S(1)}, bf16[1024,384]{1,0:T(8,128)(2,1)}, u32[]{:S(2)}) copy-start(bf16[1024,384]{1,0:T(8,128)(2,1)} %copy-done.4) | copy-start | bytes 2359300
  377.8 25.5 %all-to-all-start.10 = ((bf16[8,112,768]{2,1,0:T(8,128)(2,1)}), bf16[8,112,768]{2,1,0:T(8,128)(2,1)}, u32[]{:S(2)}, u32[]{:S(2)}) async-start(bf16[8,112,768]{2,1,0:T(8,128)(2,1)} %bitcast.271), calls=%async_computation.11 | async-start | bytes 2752512 | tf_op jit(solution)/shard_map/all_to_all | solution.py:206
  403.3 23.6 %all-to-all-start.8 = ((bf16[16,48,576]{2,1,0:T(8,128)(2,1)}), bf16[16,48,576]{2,1,0:T(8,128)(2,1)S(1)}, u32[]{:S(2)}, u32[]{:S(2)}) async-start(bf16[16,48,576]{2,1,0:T(8,128)(2,1)} %bitcast.81), calls=%async_computation.9 | async-start | bytes 1966080 | tf_op jit(solution)/shard_map/all_to_all | solution.py:206
  428.1 30.2 %copy-start.11 = (f32[256,768]{1,0:T(8,128)S(1)}, f32[256,768]{1,0:T(8,128)}, u32[]{:S(2)}) copy-start(f32[256,768]{1,0:T(8,128)} %copy-done.9) | copy-start | bytes 2359300
  428.1 23.4 %all-to-all-start.11 = ((bf16[8,112,768]{2,1,0:T(8,128)(2,1)}), bf16[8,112,768]{2,1,0:T(8,128)(2,1)}, u32[]{:S(2)}, u32[]{:S(2)}) async-start(bf16[8,112,768]{2,1,0:T(8,128)(2,1)} %broadcast_in_dim.148), calls=%async_computation.12 | async-start | bytes 2752512 | tf_op jit(solution)/shard_map/all_to_all | solution.py:206
  452.5 22.2 %all-to-all-start.9 = ((bf16[16,48,576]{2,1,0:T(8,128)(2,1)}), bf16[16,48,576]{2,1,0:T(8,128)(2,1)S(1)}, u32[]{:S(2)}, u32[]{:S(2)}) async-start(bf16[16,48,576]{2,1,0:T(8,128)(2,1)} %broadcast_in_dim.147), calls=%async_computation.10 | async-start | bytes 1966080 | tf_op jit(solution)/shard_map/all_to_all | solution.py:206
  467.2 43.2 %collective-permute-start.12 = (bf16[896,768]{1,0:T(8,128)(2,1)}, bf16[896,768]{1,0:T(8,128)(2,1)}, u32[]{:S(2)}, u32[]{:S(2)}) collective-permute-start(bf16[896,768]{1,0:T(8,128)(2,1)} %bitcast.84), channel_id=1, source_target_pairs={{0,4},{4,0},{1,5},{5,1},{2,6},{6,2},{3,7},{7,3},{8,12},{12,8},{9,1... | collective-permute-start | bytes 4128776 | tf_op jit(solution)/shard_map/ppermute | solution.py:210
  486.7 7.6 %all-to-all-start.12 = ((f32[4,1,2304]{2,1,0:T(1,128)}), f32[4,1,2304]{2,1,0:T(1,128)S(1)}, u32[]{:S(2)}, u32[]{:S(2)}) async-start(f32[4,1,2304]{2,1,0:T(1,128)} %copy.172), calls=%async_computation.13 | async-start | bytes 73728 | tf_op jit(solution)/shard_map/all_to_all | solution.py:206
  495.1 13.2 %all-to-all-start.13 = ((f32[16,1,2304]{2,1,0:T(1,128)}), f32[16,1,2304]{2,1,0:T(1,128)S(1)}, u32[]{:S(2)}, u32[]{:S(2)}) async-start(f32[16,1,2304]{2,1,0:T(1,128)} %broadcast_in_dim.153), calls=%async_computation.14 | async-start | bytes 294912 | tf_op jit(solution)/shard_map/all_to_all | solution.py:206
  (21 other events, 98.9 us)
Sparse Core Ops, SparseCore 0:
  9.8 27.4 all-gather.6
  39.5 43.2 all-gather.8
  85.2 34.2 all-gather.10
  316.8 60.9 reduce-scatter.1

commit v4 on v3

--- a/solution.py
+++ b/solution.py
@@ -13,6 +13,7 @@
 WIDTH = GROUP_HEADS * HDIM
 QUERY_BLOCK = 256
 EXTRA = 32
+JOINT_ROWS = 112
 CTX = ("x", "yh", "core")
 
 epsilon = 1e-05
@@ -176,6 +177,149 @@
     )(row_places, column_places, joined, grad_mixed, log_total, weight)
 
 
+def weight_grads_body(
+    active, grad_low, normed_two, grad_hidden, mixed, grad_attn, joint
+):
+    down_rows, up_rows = active.shape[1], normed_two.shape[0]
+    width = grad_low.shape[1]
+    joint[0, :down_rows, :] = dot(active[...], grad_low[...], 0, 0).astype(jnp.bfloat16)
+    place = down_rows
+    for panel in range(grad_hidden.shape[1] // width):
+        product = dot(normed_two[...], grad_hidden[:, panel * width : (panel + 1) * width], 1, 0)
+        joint[0, place : place + up_rows, :] = product.astype(jnp.bfloat16)
+        place += up_rows
+    joint[0, place : place + up_rows, :] = dot(mixed[...], grad_attn[...], 1, 0).astype(
+        jnp.bfloat16
+    )
+    place += up_rows
+    joint[0, place:, :] = jnp.zeros_like(joint[0, place:, :])
+
+
+def weight_grads(active, grad_low, normed_two, grad_hidden, mixed, grad_attn, members):
+    rows, hidden_width = active.shape
+    width = grad_low.shape[1]
+    down_rows, up_rows = hidden_width // members, width // members
+    out_rows = 2 * down_rows + up_rows + EXTRA
+    return pl.pallas_call(
+        weight_grads_body,
+        grid=(members,),
+        in_specs=[
+            pl.BlockSpec((rows, down_rows), lambda i: (0, i)),
+            whole(rows, width),
+            pl.BlockSpec((up_rows, rows), lambda i: (i, 0)),
+            whole(rows, hidden_width),
+            pl.BlockSpec((up_rows, rows), lambda i: (i, 0)),
+            whole(rows, width),
+        ],
+        out_specs=pl.BlockSpec((1, out_rows, width), lambda i: (i, 0, 0)),
+        out_shape=jax.ShapeDtypeStruct((members, out_rows, width), jnp.bfloat16),
+        compiler_params=pltpu.CompilerParams(vmem_limit_bytes=48 << 20),
+        cost_estimate=pl.CostEstimate(
+            flops=2 * rows * width * (2 * hidden_width + width),
+            bytes_accessed=2 * members * out_rows * width,
+            transcendentals=0,
+        ),
+    )(active, grad_low, normed_two, grad_hidden, mixed, grad_attn)
+
+
+def qkv_grads_body(core_id, own, other, grad_joined, pieces, sums):
+    first_core = core_id[0] == 0
+    grads = grad_joined[...]
+    count, piece_rows = pieces.shape[0], pieces.shape[1] - 16
+    per_half = count // 2
+    own_grads = dot(own[...], grads, 0, 0).astype(jnp.bfloat16)
+    other_grads = dot(other[...], grads, 0, 0).astype(jnp.bfloat16)
+    halves = (
+        jnp.where(first_core, own_grads, other_grads),
+        jnp.where(first_core, other_grads, own_grads),
+    )
+    for index in range(count):
+        start = (index % per_half) * piece_rows
+        pieces[index, :piece_rows, :] = halves[index // per_half][start : start + piece_rows, :]
+        pieces[index, piece_rows:, :] = jnp.zeros_like(pieces[index, piece_rows:, :])
+    sums[...] = jnp.sum(grads.astype(jnp.float32), 0, keepdims=True)
+
+
+def qkv_grads(core_id, own, other, grad_joined, count):
+    rows, half = own.shape
+    width = grad_joined.shape[1]
+    piece_rows = 2 * half // count
+    return pl.pallas_call(
+        qkv_grads_body,
+        in_specs=[pl.BlockSpec(memory_space=pltpu.SMEM)]
+        + [pl.BlockSpec(memory_space=pltpu.VMEM)] * 3,
+        out_specs=[pl.BlockSpec(memory_space=pltpu.VMEM)] * 2,
+        out_shape=[
+            jax.ShapeDtypeStruct((count, piece_rows + 16, width), jnp.bfloat16),
+            jax.ShapeDtypeStruct((1, width), jnp.float32),
+        ],
+        compiler_params=pltpu.CompilerParams(vmem_limit_bytes=48 << 20),
+        cost_estimate=pl.CostEstimate(
+            flops=4 * rows * half * width, bytes_accessed=6 * rows * half, transcendentals=0
+        ),
+    )(core_id, own, other, grad_joined)
+
+
+def unpack_body(core_id, own, other, g_qkv, g_out, g_up, g_down, vectors):
+    first_core = core_id[0] == 0
+    count = own.shape[0]
+    width = own.shape[2]
+    joint_rows = JOINT_ROWS
+    piece_rows = own.shape[1] - joint_rows - 16
+    up_rows = g_up.shape[0] // 2
+    down_rows = g_down.shape[0] // 2
+    sums = [None] * 4
+    for core in range(2):
+        pick = first_core if core == 0 else jnp.logical_not(first_core)
+        joint = jnp.concatenate(
+            [
+                jnp.where(pick, own[i, :joint_rows, :], other[i, :joint_rows, :])
+                for i in range(count)
+            ],
+            0,
+        ).astype(jnp.float32)
+        g_down[core * down_rows : (core + 1) * down_rows, :] = joint[:down_rows]
+        place = down_rows
+        for panel in range(g_up.shape[1] // width):
+            g_up[core * up_rows : (core + 1) * up_rows, panel * width : (panel + 1) * width] = (
+                joint[place : place + up_rows]
+            )
+            place += up_rows
+        g_out[core * up_rows : (core + 1) * up_rows, :] = joint[place : place + up_rows]
+        for i in range(count):
+            x_id, group = i // 2, (i % 2) * 2 + core
+            piece = jnp.where(pick, own[i, joint_rows:, :], other[i, joint_rows:, :])
+            piece = piece.astype(jnp.float32)
+            for part in range(3):
+                start = part * width + group * WIDTH
+                g_qkv[x_id * piece_rows : (x_id + 1) * piece_rows, start : start + WIDTH] = piece[
+                    :piece_rows, part * WIDTH : (part + 1) * WIDTH
+                ]
+            row = piece[piece_rows : piece_rows + 1, :]
+            sums[x_id] = row if sums[x_id] is None else sums[x_id] + row
+    for x_id in range(4):
+        vectors[x_id : x_id + 1, :] = sums[x_id]
+
+
+def unpack(core_id, own, other, shard, hidden_width, hidden_shard):
+    width = own.shape[2]
+    return pl.pallas_call(
+        unpack_body,
+        in_specs=[pl.BlockSpec(memory_space=pltpu.SMEM)]
+        + [pl.BlockSpec(memory_space=pltpu.VMEM)] * 2,
+        out_specs=[pl.BlockSpec(memory_space=pltpu.VMEM)] * 5,
+        out_shape=[
+            jax.ShapeDtypeStruct((shard, 3 * width), jnp.float32),
+            jax.ShapeDtypeStruct((shard, width), jnp.float32),
+            jax.ShapeDtypeStruct((shard, hidden_width), jnp.float32),
+            jax.ShapeDtypeStruct((hidden_shard, width), jnp.float32),
+            jax.ShapeDtypeStruct((4, width), jnp.float32),
+        ],
+        compiler_params=pltpu.CompilerParams(vmem_limit_bytes=48 << 20),
+        cost_estimate=pl.CostEstimate(flops=0, bytes_accessed=12 << 20, transcendentals=0),
+    )(core_id, own, other)
+
+
 def cross(left_side, right_side, pattern):
     return jnp.einsum(pattern, left_side, right_side, preferred_element_type=jnp.float32)
 
@@ -219,17 +363,6 @@
     half = weight.shape[1] // 2
     own = lax.dynamic_slice_in_dim(weight[0], lax.axis_index("core") * half, half, 0)
     return lax.all_gather(own, ("fsdp", "core"), axis=0, tiled=True)
-
-
-def gather_small(value):
-    count = lax.axis_size("fsdp")
-    place = lax.axis_index("fsdp")
-    gathered = jnp.zeros((count,) + value.shape, value.dtype)
-    for shift in range(count):
-        pairs = [(source, (source + shift) % count) for source in range(count)]
-        member = lax.ppermute(value, "fsdp", pairs) if shift else value
-        gathered = lax.dynamic_update_index_in_dim(gathered, member, (place - shift) % count, 0)
-    return gathered
 
 
 def sum_low(value):
@@ -263,11 +396,19 @@
     fsdp_count = lax.axis_size("fsdp")
 
     small = jnp.concatenate([norm_gains[0], biases[0], mlp_bias.reshape(-1, shard)], 0)
+    small = small.reshape(-1, 3 * WIDTH)
     own_columns = lax.dynamic_index_in_dim(
         attn_in[0].reshape(shard, 3, GROUPS, WIDTH), group_id, 2, keepdims=False
     ).reshape(shard, 3 * WIDTH)
-    w_group = gather_small(own_columns).reshape(-1, 3 * WIDTH)
-    small_all = gather_small(small).astype(jnp.float32)
+    first_all = spread(
+        jnp.concatenate(
+            [own_columns, small, jnp.zeros((16 - small.shape[0], 3 * WIDTH), jnp.bfloat16)], 0
+        ),
+        "fsdp",
+    )
+    w_group = first_all[:, :shard].reshape(-1, 3 * WIDTH)
+    small_all = first_all[:, shard : shard + small.shape[0]].reshape(fsdp_count, -1, shard)
+    small_all = small_all.astype(jnp.float32)
     w_out = gather_weight(attn_out)
     w_up = gather_weight(mlp_in)
     w_down = gather_weight(mlp_out)
@@ -289,6 +430,7 @@
         [lax.dynamic_index_in_dim(inputs, plan[step], 0, keepdims=False) for step in range(micro_count)]
     ).reshape(rows, model_width)
     top_grad = cotangent.reshape(rows, model_width)
+    core_number = core_id.astype(jnp.int32)[None]
     head_shape = (micro_count, GROUPS, local_rows, WIDTH)
 
     def forward(entering):
@@ -357,27 +499,24 @@
         attn_parts = grad_attn.reshape(micro_count, local_rows, model_width)
         grad_mixed = cross(attn_parts, w_out_groups, "mte,gde->mgtd").astype(jnp.bfloat16)
         share = None
+        grad_heads = exchange(grad_mixed.reshape(-1, local_rows, WIDTH), CTX).reshape(-1, WIDTH)
         if last:
-            members = 2 * fsdp_count
-            d_down = cross(active_low, grad_low, "tf,td->fd").astype(jnp.bfloat16)
-            d_up = cross(normed_two_low, grad_hidden, "td,tf->df").astype(jnp.bfloat16)
-            d_out = cross(mixed, attn_parts, "mgtd,mte->gde").astype(jnp.bfloat16)
-            d_up = d_up.reshape(members, shard // 2, -1, model_width).transpose(0, 2, 1, 3)
-            parts = [
-                d_down.reshape(members, -1, model_width),
-                d_up.reshape(members, -1, model_width),
-                d_out.reshape(members, -1, model_width),
-            ]
-            parts.append(jnp.zeros((members, EXTRA, model_width), jnp.bfloat16))
-            joint = jnp.concatenate(parts, 1)
-            grad_mixed, joint = lax.optimization_barrier((grad_mixed, joint))
+            joint = weight_grads(
+                active_low,
+                grad_low,
+                normed_two_low.T,
+                grad_hidden,
+                mixed.transpose(1, 3, 0, 2).reshape(model_width, rows),
+                grad_attn,
+                2 * fsdp_count,
+            )
+            grad_heads, joint = lax.optimization_barrier((grad_heads, joint))
             share = lax.psum_scatter(
                 joint.reshape(-1, model_width),
                 ("fsdp", "core"),
                 scatter_dimension=0,
                 tiled=True,
             )
-        grad_heads = exchange(grad_mixed.reshape(-1, local_rows, WIDTH), CTX).reshape(-1, WIDTH)
         grad_joined, grad_own, grad_other = attend_back(
             joined, grad_heads, log_total, w_group, row_places, column_places
         )
@@ -387,22 +526,14 @@
         returned = returned.reshape(micro_count, 2, 2, local_rows, half).astype(jnp.float32)
         grad_normed = (returned[:, 0] + returned[:, 1]).transpose(0, 2, 1, 3)
         grad_normed = grad_normed.reshape(rows, model_width)
-        if last:
-            grad_normed, share = lax.optimization_barrier((grad_normed, share))
         grad_norm_one, d_gain_one, d_shift_one = normalize_back(
             grad_normed, unit_one, spread_one, gain_rows[0]
         )
         grad_in = (grad_middle + grad_norm_one).astype(jnp.bfloat16)
         if not last:
             return grad_in
-        d_qkv = jnp.concatenate(
-            in_order(
-                cross(own, grad_joined, "td,te->de").astype(jnp.bfloat16),
-                cross(other, grad_joined, "td,te->de").astype(jnp.bfloat16),
-            ),
-            0,
-        )
-        joined_sums = jnp.sum(grad_joined.astype(jnp.float32), 0)
+        pieces, joined_sums = qkv_grads(core_number, own, other, grad_joined, 4 * fsdp_count)
+        joined_sums = joined_sums[0]
         vectors = jnp.stack(
             [
                 d_gain_one,
@@ -414,7 +545,7 @@
             ]
         )
         d_up_bias = jnp.sum(grad_hidden.astype(jnp.float32), 0)
-        return grad_in, share, d_qkv, joined_sums, vectors, d_up_bias
+        return grad_in, share, pieces, joined_sums, vectors, d_up_bias
 
     forward_pairs = [(i, i + 1) for i in range(sections - 1)]
     entering = fresh
@@ -430,21 +561,7 @@
         result = backward(grad_low, saved, False)
         received = lax.ppermute(result, "section", back_pairs)
         grad_low = jnp.where(section_id == sections - 1, top_grad, received)
-    input_grad, share, d_qkv, joined_sums, vectors, d_up_bias = backward(grad_low, saved, True)
-
-    pieces = 4 * fsdp_count
-    qkv_piece = sum_low(exchange(d_qkv.reshape(pieces, -1, 3 * WIDTH), ("fsdp", "x")))
-    qkv_all = spread(qkv_piece, CTX).reshape(4, GROUPS, -1, 3, WIDTH).transpose(0, 2, 3, 1, 4)
-    g_qkv = qkv_all.reshape(1, shard, -1).astype(jnp.float32)
-
-    joint_piece = sum_low(exchange(share.reshape(8, -1, model_width), ("x", "yh")))
-    joint_all = spread(joint_piece, ("x", "yh")).reshape(-1, model_width)
-    both = jnp.stack(in_order(joint_all, swap(joint_all))).astype(jnp.float32)
-    down_rows = mlp_out.shape[1] // 2
-    g_down = both[:, :down_rows].reshape(1, -1, model_width)
-    g_up = both[:, down_rows : 2 * down_rows].reshape(2, -1, shard // 2, model_width)
-    g_up = g_up.transpose(0, 2, 1, 3).reshape(1, shard, -1)
-    g_out = both[:, 2 * down_rows : 2 * down_rows + shard // 2].reshape(1, shard, model_width)
+    input_grad, share, pieces, joined_sums, vectors, d_up_bias = backward(grad_low, saved, True)
 
     ours = jnp.arange(fsdp_count)[:, None] == group_id
     vector_parts = jnp.concatenate(
@@ -456,8 +573,16 @@
         ],
         1,
     )
-    vector_sum = jnp.sum(exchange(vector_parts, "fsdp"), 0)
-    vector_sum = jnp.sum(spread(vector_sum, CTX), 0)
+    vector_parts = vector_parts.astype(jnp.bfloat16).reshape(4 * fsdp_count, 3 * WIDTH)
+    pieces = pieces.at[:, pieces.shape[1] - 16, :].set(vector_parts)
+    qkv_piece = sum_low(exchange(pieces, ("fsdp", "x")))
+    qkv_piece = jnp.pad(qkv_piece, ((0, 0), (0, model_width - 3 * WIDTH)))
+    joint_piece = sum_low(exchange(share.reshape(8, -1, model_width), ("x", "yh")))
+    both = spread(jnp.concatenate([joint_piece, qkv_piece], 0), ("x", "yh"))
+    g_qkv, g_out, g_up, g_down, vector_sum = unpack(
+        core_number, both, swap(both), shard, mlp_in.shape[2], mlp_out.shape[1]
+    )
+    vector_sum = vector_sum[:, : 3 * WIDTH].reshape(-1)
     own_vectors = vector_sum[: 8 * shard].reshape(8, shard)
     own_up_bias = vector_sum[8 * shard :]
     order = (2, 6, 7, 3, 4, 5)
@@ -466,10 +591,10 @@
     return (
         layer_out.reshape(out_shape),
         input_grad.reshape(out_shape),
-        g_qkv,
-        g_out,
-        g_up,
-        g_down,
+        g_qkv[None],
+        g_out[None],
+        g_up[None],
+        g_down[None],
         own_vectors[None, :2],
         g_biases[None],
         own_up_bias[None],

time: 534 us -> 474 us (0.89)
  the two profiles are of different devices: /device:TPU:1 before, /device:TPU:33 now
where the time goes in v4:
time: 474 us; the launch traced here: 465 us
  blocking collectives  123 us (26%)
  waiting for transfers between devices  121 us (26%)
  Pallas kernels  65.7 us (14%)
  starting transfers between devices  45.8 us (10%)
  matrix products  40.1 us (8%)
  local copies, waits for them, and re-layouts  27.9 us (6%)
  between operations  22.7 us (5%)
  other arithmetic  18.7 us (4%)
    all_to_all x6, blocking collectives, exchange(): return lax.all_to_all(value, axes, 0, 0, tiled=True)  123 us
    all_to_all x6, waiting for transfers between devices, exchange(): return lax.all_to_all(value, axes, 0, 0, tiled=True)  65.4 us
    dot_general x10, matrix products, cross(): jnp.einsum(pattern, left_side, right_side, preferred_element_type=jnp.flo...  40.1 us
    all_to_all x6, starting transfers between devices, exchange(): return lax.all_to_all(value, axes, 0, 0, tiled=True)  36 us
    pallas_call x2, Pallas kernels, attend_back(): pl.pallas_call(attend_back_body, grid=(count // QUERY_BLOCK,), in_specs=[...  30 us
    pallas_call x2, Pallas kernels, attend(): pl.pallas_call(attend_body, grid=(count // QUERY_BLOCK,), in_specs=[pl.Bl...  21.6 us
    all_gather x3, waiting for transfers between devices, gather_weight(): return lax.all_gather(own, ('fsdp', 'core'), axis=0, tiled=True)  18.6 us
    reduce_scatter x1, waiting for transfers between devices, backward(): lax.psum_scatter(joint.reshape(-1, model_width), ('fsdp', 'core'), scatte...  12.2 us
  transfers between devices with their start and end apart: 17, of which 12 were waited for; matrix products, arithmetic and copies ran while one was open for 7% of the time, Pallas kernels for 8%

profile of v4, /device:TPU:33, one launch (start us, length us, event | category | flops | bytes accessed | tf_op | source)
XLA Modules:
  0.0 465.4 jit_solution(4393280486276193052)
XLA Ops:
  7.3 1.7 constant_dynamic-slice_fusion.3
  10.0 1.9 constant_dynamic-slice_fusion.1
  16.5 4.9 %all-to-all-start = ((bf16[4,208,576]{2,1,0:T(8,128)(2,1)}), bf16[4,208,576]{2,1,0:T(8,128)(2,1)S(1)}, u32[]{:S(2)}, u32[]{:S(2)}) async-start(bf16[4,208,576]{2,1,0:T(8,128)(2,1)} %broadcast_in_dim.112), calls=%async_computation | async-start | bytes 2129920 | tf_op jit(solution)/shard_map/all_to_all | solution.py:350
  30.6 9.1 %all-to-all-done = bf16[4,208,576]{2,1,0:T(8,128)(2,1)S(1)} async-done(((bf16[4,208,576]{2,1,0:T(8,128)(2,1)}), bf16[4,208,576]{2,1,0:T(8,128)(2,1)S(1)}, u32[]{:S(2)}, u32[]{:S(2)}) %all-to-all-start) | async-done | bytes 958496 | tf_op jit(solution)/shard_map/all_to_all | solution.py:350
  41.8 8.4 %all-to-all-start.1 = ((bf16[16,64,384]{2,1,0:T(8,128)(2,1)}), bf16[16,64,384]{2,1,0:T(8,128)(2,1)S(1)}, u32[]{:S(2)}, u32[]{:S(2)}) async-start(bf16[16,64,384]{2,1,0:T(8,128)(2,1)} %bitcast.11), calls=%async_computation.1 | async-start | bytes 1572864 | tf_op jit(solution)/shard_map/all_to_all | solution.py:350
  50.2 14.1 %all-to-all-done.1 = bf16[16,64,384]{2,1,0:T(8,128)(2,1)S(1)} async-done(((bf16[16,64,384]{2,1,0:T(8,128)(2,1)}), bf16[16,64,384]{2,1,0:T(8,128)(2,1)S(1)}, u32[]{:S(2)}, u32[]{:S(2)}) %all-to-all-start.1) | async-done | bytes 786464 | tf_op jit(solution)/shard_map/all_to_all | solution.py:350
  67.8 11.2 %shard_map.178 = (bf16[1024,576]{1,0:T(8,128)(2,1)}, bf16[1024,192]{1,0:T(8,128)(2,1)}, f32[8,1024]{1,0:T(8,128)}) custom-call(s32[1,1024]{1,0:T(1,128)S(1)} %add.258.row_places, s32[1024,1]{1,0:T(8,128)S(1)} %add.308.column_places, bf16[1024,384]{1,0:T(8,128)(2,1)S(1)} %bitcast.220, bf16[1024,384]{1,0:T(8,128)(2,1)S(1)} %collective-permute-done.other, ...), custom_call_target="tpu_custom_call" | custom-call | flops 805306368 | bytes 1572864 | tf_op jit(solution)/shard_map/pallas_call | solution.py:70
  78.9 3.7 all-to-all-start.2
  83.0 10.7 %all-to-all-done.2 = bf16[16,64,192]{2,1,0:T(8,128)(2,1)S(1)} async-done(((bf16[16,64,192]{2,1,0:T(8,128)(2,1)}), bf16[16,64,192]{2,1,0:T(8,128)(2,1)S(1)}, u32[]{:S(2)}, u32[]{:S(2)}) %all-to-all-start.2) | async-done | bytes 393248 | tf_op jit(solution)/shard_map/all_to_all | solution.py:350
  93.8 2.0 fusion.133
  96.1 18.6 %all-gather.11.cloned.1.call-done = bf16[1,3072,768]{2,1,0:T(8,128)(2,1)} async-done(((bf16[1,384,768]{2,1,0:T(8,128)(2,1)}), bf16[1,3072,768]{2,1,0:T(8,128)(2,1)}) %all-gather.11.cloned.1.call-update) | async-done | bytes 4718608 | tf_op jit(solution)/shard_map/all_gather | solution.py:365
  114.7 6.8 %fusion.67 = bf16[256,768]{1,0:T(8,128)(2,1)S(1)} fusion(f32[256,768]{1,0:T(8,128)S(1)} %get-tuple-element.138, bf16[1,3072,768]{2,1,0:T(8,128)(2,1)} %all-gather.11.cloned.1.call-done, bf16[1,768,3072]{2,1,0:T(8,128)(2,1)} %all-gather.9.cloned.1.call-done, f32[3072]{0:T(1024)S(1)} %add.275, f32[768]{0:T(1024)S(1)} %add.281, f32[768]{0:T(1024)S(1)} %add.272, ...), kind=kOutput, calls=%fused_computation.55 | convolution fusion | flops 2425356288 | bytes 10640384 | tf_op jit(solution)/shard_map/tf,fd->td/dot_general | solution.py:324
  121.5 3.1 collective-permute-start.1
  124.8 8.0 %collective-permute-done.1 = bf16[256,768]{1,0:T(8,128)(2,1)S(1)} collective-permute-done((bf16[256,768]{1,0:T(8,128)(2,1)S(1)}, bf16[256,768]{1,0:T(8,128)(2,1)S(1)}, u32[]{:S(2)}, u32[]{:S(2)}) %collective-permute-start.1) | collective-permute-done | bytes 393248 | tf_op jit(solution)/shard_map/ppermute | solution.py:554
  133.9 22.1 %all_to_all.60 = bf16[16,64,384]{2,1,0:T(8,128)(2,1)S(1)} all-to-all(bf16[16,64,384]{2,1,0:T(8,128)(2,1)S(1)} %bitcast.231), channel_id=1, replica_groups=mesh['section'=2,'x'=4,'yh'=2,'core'=2,'fsdp'=4] {'x','yh','core'}, dimensions={0} | all-to-all | bytes 1572864 | tf_op jit(solution)/shard_map/all_to_all | solution.py:350
  156.4 1.9 collective-permute-done.2.other
  158.3 10.4 %shard_map.179 = (bf16[1024,576]{1,0:T(8,128)(2,1)S(1)}, bf16[1024,192]{1,0:T(8,128)(2,1)S(1)}, f32[8,1024]{1,0:T(8,128)S(1)}) custom-call(s32[1,1024]{1,0:T(1,128)S(1)} %add.258.row_places, s32[1024,1]{1,0:T(8,128)S(1)} %add.308.column_places, bf16[1024,384]{1,0:T(8,128)(2,1)S(1)} %bitcast.217, bf16[1024,384]{1,0:T(8,128)(2,1)S(1)} %collective-permute-done.2.other, ...), custom_call_target="tpu_custom_call" | custom-call | flops 805306368 | bytes 1572864 | tf_op jit(solution)/shard_map/pallas_call | solution.py:70
  168.7 14.4 %all_to_all.61 = bf16[16,64,192]{2,1,0:T(8,128)(2,1)S(1)} all-to-all(bf16[16,64,192]{2,1,0:T(8,128)(2,1)S(1)} %bitcast.222), channel_id=1, replica_groups=mesh['section'=2,'x'=4,'yh'=2,'core'=2,'fsdp'=4] {'x','yh','core'}, dimensions={0} | all-to-all | bytes 786432 | tf_op jit(solution)/shard_map/all_to_all | solution.py:350
  184.1 3.9 multiply_convert_fusion
  188.0 10.0 %fusion.124 = (f32[256]{0:T(256)S(1)}, f32[256]{0:T(256)S(1)}, f32[256,768]{1,0:T(8,128)}) fusion(f32[256]{0:T(256)S(1)} %add_rsqrt_fusion.1, f32[256,768]{1,0:T(8,128)} %copy-done.20, f32[256]{0:T(256)S(1)} %broadcast_multiply_fusion.9, f32[768]{0:T(1024)S(1)} %mul.319, bf16[1,768,3072]{2,1,0:T(8,128)(2,1)} %all-gather.9.cloned.1.call-done, ...), kind=kOutput, calls=%fused_computation.178 | convolution fusion | flops 2432826880 | bytes 14556160 | tf_op jit(solution)/shard_map/tf,df->td/dot_general | solution.py:324
  197.9 2.7 fusion.129
  201.3 15.0 %all_to_all.62 = bf16[16,64,192]{2,1,0:T(8,128)(2,1)S(1)} all-to-all(bf16[16,64,192]{2,1,0:T(8,128)(2,1)S(1)} %bitcast.238), channel_id=1, replica_groups=mesh['section'=2,'x'=4,'yh'=2,'core'=2,'fsdp'=4] {'x','yh','core'}, dimensions={0} | all-to-all | bytes 786432 | tf_op jit(solution)/shard_map/all_to_all | solution.py:350
  216.3 15.5 %shard_map.180 = (bf16[1024,576]{1,0:T(8,128)(2,1)}, bf16[1024,384]{1,0:T(8,128)(2,1)S(1)}, bf16[1024,384]{1,0:T(8,128)(2,1)S(1)}) custom-call(s32[1,1024]{1,0:T(1,128)S(1)} %add.258.row_places, s32[1024,1]{1,0:T(8,128)S(1)} %copy-done.11, bf16[1024,576]{1,0:T(8,128)(2,1)} %copy-done.17, bf16[1024,192]{1,0:T(8,128)(2,1)S(1)} %bitcast.221, ...), custom_call_target="tpu_custom_call" | custom-call | flops 2013265920 | bytes 3145728 | tf_op jit(solution)/shard_map/pallas_call | solution.py:150
  231.7 1.4 collective-permute-start.3
  233.1 1.9 collective-permute-done.3
  235.2 17.5 %all_to_all.63 = bf16[16,64,384]{2,1,0:T(8,128)(2,1)S(1)} all-to-all(bf16[16,64,384]{2,1,0:T(8,128)(2,1)S(1)} %bitcast.235), channel_id=1, replica_groups=mesh['section'=2,'x'=4,'yh'=2,'core'=2,'fsdp'=4] {'x','yh','core'}, dimensions={0} | all-to-all | bytes 1572864 | tf_op jit(solution)/shard_map/all_to_all | solution.py:350
  256.7 11.1 %collective-permute-done.4 = bf16[256,768]{1,0:T(8,128)(2,1)S(1)} collective-permute-done((bf16[256,768]{1,0:T(8,128)(2,1)}, bf16[256,768]{1,0:T(8,128)(2,1)S(1)}, u32[]{:S(2)}, u32[]{:S(2)}) %collective-permute-start.4) | collective-permute-done | bytes 393248 | tf_op jit(solution)/shard_map/ppermute | solution.py:562
  267.9 6.8 %fusion.137 = (bf16[3072]{0:T(1024)(128)(2,1)S(1)}, bf16[256,3072]{1,0:T(8,128)(2,1)S(1)}) fusion(f32[256,3072]{1,0:T(8,128)} %get-tuple-element.143, bf16[256,768]{1,0:T(8,128)(2,1)S(1)} %get-tuple-element.101.grad_low, bf16[1,3072,768]{2,1,0:T(8,128)(2,1)} %all-gather.11.cloned.1.call-done), kind=kOutput, calls=%fused_computation.187 | convolution fusion | flops 1224471552 | bytes 9836544 | tf_op jit(solution)/shard_map/td,fd->tf/dot_general | solution.py:324
  274.8 4.3 fusion.8
  283.0 5.2 %all-to-all-start.7 = ((bf16[16,64,192]{2,1,0:T(8,128)(2,1)}), bf16[16,64,192]{2,1,0:T(8,128)(2,1)}, u32[]{:S(2)}, u32[]{:S(2)}) async-start(bf16[16,64,192]{2,1,0:T(8,128)(2,1)} %bitcast.237), calls=%async_computation.7 | async-start | bytes 1048576 | tf_op jit(solution)/shard_map/all_to_all | solution.py:350
  289.6 1.9 reshape.583.mixed
  292.7 1.4 copy-done.5
  294.1 7.8 %shard_map.181 = bf16[8,896,768]{2,1,0:T(8,128)(2,1)} custom-call(bf16[256,3072]{1,0:T(8,128)(2,1)S(1)} %get-tuple-element.142.active, bf16[256,768]{1,0:T(8,128)(2,1)S(1)} %get-tuple-element.101.grad_low, bf16[768,256]{1,0:T(8,128)(2,1)S(1)} %copy.69.normed_two, bf16[256,3072]{1,0:T(8,128)(2,1)S(1)} %copy-done.5, bf16[768,256]{1,0:T(8,128)(2,1)S(1)} %reshape.583.mixed, ...), custom_call_target="tpu_custom_call" | custom-call | flops 2717908992 | bytes 11010048 | tf_op jit(solution)/shard_map/pallas_call | solution.py:203
  303.2 14.6 %shard_map.182 = (bf16[1024,576]{1,0:T(8,128)(2,1)S(1)}, bf16[1024,384]{1,0:T(8,128)(2,1)S(1)}, bf16[1024,384]{1,0:T(8,128)(2,1)S(1)}) custom-call(s32[1,1024]{1,0:T(1,128)S(1)} %add.258.row_places, s32[1024,1]{1,0:T(8,128)S(1)} %copy-done.12, bf16[1024,576]{1,0:T(8,128)(2,1)} %copy-done.17, bf16[1024,192]{1,0:T(8,128)(2,1)} %bitcast.57.grad_mixed, ...), custom_call_target="tpu_custom_call" | custom-call | flops 2013265920 | bytes 3145728 | tf_op jit(solution)/shard_map/pallas_call | solution.py:150
  318.1 2.0 collective-permute-done.5
  321.2 7.4 %all-to-all-start.8 = ((bf16[16,64,384]{2,1,0:T(8,128)(2,1)}), bf16[16,64,384]{2,1,0:T(8,128)(2,1)}, u32[]{:S(2)}, u32[]{:S(2)}) async-start(bf16[16,64,384]{2,1,0:T(8,128)(2,1)} %bitcast.234), calls=%async_computation.8 | async-start | bytes 1572864 | tf_op jit(solution)/shard_map/all_to_all | solution.py:350
  330.3 1.4 shard_map.183
  331.8 11.1 %all-to-all-done.8 = bf16[16,64,384]{2,1,0:T(8,128)(2,1)} async-done(((bf16[16,64,384]{2,1,0:T(8,128)(2,1)}), bf16[16,64,384]{2,1,0:T(8,128)(2,1)}, u32[]{:S(2)}, u32[]{:S(2)}) %all-to-all-start.8) | async-done | bytes 786464 | tf_op jit(solution)/shard_map/all_to_all | solution.py:350
  347.1 21.8 %all_to_all.64 = bf16[16,64,576]{2,1,0:T(8,128)(2,1)} all-to-all(bf16[16,64,576]{2,1,0:T(8,128)(2,1)S(1)} %scatter.4), channel_id=1, replica_groups=mesh['section'=2,'x'=4,'yh'=2,'core'=2,'fsdp'=4] {'fsdp','x'}, dimensions={0} | all-to-all | bytes 2359296 | tf_op jit(solution)/shard_map/all_to_all | solution.py:350
  368.9 12.2 %reduce-scatter.2.cloned.1.call-done = bf16[896,768]{1,0:T(8,128)(2,1)} async-done(((bf16[7168,768]{1,0:T(8,128)(2,1)}), bf16[896,768]{1,0:T(8,128)(2,1)}) %reduce-scatter.2.cloned.1.call-update) | async-done | bytes 1376272 | tf_op jit(solution)/shard_map/reduce_scatter | solution.py:514
  381.0 6.4 %all-to-all-start.9 = ((bf16[8,112,768]{2,1,0:T(8,128)(2,1)}), bf16[8,112,768]{2,1,0:T(8,128)(2,1)S(1)}, u32[]{:S(2)}, u32[]{:S(2)}) async-start(bf16[8,112,768]{2,1,0:T(8,128)(2,1)} %bitcast.243), calls=%async_computation.10 | async-start | bytes 2752512 | tf_op jit(solution)/shard_map/all_to_all | solution.py:350
  387.5 1.5 reduce_sum.255
  389.0 20.4 %all-to-all-done.9 = bf16[8,112,768]{2,1,0:T(8,128)(2,1)S(1)} async-done(((bf16[8,112,768]{2,1,0:T(8,128)(2,1)}), bf16[8,112,768]{2,1,0:T(8,128)(2,1)S(1)}, u32[]{:S(2)}, u32[]{:S(2)}) %all-to-all-start.9) | async-done | bytes 1376288 | tf_op jit(solution)/shard_map/all_to_all | solution.py:350
  409.8 32.7 %all_to_all.65.own = bf16[8,176,768]{2,1,0:T(8,128)(2,1)S(1)} all-to-all(bf16[8,176,768]{2,1,0:T(8,128)(2,1)S(1)} %broadcast_in_dim.126), channel_id=1, replica_groups=mesh['section'=2,'x'=4,'yh'=2,'core'=2,'fsdp'=4] {'x','yh'}, dimensions={0} | all-to-all | bytes 4325376 | tf_op jit(solution)/shard_map/all_to_all | solution.py:350
  442.5 2.0 collective-permute-start.6
  444.5 4.5 fusion.64
  449.1 2.6 fusion.95
  451.7 4.9 %shard_map.184 = (f32[192,2304]{1,0:T(8,128)}, f32[192,768]{1,0:T(8,128)}, f32[192,3072]{1,0:T(8,128)}, f32[768,768]{1,0:T(8,128)}, f32[4,768]{1,0:T(4,128)S(1)}) custom-call(s32[1]{0:T(128)} %bitcast.68.core_id, bf16[8,176,768]{2,1,0:T(8,128)(2,1)S(1)} %all_to_all.65.own, bf16[8,176,768]{2,1,0:T(8,128)(2,1)} %collective-permute-done.6.other), custom_call_target="tpu_custom_call" | custom-call | bytes 12582912 | tf_op jit(solution)/shard_map/pallas_call | solution.py:306
  (236 shorter events, 38.0 us)
Async XLA Ops:
  7.2 4.8 %copy-start.37 = (bf16[1,768]{1,0:T(2,128)(2,1)S(1)}, bf16[1,768]{1,0:T(2,128)(2,1)}, u32[]{:S(2)}) copy-start(bf16[1,768]{1,0:T(2,128)(2,1)} %param.23) | copy-start | bytes 4612
  7.2 4.9 %copy-start.36 = (bf16[1,6,192]{2,1,0:T(8,128)(2,1)S(1)}, bf16[1,6,192]{2,1,0:T(8,128)(2,1)}, u32[]{:S(2)}) copy-start(bf16[1,6,192]{2,1,0:T(8,128)(2,1)} %param.22) | copy-start | bytes 6916
  7.2 4.9 %copy-start.38 = (bf16[1,2,192]{2,1,0:T(2,128)(2,1)S(1)}, bf16[1,2,192]{2,1,0:T(2,128)(2,1)}, u32[]{:S(2)}) copy-start(bf16[1,2,192]{2,1,0:T(2,128)(2,1)} %param.21) | copy-start | bytes 2308
  7.2 5.2 %copy-start.31 = (bf16[1,192,2304]{2,1,0:T(8,128)(2,1)S(1)}, bf16[1,192,2304]{2,1,0:T(8,128)(2,1)}, u32[]{:S(2)}) copy-start(bf16[1,192,2304]{2,1,0:T(8,128)(2,1)} %param.17) | copy-start | bytes 2654212
  7.2 86.5 %all-gather.7.cloned.1.call-start = ((), (), s32[]{:S(2)}) async-start(), calls=%async_computation.14 | async-start | bytes 1327104 | tf_op jit(solution)/shard_map/all_gather | solution.py:365
  9.0 87.0 %all-gather.9.cloned.1.call-start = ((), (), s32[]{:S(2)}) async-start(), calls=%async_computation.15 | async-start | bytes 5308416 | tf_op jit(solution)/shard_map/all_gather | solution.py:365
  10.0 104.7 %all-gather.11.cloned.1.call-start = ((), (), s32[]{:S(2)}) async-start(), calls=%async_computation.16 | async-start | bytes 5308416 | tf_op jit(solution)/shard_map/all_gather | solution.py:365
  13.5 7.8 %copy-start.33 = (s32[4]{0:T(128)S(1)}, s32[4]{0:T(128)}, u32[]{:S(2)}) copy-start(s32[4]{0:T(128)} %param.15) | copy-start | bytes 52
  13.5 16.2 %copy-start.32 = (bf16[4,1,64,768]{3,2,1,0:T(8,128)(2,1)S(1)}, bf16[4,1,64,768]{3,2,1,0:T(8,128)(2,1)}, u32[]{:S(2)}) copy-start(bf16[4,1,64,768]{3,2,1,0:T(8,128)(2,1)} %param.13) | copy-start | bytes 1179652
  16.5 23.2 %all-to-all-start = ((bf16[4,208,576]{2,1,0:T(8,128)(2,1)}), bf16[4,208,576]{2,1,0:T(8,128)(2,1)S(1)}, u32[]{:S(2)}, u32[]{:S(2)}) async-start(bf16[4,208,576]{2,1,0:T(8,128)(2,1)} %broadcast_in_dim.112), calls=%async_computation | async-start | bytes 2129920 | tf_op jit(solution)/shard_map/all_to_all | solution.py:350
  29.9 12.0 %copy-start.24 = (bf16[4,1,64,768]{3,2,1,0:T(8,128)(2,1)}, bf16[4,1,64,768]{3,2,1,0:T(8,128)(2,1)S(1)}, u32[]{:S(2)}) copy-start(bf16[4,1,64,768]{3,2,1,0:T(8,128)(2,1)S(1)} %get-tuple-element.113) | copy-start | bytes 1179652
  29.9 20.3 %copy-start.42 = (s32[32]{0:T(128)S(1)}, s32[32]{0:T(128)}, u32[]{:S(2)}) copy-start(s32[32]{0:T(128)} %param.16) | copy-start | bytes 388
  41.8 22.5 %all-to-all-start.1 = ((bf16[16,64,384]{2,1,0:T(8,128)(2,1)}), bf16[16,64,384]{2,1,0:T(8,128)(2,1)S(1)}, u32[]{:S(2)}, u32[]{:S(2)}) async-start(bf16[16,64,384]{2,1,0:T(8,128)(2,1)} %bitcast.11), calls=%async_computation.1 | async-start | bytes 1572864 | tf_op jit(solution)/shard_map/all_to_all | solution.py:350
  64.4 3.4 collective-permute-start
  66.2 92.1 %copy-start.10 = (s32[1024,1]{1,0:T(8,128)}, s32[1024,1]{1,0:T(8,128)S(1)}, u32[]{:S(2)}) copy-start(s32[1024,1]{1,0:T(8,128)S(1)} %add.308.column_places) | copy-start | bytes 12292
  67.8 148.5 %copy-start.6 = (bf16[768,576]{1,0:T(8,128)(2,1)}, bf16[768,576]{1,0:T(8,128)(2,1)S(1)}, u32[]{:S(2)}) copy-start(bf16[768,576]{1,0:T(8,128)(2,1)S(1)} %pad_maximum_fusion.weight) | copy-start | bytes 2654212
  78.9 14.8 %all-to-all-start.2 = ((bf16[16,64,192]{2,1,0:T(8,128)(2,1)}), bf16[16,64,192]{2,1,0:T(8,128)(2,1)S(1)}, u32[]{:S(2)}, u32[]{:S(2)}) async-start(bf16[16,64,192]{2,1,0:T(8,128)(2,1)} %bitcast.17), calls=%async_computation.2 | async-start | bytes 1048576 | tf_op jit(solution)/shard_map/all_to_all | solution.py:350
  83.0 38.6 %copy-start.34 = (f32[768]{0:T(1024)}, f32[768]{0:T(1024)S(1)}, u32[]{:S(2)}) copy-start(f32[768]{0:T(1024)S(1)} %add.281) | copy-start | bytes 9220
  96.0 36.8 %copy-start.25 = (bf16[4,1,64,768]{3,2,1,0:T(8,128)(2,1)S(1)}, bf16[4,1,64,768]{3,2,1,0:T(8,128)(2,1)}, u32[]{:S(2)}) copy-start(bf16[4,1,64,768]{3,2,1,0:T(8,128)(2,1)} %copy-done.24) | copy-start | bytes 1179652
  121.5 11.3 %collective-permute-start.1 = (bf16[256,768]{1,0:T(8,128)(2,1)S(1)}, bf16[256,768]{1,0:T(8,128)(2,1)S(1)}, u32[]{:S(2)}, u32[]{:S(2)}) collective-permute-start(bf16[256,768]{1,0:T(8,128)(2,1)S(1)} %fusion.67), channel_id=1, source_target_pairs={{0,64},{1,65},{2,66},{3,67},{4,68},{5,69},{6,70},{7,71},{8,72},{9,... | collective-permute-start | bytes 1179656 | tf_op jit(solution)/shard_map/ppermute | solution.py:554
  133.1 121.1 %copy-start.18 = (bf16[256,768]{1,0:T(8,128)(2,1)}, bf16[256,768]{1,0:T(8,128)(2,1)S(1)}, u32[]{:S(2)}) copy-start(bf16[256,768]{1,0:T(8,128)(2,1)S(1)} %get-tuple-element.111) | copy-start | bytes 1179652
  133.9 50.2 %slice-start = ((s8[4718592]{0:T(1024)(128)(4,1)}), s8[4194304]{0:T(1024)(128)(4,1)S(1)}, s32[]{:S(2)}) async-start(s8[4718592]{0:T(1024)(128)(4,1)} %bitcast.262), calls=%async_computation.17 | async-start | bytes 8388608
  156.0 27.2 %copy-start.8 = (bf16[16,64,384]{2,1,0:T(8,128)(2,1)}, bf16[16,64,384]{2,1,0:T(8,128)(2,1)S(1)}, u32[]{:S(2)}) copy-start(bf16[16,64,384]{2,1,0:T(8,128)(2,1)S(1)} %all_to_all.60) | copy-start | bytes 2359300
  156.0 27.2 %copy-start.39 = (bf16[1,768,768]{2,1,0:T(8,128)(2,1)S(1)}, bf16[1,768,768]{2,1,0:T(8,128)(2,1)}, u32[]{:S(2)}) copy-start(bf16[1,768,768]{2,1,0:T(8,128)(2,1)} %all-gather.7.cloned.1.call-done) | copy-start | bytes 3538948
  156.0 28.1 %slice-start.1 = ((s8[4718592]{0:T(1024)(128)(4,1)}), s8[524288]{0:T(1024)(128)(4,1)S(1)}, s32[]{:S(2)}) async-start(s8[4718592]{0:T(1024)(128)(4,1)} %bitcast.262), calls=%async_computation.18 | async-start | bytes 1048576
  156.0 2.3 collective-permute-start.2
  158.3 24.9 %copy-start.13 = (bf16[1024,384]{1,0:T(8,128)(2,1)}, bf16[1024,384]{1,0:T(8,128)(2,1)S(1)}, u32[]{:S(2)}) copy-start(bf16[1024,384]{1,0:T(8,128)(2,1)S(1)} %collective-permute-done.2.other) | copy-start | bytes 2359300
  168.7 19.2 %copy-start.17 = (bf16[1024,576]{1,0:T(8,128)(2,1)}, bf16[1024,576]{1,0:T(8,128)(2,1)S(1)}, u32[]{:S(2)}) copy-start(bf16[1024,576]{1,0:T(8,128)(2,1)S(1)} %get-tuple-element.41.joined) | copy-start | bytes 3538948
  183.1 4.8 %copy-start.26 = (bf16[16,64,192]{2,1,0:T(8,128)(2,1)}, bf16[16,64,192]{2,1,0:T(8,128)(2,1)S(1)}, u32[]{:S(2)}) copy-start(bf16[16,64,192]{2,1,0:T(8,128)(2,1)S(1)} %all_to_all.61) | copy-start | bytes 1179652
  188.0 104.7 %copy-start.2 = (bf16[256,3072]{1,0:T(8,128)(2,1)}, bf16[256,3072]{1,0:T(8,128)(2,1)S(1)}, u32[]{:S(2)}) copy-start(bf16[256,3072]{1,0:T(8,128)(2,1)S(1)} %get-tuple-element.142.active) | copy-start | bytes 4718596
  197.9 18.3 %copy-start.11 = (s32[1024,1]{1,0:T(8,128)S(1)}, s32[1024,1]{1,0:T(8,128)}, u32[]{:S(2)}) copy-start(s32[1024,1]{1,0:T(8,128)} %copy-done.10) | copy-start | bytes 12292
  231.7 3.3 collective-permute-start.3
  255.4 12.4 %collective-permute-start.4 = (bf16[256,768]{1,0:T(8,128)(2,1)}, bf16[256,768]{1,0:T(8,128)(2,1)S(1)}, u32[]{:S(2)}, u32[]{:S(2)}) collective-permute-start(bf16[256,768]{1,0:T(8,128)(2,1)} %fusion.90), channel_id=1, source_target_pairs={{64,0},{65,1},{66,2},{67,3},{68,4},{69,5},{70,6},{71,7},{72,8},{73... | collective-permute-start | bytes 1179656 | tf_op jit(solution)/shard_map/ppermute | solution.py:562
  274.7 4.4 copy-start.4
  280.3 8.0 %copy-start.27 = (bf16[16,64,192]{2,1,0:T(8,128)(2,1)S(1)}, bf16[16,64,192]{2,1,0:T(8,128)(2,1)}, u32[]{:S(2)}) copy-start(bf16[16,64,192]{2,1,0:T(8,128)(2,1)} %copy-done.26) | copy-start | bytes 1179652
  283.0 18.8 %all-to-all-start.7 = ((bf16[16,64,192]{2,1,0:T(8,128)(2,1)}), bf16[16,64,192]{2,1,0:T(8,128)(2,1)}, u32[]{:S(2)}, u32[]{:S(2)}) async-start(bf16[16,64,192]{2,1,0:T(8,128)(2,1)} %bitcast.237), calls=%async_computation.7 | async-start | bytes 1048576 | tf_op jit(solution)/shard_map/all_to_all | solution.py:350
  288.2 92.8 %reduce-scatter.2.cloned.1.call-start = ((), (), s32[]{:S(2)}) async-start(), calls=%async_computation.13 | async-start | bytes 12386304 | tf_op jit(solution)/shard_map/reduce_scatter | solution.py:514
  317.8 11.2 %copy-start.9 = (bf16[16,64,384]{2,1,0:T(8,128)(2,1)S(1)}, bf16[16,64,384]{2,1,0:T(8,128)(2,1)}, u32[]{:S(2)}) copy-start(bf16[16,64,384]{2,1,0:T(8,128)(2,1)} %copy-done.8) | copy-start | bytes 2359300
  317.8 11.2 %copy-start.14 = (bf16[1024,384]{1,0:T(8,128)(2,1)S(1)}, bf16[1024,384]{1,0:T(8,128)(2,1)}, u32[]{:S(2)}) copy-start(bf16[1024,384]{1,0:T(8,128)(2,1)} %copy-done.13) | copy-start | bytes 2359300
  317.8 2.4 collective-permute-start.5
  321.2 21.7 %all-to-all-start.8 = ((bf16[16,64,384]{2,1,0:T(8,128)(2,1)}), bf16[16,64,384]{2,1,0:T(8,128)(2,1)}, u32[]{:S(2)}, u32[]{:S(2)}) async-start(bf16[16,64,384]{2,1,0:T(8,128)(2,1)} %bitcast.234), calls=%async_computation.8 | async-start | bytes 1572864 | tf_op jit(solution)/shard_map/all_to_all | solution.py:350
  345.2 35.9 %copy-start.23 = (f32[32,8,2,384]{3,1,2,0:T(8,128)}, f32[32,8,2,384]{3,1,2,0:T(8,128)S(1)}, u32[]{:S(2)}) copy-start(f32[32,8,2,384]{3,1,2,0:T(8,128)S(1)} %copy.89) | copy-start | bytes 2359300
  381.0 28.4 %all-to-all-start.9 = ((bf16[8,112,768]{2,1,0:T(8,128)(2,1)}), bf16[8,112,768]{2,1,0:T(8,128)(2,1)S(1)}, u32[]{:S(2)}, u32[]{:S(2)}) async-start(bf16[8,112,768]{2,1,0:T(8,128)(2,1)} %bitcast.243), calls=%async_computation.10 | async-start | bytes 2752512 | tf_op jit(solution)/shard_map/all_to_all | solution.py:350
  409.6 34.9 %copy-start.3 = (bf16[256,3072]{1,0:T(8,128)(2,1)S(1)}, bf16[256,3072]{1,0:T(8,128)(2,1)}, u32[]{:S(2)}) copy-start(bf16[256,3072]{1,0:T(8,128)(2,1)} %copy-done.2) | copy-start | bytes 4718596
  409.6 34.8 %copy-start.22 = (f32[256,768]{1,0:T(8,128)S(1)}, f32[256,768]{1,0:T(8,128)}, u32[]{:S(2)}) copy-start(f32[256,768]{1,0:T(8,128)} %copy-done.20) | copy-start | bytes 2359300
  409.6 34.8 %copy-start.35 = (f32[768]{0:T(1024)S(1)}, f32[768]{0:T(1024)}, u32[]{:S(2)}) copy-start(f32[768]{0:T(1024)} %copy-done.34) | copy-start | bytes 9220
  442.5 9.3 %collective-permute-start.6 = (bf16[8,176,768]{2,1,0:T(8,128)(2,1)S(1)}, bf16[8,176,768]{2,1,0:T(8,128)(2,1)}, u32[]{:S(2)}, u32[]{:S(2)}) collective-permute-start(bf16[8,176,768]{2,1,0:T(8,128)(2,1)S(1)} %all_to_all.65.own), channel_id=1, source_target_pairs={{0,4},{4,0},{1,5},{5,1},{2,6},{6,2},{3,7},{7,3},{8,12},{12,8},{9,1... | collective-permute-start | bytes 6488072 | tf_op jit(solution)/shard_map/ppermute | solution.py:354
  449.1 9.5 %copy-start.1 = (bf16[1,192,3072]{2,1,0:T(8,128)(2,1)S(1)}, bf16[1,192,3072]{2,1,0:T(8,128)(2,1)}, u32[]{:S(2)}) copy-start(bf16[1,192,3072]{2,1,0:T(8,128)(2,1)} %param.19) | copy-start | bytes 3538948
  (14 other events, 32.5 us)
Sparse Core Ops, SparseCore 0:
  10.3 27.1 all-gather.6
  39.8 38.1 all-gather.8
  80.3 34.3 all-gather.10
  302.0 79.0 reduce-scatter.1

commit v5 on v4

--- a/solution.py
+++ b/solution.py
@@ -178,39 +178,57 @@
 
 
 def weight_grads_body(
-    active, grad_low, normed_two, grad_hidden, mixed, grad_attn, joint
+    active,
+    active_other,
+    grad_low,
+    grad_low_other,
+    normed_two,
+    normed_two_other,
+    grad_hidden,
+    grad_hidden_other,
+    mixed,
+    mixed_other,
+    grad_attn,
+    grad_attn_other,
+    joint,
 ):
     down_rows, up_rows = active.shape[1], normed_two.shape[0]
     width = grad_low.shape[1]
-    joint[0, :down_rows, :] = dot(active[...], grad_low[...], 0, 0).astype(jnp.bfloat16)
+    product = dot(active[...], grad_low[...], 0, 0)
+    product += dot(active_other[...], grad_low_other[...], 0, 0)
+    joint[0, :down_rows, :] = product.astype(jnp.bfloat16)
     place = down_rows
     for panel in range(grad_hidden.shape[1] // width):
-        product = dot(normed_two[...], grad_hidden[:, panel * width : (panel + 1) * width], 1, 0)
+        columns = slice(panel * width, (panel + 1) * width)
+        product = dot(normed_two[...], grad_hidden[:, columns], 1, 0)
+        product += dot(normed_two_other[...], grad_hidden_other[:, columns], 1, 0)
         joint[0, place : place + up_rows, :] = product.astype(jnp.bfloat16)
         place += up_rows
-    joint[0, place : place + up_rows, :] = dot(mixed[...], grad_attn[...], 1, 0).astype(
-        jnp.bfloat16
-    )
+    product = dot(mixed[...], grad_attn[...], 1, 0)
+    product += dot(mixed_other[...], grad_attn_other[...], 1, 0)
+    joint[0, place : place + up_rows, :] = product.astype(jnp.bfloat16)
     place += up_rows
     joint[0, place:, :] = jnp.zeros_like(joint[0, place:, :])
 
 
-def weight_grads(active, grad_low, normed_two, grad_hidden, mixed, grad_attn, members):
-    rows, hidden_width = active.shape
+def weight_grads(pairs, members):
+    (active, _), (grad_low, _), (normed_two, _), (grad_hidden, _) = pairs[:4]
+    rows, hidden_width = grad_hidden.shape
     width = grad_low.shape[1]
-    down_rows, up_rows = hidden_width // members, width // members
+    down_rows, up_rows = active.shape[1] // members, normed_two.shape[0] // members
     out_rows = 2 * down_rows + up_rows + EXTRA
+    specs = [
+        pl.BlockSpec((rows, down_rows), lambda i: (0, i)),
+        whole(rows, width),
+        pl.BlockSpec((up_rows, rows), lambda i: (i, 0)),
+        whole(rows, hidden_width),
+        pl.BlockSpec((up_rows, rows), lambda i: (i, 0)),
+        whole(rows, width),
+    ]
     return pl.pallas_call(
         weight_grads_body,
         grid=(members,),
-        in_specs=[
-            pl.BlockSpec((rows, down_rows), lambda i: (0, i)),
-            whole(rows, width),
-            pl.BlockSpec((up_rows, rows), lambda i: (i, 0)),
-            whole(rows, hidden_width),
-            pl.BlockSpec((up_rows, rows), lambda i: (i, 0)),
-            whole(rows, width),
-        ],
+        in_specs=[spec for spec in specs for _ in range(2)],
         out_specs=pl.BlockSpec((1, out_rows, width), lambda i: (i, 0, 0)),
         out_shape=jax.ShapeDtypeStruct((members, out_rows, width), jnp.bfloat16),
         compiler_params=pltpu.CompilerParams(vmem_limit_bytes=48 << 20),
@@ -219,7 +237,7 @@
             bytes_accessed=2 * members * out_rows * width,
             transcendentals=0,
         ),
-    )(active, grad_low, normed_two, grad_hidden, mixed, grad_attn)
+    )(*[value for pair in pairs for value in pair])
 
 
 def qkv_grads_body(core_id, own, other, grad_joined, pieces, sums):
@@ -359,10 +377,36 @@
     return jnp.where(first, own, other), jnp.where(first, other, own)
 
 
-def gather_weight(weight):
-    half = weight.shape[1] // 2
-    own = lax.dynamic_slice_in_dim(weight[0], lax.axis_index("core") * half, half, 0)
-    return lax.all_gather(own, ("fsdp", "core"), axis=0, tiled=True)
+def gather_weights(attn_out, mlp_in, mlp_out):
+    core_id = lax.axis_index("core")
+    width = attn_out.shape[2]
+    out_half, up_half, down_half = (
+        lax.dynamic_slice_in_dim(
+            weight[0], core_id * (weight.shape[1] // 2), weight.shape[1] // 2, 0
+        )
+        for weight in (attn_out, mlp_in, mlp_out)
+    )
+    panels = [up_half[:, start : start + width] for start in range(0, mlp_in.shape[2], width)]
+    packed = jnp.concatenate([down_half] + panels + [out_half], 0)
+    everyone = lax.all_gather(packed, ("fsdp", "core"), axis=0)
+    down_rows, up_rows = down_half.shape[0], up_half.shape[0]
+    w_down = everyone[:, :down_rows].reshape(-1, width)
+    w_up = jnp.concatenate(
+        [
+            everyone[:, start : start + up_rows].reshape(-1, width)
+            for start in range(down_rows, 2 * down_rows, up_rows)
+        ],
+        1,
+    )
+    w_out = everyone[:, 2 * down_rows :].reshape(-1, width)
+    return w_out, w_up, w_down
+
+
+def split_cores(value, axis):
+    core_id = lax.axis_index("core")
+    kept = lax.dynamic_index_in_dim(value, core_id, axis, keepdims=False)
+    sent = lax.dynamic_index_in_dim(value, 1 - core_id, axis, keepdims=False)
+    return kept, swap(sent)
 
 
 def sum_low(value):
@@ -409,9 +453,7 @@
     w_group = first_all[:, :shard].reshape(-1, 3 * WIDTH)
     small_all = first_all[:, shard : shard + small.shape[0]].reshape(fsdp_count, -1, shard)
     small_all = small_all.astype(jnp.float32)
-    w_out = gather_weight(attn_out)
-    w_up = gather_weight(mlp_in)
-    w_down = gather_weight(mlp_out)
+    w_out, w_up, w_down = gather_weights(attn_out, mlp_in, mlp_out)
     model_width = w_out.shape[0]
     half = model_width // 2
     w_group = jnp.concatenate(in_order(w_group[:half], w_group[half:]), 0)
@@ -501,19 +543,26 @@
         share = None
         grad_heads = exchange(grad_mixed.reshape(-1, local_rows, WIDTH), CTX).reshape(-1, WIDTH)
         if last:
+            active_pair = split_cores(active_low.reshape(rows, fsdp_count, 2, -1), 2)
+            normed_pair = split_cores(normed_two_low.T.reshape(fsdp_count, 2, -1, rows), 1)
+            mixed_pair = split_cores(
+                mixed.transpose(1, 3, 0, 2).reshape(fsdp_count, 2, -1, rows), 1
+            )
             joint = weight_grads(
-                active_low,
-                grad_low,
-                normed_two_low.T,
-                grad_hidden,
-                mixed.transpose(1, 3, 0, 2).reshape(model_width, rows),
-                grad_attn,
-                2 * fsdp_count,
+                [
+                    [value.reshape(rows, -1) for value in active_pair],
+                    (grad_low, swap(grad_low)),
+                    [value.reshape(-1, rows) for value in normed_pair],
+                    (grad_hidden, swap(grad_hidden)),
+                    [value.reshape(-1, rows) for value in mixed_pair],
+                    (grad_attn, swap(grad_attn)),
+                ],
+                fsdp_count,
             )
             grad_heads, joint = lax.optimization_barrier((grad_heads, joint))
             share = lax.psum_scatter(
                 joint.reshape(-1, model_width),
-                ("fsdp", "core"),
+                "fsdp",
                 scatter_dimension=0,
                 tiled=True,
             )
@@ -578,6 +627,7 @@
     qkv_piece = sum_low(exchange(pieces, ("fsdp", "x")))
     qkv_piece = jnp.pad(qkv_piece, ((0, 0), (0, model_width - 3 * WIDTH)))
     joint_piece = sum_low(exchange(share.reshape(8, -1, model_width), ("x", "yh")))
+    joint_piece, layer_out = lax.optimization_barrier((joint_piece, layer_out))
     both = spread(jnp.concatenate([joint_piece, qkv_piece], 0), ("x", "yh"))
     g_qkv, g_out, g_up, g_down, vector_sum = unpack(
         core_number, both, swap(both), shard, mlp_in.shape[2], mlp_out.shape[1]

time: 474 us -> 465 us (0.981)
  the two profiles are of different devices: /device:TPU:33 before, /device:TPU:1 now
where the time goes in v5:
time: 465 us; the launch traced here: 457 us
  blocking collectives  123 us (26%)
  waiting for transfers between devices  76.1 us (16%)
  Pallas kernels  65.4 us (14%)
  local copies, waits for them, and re-layouts  57 us (12%)
  starting transfers between devices  51.7 us (11%)
  matrix products  39.7 us (9%)
  between operations  23.5 us (5%)
  other arithmetic  20.3 us (4%)
    all_to_all x6, blocking collectives, exchange(): return lax.all_to_all(value, axes, 0, 0, tiled=True)  123 us
    all_to_all x6, waiting for transfers between devices, exchange(): return lax.all_to_all(value, axes, 0, 0, tiled=True)  61 us
    all_to_all x6, starting transfers between devices, exchange(): return lax.all_to_all(value, axes, 0, 0, tiled=True)  40.3 us
    dot_general x10, matrix products, cross(): jnp.einsum(pattern, left_side, right_side, preferred_element_type=jnp.flo...  39.7 us
    pallas_call x2, Pallas kernels, attend_back(): pl.pallas_call(attend_back_body, grid=(count // QUERY_BLOCK,), in_specs=[...  30 us
    pallas_call x2, Pallas kernels, attend(): pl.pallas_call(attend_body, grid=(count // QUERY_BLOCK,), in_specs=[pl.Bl...  21.7 us
    unnamed x151, local copies, waits for them, and re-layouts  13.6 us
  transfers between devices with their start and end apart: 21, of which 11 were waited for; matrix products, arithmetic and copies ran while one was open for 14% of the time, Pallas kernels for 8%

profile of v5, /device:TPU:1, one launch (start us, length us, event | category | flops | bytes accessed | tf_op | source)
XLA Modules:
  0.0 456.7 jit_solution(1179281471725765873)
XLA Ops:
  15.3 5.9 %all-to-all-start = ((bf16[4,208,576]{2,1,0:T(8,128)(2,1)}), bf16[4,208,576]{2,1,0:T(8,128)(2,1)S(1)}, u32[]{:S(2)}, u32[]{:S(2)}) async-start(bf16[4,208,576]{2,1,0:T(8,128)(2,1)} %broadcast_in_dim.112), calls=%async_computation | async-start | bytes 2129920 | tf_op jit(solution)/shard_map/all_to_all | solution.py:368
  30.4 11.1 %all-to-all-done = bf16[4,208,576]{2,1,0:T(8,128)(2,1)S(1)} async-done(((bf16[4,208,576]{2,1,0:T(8,128)(2,1)}), bf16[4,208,576]{2,1,0:T(8,128)(2,1)S(1)}, u32[]{:S(2)}, u32[]{:S(2)}) %all-to-all-start) | async-done | bytes 958496 | tf_op jit(solution)/shard_map/all_to_all | solution.py:368
  44.3 12.0 %all-to-all-start.1 = ((bf16[16,64,384]{2,1,0:T(8,128)(2,1)}), bf16[16,64,384]{2,1,0:T(8,128)(2,1)S(1)}, u32[]{:S(2)}, u32[]{:S(2)}) async-start(bf16[16,64,384]{2,1,0:T(8,128)(2,1)} %bitcast.19), calls=%async_computation.1 | async-start | bytes 1572864 | tf_op jit(solution)/shard_map/all_to_all | solution.py:368
  56.3 14.1 %all-to-all-done.1 = bf16[16,64,384]{2,1,0:T(8,128)(2,1)S(1)} async-done(((bf16[16,64,384]{2,1,0:T(8,128)(2,1)}), bf16[16,64,384]{2,1,0:T(8,128)(2,1)S(1)}, u32[]{:S(2)}, u32[]{:S(2)}) %all-to-all-start.1) | async-done | bytes 786464 | tf_op jit(solution)/shard_map/all_to_all | solution.py:368
  74.5 11.2 %shard_map.178 = (bf16[1024,576]{1,0:T(8,128)(2,1)}, bf16[1024,192]{1,0:T(8,128)(2,1)}, f32[8,1024]{1,0:T(8,128)}) custom-call(s32[1,1024]{1,0:T(1,128)S(1)} %add.273.row_places, s32[1024,1]{1,0:T(8,128)S(1)} %add.323.column_places, bf16[1024,384]{1,0:T(8,128)(2,1)S(1)} %bitcast.199, bf16[1024,384]{1,0:T(8,128)(2,1)S(1)} %collective-permute-done.other, ...), custom_call_target="tpu_custom_call" | custom-call | flops 805306368 | bytes 1572864 | tf_op jit(solution)/shard_map/pallas_call | solution.py:70
  85.7 3.7 all-to-all-start.2
  90.6 9.9 %all-to-all-done.2 = bf16[16,64,192]{2,1,0:T(8,128)(2,1)S(1)} async-done(((bf16[16,64,192]{2,1,0:T(8,128)(2,1)}), bf16[16,64,192]{2,1,0:T(8,128)(2,1)S(1)}, u32[]{:S(2)}, u32[]{:S(2)}) %all-to-all-start.2) | async-done | bytes 393248 | tf_op jit(solution)/shard_map/all_to_all | solution.py:368
  100.6 4.9 %fusion.86 = (bf16[8,96,768]{2,1,0:T(8,128)(2,1)}, bf16[8,96,768]{2,1,0:T(8,128)(2,1)}, bf16[8,96,768]{2,1,0:T(8,128)(2,1)}, bf16[8,96,768]{2,1,0:T(8,128)(2,1)}, bf16[8,96,768]{2,1,0:T(8,128)(2,1)S(1)}) fusion(bf16[8,864,768]{2,1,0:T(8,128)(2,1)} %bitcast.205), kind=kLoop, calls=%fused_computation.187 | loop fusion | bytes 11796480 | tf_op jit(solution)/shard_map/slice | solution.py:396
  105.5 5.3 %slice.280 = bf16[8,384,768]{2,1,0:T(8,128)(2,1)} slice(bf16[8,864,768]{2,1,0:T(8,128)(2,1)} %bitcast.206), slice={[0:8], [0:384], [0:768]} | slice | bytes 9437184 | tf_op jit(solution)/shard_map/slice | solution.py:393
  111.6 6.7 %fusion.26 = bf16[256,768]{1,0:T(8,128)(2,1)S(1)} fusion(f32[256,768]{1,0:T(8,128)S(1)} %get-tuple-element.155, bf16[3072,768]{1,0:T(8,128)(2,1)} %bitcast.212, f32[3072]{0:T(1024)S(1)} %add.289, f32[768]{0:T(1024)S(1)} %add.294, f32[768]{0:T(1024)S(1)} %add.286, f32[768]{0:T(1024)S(1)} %mul.320, f32[256]{0:T(256)S(1)} %add_rsqrt_fusion.3, ...), kind=kOutput, calls=%fused_computation.46 | convolution fusion | flops 2444230656 | bytes 10640384 | tf_op jit(solution)/shard_map/tf,fd->td/dot_general | solution.py:342
  118.3 2.4 collective-permute-start.1
  120.8 6.8 %collective-permute-done.1 = bf16[256,768]{1,0:T(8,128)(2,1)S(1)} collective-permute-done((bf16[256,768]{1,0:T(8,128)(2,1)S(1)}, bf16[256,768]{1,0:T(8,128)(2,1)S(1)}, u32[]{:S(2)}, u32[]{:S(2)}) %collective-permute-start.1) | collective-permute-done | bytes 393248 | tf_op jit(solution)/shard_map/ppermute | solution.py:603
  128.7 20.6 %all_to_all.60 = bf16[16,64,384]{2,1,0:T(8,128)(2,1)S(1)} all-to-all(bf16[16,64,384]{2,1,0:T(8,128)(2,1)S(1)} %bitcast.218), channel_id=1, replica_groups=mesh['section'=2,'x'=4,'yh'=2,'core'=2,'fsdp'=4] {'x','yh','core'}, dimensions={0} | all-to-all | bytes 1572864 | tf_op jit(solution)/shard_map/all_to_all | solution.py:368
  149.7 1.9 collective-permute-done.2.other
  151.6 10.5 %shard_map.179 = (bf16[1024,576]{1,0:T(8,128)(2,1)S(1)}, bf16[1024,192]{1,0:T(8,128)(2,1)S(1)}, f32[8,1024]{1,0:T(8,128)S(1)}) custom-call(s32[1,1024]{1,0:T(1,128)S(1)} %add.273.row_places, s32[1024,1]{1,0:T(8,128)S(1)} %add.323.column_places, bf16[1024,384]{1,0:T(8,128)(2,1)S(1)} %bitcast.196, bf16[1024,384]{1,0:T(8,128)(2,1)S(1)} %collective-permute-done.2.other, ...), custom_call_target="tpu_custom_call" | custom-call | flops 805306368 | bytes 1572864 | tf_op jit(solution)/shard_map/pallas_call | solution.py:70
  162.2 14.8 %all_to_all.61 = bf16[16,64,192]{2,1,0:T(8,128)(2,1)S(1)} all-to-all(bf16[16,64,192]{2,1,0:T(8,128)(2,1)S(1)} %bitcast.203), channel_id=1, replica_groups=mesh['section'=2,'x'=4,'yh'=2,'core'=2,'fsdp'=4] {'x','yh','core'}, dimensions={0} | all-to-all | bytes 786432 | tf_op jit(solution)/shard_map/all_to_all | solution.py:368
  178.0 6.0 %multiply_convert_fusion = (bf16[256,3072]{1,0:T(8,128)(2,1)}, f32[256,3072]{1,0:T(8,128)}) fusion(f32[3072]{0:T(1024)S(1)} %add.289, bf16[768,768]{1,0:T(8,128)(2,1)S(1)} %bitcast.241, bf16[768,768]{1,0:T(8,128)(2,1)S(1)} %bitcast.245, bf16[768,768]{1,0:T(8,128)(2,1)S(1)} %bitcast.249, bf16[768,768]{1,0:T(8,128)(2,1)S(1)} %bitcast.237, f32[768]{0:T(1024)S(1)} %add.286, ...), kind=kOutput, calls=%fused_computation.19 | convolution fusion | flops 1235681280 | bytes 10244096 | tf_op jit(solution)/shard_map/td,df->tf/dot_general | solution.py:342
  184.0 10.1 %fusion.79 = (f32[256]{0:T(256)S(1)}, f32[256]{0:T(256)S(1)}, f32[256,768]{1,0:T(8,128)}) fusion(f32[256]{0:T(256)S(1)} %add_rsqrt_fusion.1, f32[256,768]{1,0:T(8,128)S(1)} %get-tuple-element.157, f32[256]{0:T(256)S(1)} %broadcast_multiply_fusion.9, f32[768]{0:T(1024)S(1)} %mul.320, bf16[768,768]{1,0:T(8,128)(2,1)} %bitcast.240, ...), kind=kOutput, calls=%fused_computation.182 | convolution fusion | flops 2451701248 | bytes 14556160 | tf_op jit(solution)/shard_map/tf,df->td/dot_general | solution.py:342
  194.2 2.4 fusion.85
  197.3 15.0 %all_to_all.62 = bf16[16,64,192]{2,1,0:T(8,128)(2,1)S(1)} all-to-all(bf16[16,64,192]{2,1,0:T(8,128)(2,1)S(1)} %bitcast.224), channel_id=1, replica_groups=mesh['section'=2,'x'=4,'yh'=2,'core'=2,'fsdp'=4] {'x','yh','core'}, dimensions={0} | all-to-all | bytes 786432 | tf_op jit(solution)/shard_map/all_to_all | solution.py:368
  212.3 15.5 %shard_map.180 = (bf16[1024,576]{1,0:T(8,128)(2,1)}, bf16[1024,384]{1,0:T(8,128)(2,1)S(1)}, bf16[1024,384]{1,0:T(8,128)(2,1)S(1)}) custom-call(s32[1,1024]{1,0:T(1,128)S(1)} %add.273.row_places, s32[1024,1]{1,0:T(8,128)S(1)} %add.323.column_places, bf16[1024,576]{1,0:T(8,128)(2,1)} %copy-done.12, bf16[1024,192]{1,0:T(8,128)(2,1)S(1)} %bitcast.202, ...), custom_call_target="tpu_custom_call" | custom-call | flops 2013265920 | bytes 3145728 | tf_op jit(solution)/shard_map/pallas_call | solution.py:150
  227.7 1.4 collective-permute-start.3
  229.1 1.9 collective-permute-done.3
  231.2 17.5 %all_to_all.63 = bf16[16,64,384]{2,1,0:T(8,128)(2,1)S(1)} all-to-all(bf16[16,64,384]{2,1,0:T(8,128)(2,1)S(1)} %bitcast.221), channel_id=1, replica_groups=mesh['section'=2,'x'=4,'yh'=2,'core'=2,'fsdp'=4] {'x','yh','core'}, dimensions={0} | all-to-all | bytes 1572864 | tf_op jit(solution)/shard_map/all_to_all | solution.py:368
  252.5 4.1 reshape.603
  256.6 4.4 constant_dynamic-slice_fusion.4
  262.8 1.9 constant_dynamic-slice_fusion.1
  265.7 1.7 fusion.81
  267.4 7.5 %fusion.80 = (bf16[3072]{0:T(1024)(128)(2,1)}, bf16[256,3072]{1,0:T(8,128)(2,1)S(1)}) fusion(f32[256,3072]{1,0:T(8,128)} %get-tuple-element.160, bf16[256,768]{1,0:T(8,128)(2,1)S(1)} %get-tuple-element.107.grad_low, bf16[3072,768]{1,0:T(8,128)(2,1)} %bitcast.214), kind=kOutput, calls=%fused_computation.183 | convolution fusion | flops 1224471552 | bytes 9836544 | tf_op jit(solution)/shard_map/td,fd->tf/dot_general | solution.py:342
  275.4 1.9 fusion.77
  280.3 3.1 fusion.82
  286.1 4.1 all-to-all-start.7
  290.3 4.6 %copy.92 = bf16[256,4,1,384]{0,3,1,2:T(8,128)(2,1)} copy(bf16[256,4,1,384]{3,2,1,0:T(2,128)(2,1)} %get-tuple-element.126) | data formatting | bytes 1572864
  294.9 1.4 copy.78.active
  298.8 7.4 %shard_map.181 = bf16[4,896,768]{2,1,0:T(8,128)(2,1)} custom-call(bf16[256,1536]{1,0:T(8,128)(2,1)S(1)} %copy.78.active, bf16[256,1536]{1,0:T(8,128)(2,1)S(1)} %bitcast.193, bf16[256,768]{1,0:T(8,128)(2,1)S(1)} %get-tuple-element.107.grad_low, bf16[256,768]{1,0:T(8,128)(2,1)} %collective-permute-done.6.grad_low_other, bf16[384,256]{1,0:T(8,128)(2,1)S(1)} %bitcast.200, ...), custom_call_target="tpu_custom_call" | custom-call | flops 2717908992 | bytes 5505024 | tf_op jit(solution)/shard_map/pallas_call | solution.py:228
  307.6 14.5 %shard_map.182 = (bf16[1024,576]{1,0:T(8,128)(2,1)S(1)}, bf16[1024,384]{1,0:T(8,128)(2,1)S(1)}, bf16[1024,384]{1,0:T(8,128)(2,1)S(1)}) custom-call(s32[1,1024]{1,0:T(1,128)S(1)} %add.273.row_places, s32[1024,1]{1,0:T(8,128)S(1)} %copy-done.7, bf16[1024,576]{1,0:T(8,128)(2,1)} %copy-done.12, bf16[1024,192]{1,0:T(8,128)(2,1)} %bitcast.62.grad_mixed, ...), custom_call_target="tpu_custom_call" | custom-call | flops 2013265920 | bytes 3145728 | tf_op jit(solution)/shard_map/pallas_call | solution.py:150
  322.5 2.1 collective-permute-done.11
  325.7 7.6 %all-to-all-start.9 = ((bf16[16,64,384]{2,1,0:T(8,128)(2,1)}), bf16[16,64,384]{2,1,0:T(8,128)(2,1)}, u32[]{:S(2)}, u32[]{:S(2)}) async-start(bf16[16,64,384]{2,1,0:T(8,128)(2,1)} %bitcast.78), calls=%async_computation.10 | async-start | bytes 1572864 | tf_op jit(solution)/shard_map/all_to_all | solution.py:368
  335.0 1.4 shard_map.183
  336.6 10.8 %all-to-all-done.9 = bf16[16,64,384]{2,1,0:T(8,128)(2,1)} async-done(((bf16[16,64,384]{2,1,0:T(8,128)(2,1)}), bf16[16,64,384]{2,1,0:T(8,128)(2,1)}, u32[]{:S(2)}, u32[]{:S(2)}) %all-to-all-start.9) | async-done | bytes 786464 | tf_op jit(solution)/shard_map/all_to_all | solution.py:368
  352.1 24.6 %all_to_all.64 = bf16[16,64,576]{2,1,0:T(8,128)(2,1)} all-to-all(bf16[16,64,576]{2,1,0:T(8,128)(2,1)S(1)} %scatter.4), channel_id=1, replica_groups=mesh['section'=2,'x'=4,'yh'=2,'core'=2,'fsdp'=4] {'fsdp','x'}, dimensions={0} | all-to-all | bytes 2359296 | tf_op jit(solution)/shard_map/all_to_all | solution.py:368
  377.7 7.0 %all-to-all-start.8 = ((bf16[8,112,768]{2,1,0:T(8,128)(2,1)}), bf16[8,112,768]{2,1,0:T(8,128)(2,1)S(1)}, u32[]{:S(2)}, u32[]{:S(2)}) async-start(bf16[8,112,768]{2,1,0:T(8,128)(2,1)} %bitcast.230), calls=%async_computation.9 | async-start | bytes 2752512 | tf_op jit(solution)/shard_map/all_to_all | solution.py:368
  384.7 5.0 %fusion.27 = bf16[256,768]{1,0:T(8,128)(2,1)} fusion(f32[256,768]{1,0:T(8,128)S(1)} %copy-done.19, bf16[256,3072]{1,0:T(8,128)(2,1)} %get-tuple-element.159, bf16[3072,768]{1,0:T(8,128)(2,1)} %bitcast.215, f32[768]{0:T(1024)S(1)} %copy-done.63), kind=kOutput, calls=%fused_computation.47 | convolution fusion | flops 1208549376 | bytes 7474176 | tf_op jit(solution)/shard_map/tf,fd->td/dot_general | solution.py:342
  390.0 15.1 %all-to-all-done.8 = bf16[8,112,768]{2,1,0:T(8,128)(2,1)S(1)} async-done(((bf16[8,112,768]{2,1,0:T(8,128)(2,1)}), bf16[8,112,768]{2,1,0:T(8,128)(2,1)S(1)}, u32[]{:S(2)}, u32[]{:S(2)}) %all-to-all-start.8) | async-done | bytes 1376288 | tf_op jit(solution)/shard_map/all_to_all | solution.py:368
  405.4 30.5 %all_to_all.65.own = bf16[8,176,768]{2,1,0:T(8,128)(2,1)S(1)} all-to-all(bf16[8,176,768]{2,1,0:T(8,128)(2,1)S(1)} %broadcast_in_dim.126), channel_id=1, replica_groups=mesh['section'=2,'x'=4,'yh'=2,'core'=2,'fsdp'=4] {'x','yh'}, dimensions={0} | all-to-all | bytes 4325376 | tf_op jit(solution)/shard_map/all_to_all | solution.py:368
  435.9 2.6 collective-permute-start.12
  438.6 2.6 fusion.49
  442.5 4.8 %shard_map.184 = (f32[192,2304]{1,0:T(8,128)}, f32[192,768]{1,0:T(8,128)}, f32[192,3072]{1,0:T(8,128)}, f32[768,768]{1,0:T(8,128)}, f32[4,768]{1,0:T(4,128)S(1)}) custom-call(s32[1]{0:T(128)} %bitcast.86.core_id, bf16[8,176,768]{2,1,0:T(8,128)(2,1)S(1)} %all_to_all.65.own, bf16[8,176,768]{2,1,0:T(8,128)(2,1)} %collective-permute-done.12.other), custom_call_target="tpu_custom_call" | custom-call | bytes 12582912 | tf_op jit(solution)/shard_map/pallas_call | solution.py:324
  (303 shorter events, 50.8 us)
Async XLA Ops:
  7.2 93.3 %all-gather.3.cloned.1.call-start = ((), (), s32[]{:S(2)}) async-start(), calls=%async_computation.14 | async-start | bytes 11943936 | tf_op jit(solution)/shard_map/all_gather | solution.py:391
  12.3 17.2 %copy-start.44 = (bf16[4,1,64,768]{3,2,1,0:T(8,128)(2,1)S(1)}, bf16[4,1,64,768]{3,2,1,0:T(8,128)(2,1)}, u32[]{:S(2)}) copy-start(bf16[4,1,64,768]{3,2,1,0:T(8,128)(2,1)} %param.13) | copy-start | bytes 1179652
  15.3 26.3 %all-to-all-start = ((bf16[4,208,576]{2,1,0:T(8,128)(2,1)}), bf16[4,208,576]{2,1,0:T(8,128)(2,1)S(1)}, u32[]{:S(2)}, u32[]{:S(2)}) async-start(bf16[4,208,576]{2,1,0:T(8,128)(2,1)} %broadcast_in_dim.112), calls=%async_computation | async-start | bytes 2129920 | tf_op jit(solution)/shard_map/all_to_all | solution.py:368
  29.7 26.5 %copy-start.67 = (s32[32]{0:T(128)S(1)}, s32[32]{0:T(128)}, u32[]{:S(2)}) copy-start(s32[32]{0:T(128)} %param.16) | copy-start | bytes 388
  44.3 26.1 %all-to-all-start.1 = ((bf16[16,64,384]{2,1,0:T(8,128)(2,1)}), bf16[16,64,384]{2,1,0:T(8,128)(2,1)S(1)}, u32[]{:S(2)}, u32[]{:S(2)}) async-start(bf16[16,64,384]{2,1,0:T(8,128)(2,1)} %bitcast.19), calls=%async_computation.1 | async-start | bytes 1572864 | tf_op jit(solution)/shard_map/all_to_all | solution.py:368
  70.4 4.1 collective-permute-start
  72.2 140.0 %copy-start.6 = (s32[1024,1]{1,0:T(8,128)}, s32[1024,1]{1,0:T(8,128)S(1)}, u32[]{:S(2)}) copy-start(s32[1024,1]{1,0:T(8,128)S(1)} %add.323.column_places) | copy-start | bytes 12292
  74.5 137.7 %copy-start.2 = (bf16[768,576]{1,0:T(8,128)(2,1)}, bf16[768,576]{1,0:T(8,128)(2,1)S(1)}, u32[]{:S(2)}) copy-start(bf16[768,576]{1,0:T(8,128)(2,1)S(1)} %pad_maximum_fusion.1.weight) | copy-start | bytes 2654212
  85.7 14.8 %all-to-all-start.2 = ((bf16[16,64,192]{2,1,0:T(8,128)(2,1)}), bf16[16,64,192]{2,1,0:T(8,128)(2,1)S(1)}, u32[]{:S(2)}, u32[]{:S(2)}) async-start(bf16[16,64,192]{2,1,0:T(8,128)(2,1)} %bitcast.25), calls=%async_computation.2 | async-start | bytes 1048576 | tf_op jit(solution)/shard_map/all_to_all | solution.py:368
  90.4 87.6 %copy-start.54 = (f32[768]{0:T(1024)}, f32[768]{0:T(1024)S(1)}, u32[]{:S(2)}) copy-start(f32[768]{0:T(1024)S(1)} %add.286) | copy-start | bytes 9220
  90.4 93.6 %copy-start.46 = (f32[768]{0:T(1024)}, f32[768]{0:T(1024)S(1)}, u32[]{:S(2)}) copy-start(f32[768]{0:T(1024)S(1)} %mul.320) | copy-start | bytes 9220
  90.6 21.0 %copy-start.62 = (f32[768]{0:T(1024)}, f32[768]{0:T(1024)S(1)}, u32[]{:S(2)}) copy-start(f32[768]{0:T(1024)S(1)} %add.294) | copy-start | bytes 9220
  118.3 9.4 %collective-permute-start.1 = (bf16[256,768]{1,0:T(8,128)(2,1)S(1)}, bf16[256,768]{1,0:T(8,128)(2,1)S(1)}, u32[]{:S(2)}, u32[]{:S(2)}) collective-permute-start(bf16[256,768]{1,0:T(8,128)(2,1)S(1)} %fusion.26), channel_id=1, source_target_pairs={{0,64},{1,65},{2,66},{3,67},{4,68},{5,69},{6,70},{7,71},{8,72},{9,... | collective-permute-start | bytes 1179656 | tf_op jit(solution)/shard_map/ppermute | solution.py:603
  127.9 122.3 %copy-start.15 = (bf16[256,768]{1,0:T(8,128)(2,1)}, bf16[256,768]{1,0:T(8,128)(2,1)S(1)}, u32[]{:S(2)}) copy-start(bf16[256,768]{1,0:T(8,128)(2,1)S(1)} %get-tuple-element.117) | copy-start | bytes 1179652
  128.2 122.0 %copy-start.48 = (f32[256]{0:T(256)}, f32[256]{0:T(256)S(1)}, u32[]{:S(2)}) copy-start(f32[256]{0:T(256)S(1)} %add_rsqrt_fusion.2) | copy-start | bytes 3076
  149.3 27.7 %copy-start.4 = (bf16[16,64,384]{2,1,0:T(8,128)(2,1)}, bf16[16,64,384]{2,1,0:T(8,128)(2,1)S(1)}, u32[]{:S(2)}) copy-start(bf16[16,64,384]{2,1,0:T(8,128)(2,1)S(1)} %all_to_all.60) | copy-start | bytes 2359300
  149.3 27.7 %copy-start.32 = (bf16[8,96,768]{2,1,0:T(8,128)(2,1)S(1)}, bf16[8,96,768]{2,1,0:T(8,128)(2,1)}, u32[]{:S(2)}) copy-start(bf16[8,96,768]{2,1,0:T(8,128)(2,1)} %copy-done.31) | copy-start | bytes 3538948
  149.3 2.3 collective-permute-start.2
  151.6 25.4 %copy-start.8 = (bf16[1024,384]{1,0:T(8,128)(2,1)}, bf16[1024,384]{1,0:T(8,128)(2,1)S(1)}, u32[]{:S(2)}) copy-start(bf16[1024,384]{1,0:T(8,128)(2,1)S(1)} %collective-permute-done.2.other) | copy-start | bytes 2359300
  162.2 21.8 %copy-start.12 = (bf16[1024,576]{1,0:T(8,128)(2,1)}, bf16[1024,576]{1,0:T(8,128)(2,1)S(1)}, u32[]{:S(2)}) copy-start(bf16[1024,576]{1,0:T(8,128)(2,1)S(1)} %get-tuple-element.43.joined) | copy-start | bytes 3538948
  162.2 50.1 %copy-start.13 = (f32[8,1024]{1,0:T(8,128)}, f32[8,1024]{1,0:T(8,128)S(1)}, u32[]{:S(2)}) copy-start(f32[8,1024]{1,0:T(8,128)S(1)} %get-tuple-element.44.log_total) | copy-start | bytes 98308
  162.2 15.8 %copy-start.35 = (bf16[8,96,768]{2,1,0:T(8,128)(2,1)S(1)}, bf16[8,96,768]{2,1,0:T(8,128)(2,1)}, u32[]{:S(2)}) copy-start(bf16[8,96,768]{2,1,0:T(8,128)(2,1)} %get-tuple-element.120) | copy-start | bytes 3538948
  162.2 15.8 %copy-start.37 = (bf16[8,96,768]{2,1,0:T(8,128)(2,1)S(1)}, bf16[8,96,768]{2,1,0:T(8,128)(2,1)}, u32[]{:S(2)}) copy-start(bf16[8,96,768]{2,1,0:T(8,128)(2,1)} %get-tuple-element.121) | copy-start | bytes 3538948
  162.2 15.8 %copy-start.39 = (bf16[8,96,768]{2,1,0:T(8,128)(2,1)S(1)}, bf16[8,96,768]{2,1,0:T(8,128)(2,1)}, u32[]{:S(2)}) copy-start(bf16[8,96,768]{2,1,0:T(8,128)(2,1)} %get-tuple-element.122) | copy-start | bytes 3538948
  162.2 15.8 %copy-start.41 = (bf16[8,96,768]{2,1,0:T(8,128)(2,1)S(1)}, bf16[8,96,768]{2,1,0:T(8,128)(2,1)}, u32[]{:S(2)}) copy-start(bf16[8,96,768]{2,1,0:T(8,128)(2,1)} %get-tuple-element.123) | copy-start | bytes 3538948
  177.7 16.5 %copy-start.17 = (f32[256,768]{1,0:T(8,128)}, f32[256,768]{1,0:T(8,128)S(1)}, u32[]{:S(2)}) copy-start(f32[256,768]{1,0:T(8,128)S(1)} %get-tuple-element.157) | copy-start | bytes 2359300
  177.7 16.5 %copy-start.50 = (f32[256]{0:T(256)}, f32[256]{0:T(256)S(1)}, u32[]{:S(2)}) copy-start(f32[256]{0:T(256)S(1)} %broadcast_multiply_fusion.9) | copy-start | bytes 3076
  178.0 16.2 %copy-start.52 = (f32[256]{0:T(256)}, f32[256]{0:T(256)S(1)}, u32[]{:S(2)}) copy-start(f32[256]{0:T(256)S(1)} %add_rsqrt_fusion.1) | copy-start | bytes 3076
  227.7 3.3 collective-permute-start.3
  251.2 14.5 %collective-permute-start.4 = (bf16[256,768]{1,0:T(8,128)(2,1)}, bf16[256,768]{1,0:T(8,128)(2,1)}, u32[]{:S(2)}, u32[]{:S(2)}) collective-permute-start(bf16[256,768]{1,0:T(8,128)(2,1)} %fusion.44), channel_id=1, source_target_pairs={{64,0},{65,1},{66,2},{67,3},{68,4},{69,5},{70,6},{71,7},{72,8},{73... | collective-permute-start | bytes 1179656 | tf_op jit(solution)/shard_map/ppermute | solution.py:611
  262.0 22.2 %collective-permute-start.5 = (bf16[256,4,384]{2,0,1:T(8,128)(2,1)}, bf16[256,4,384]{2,0,1:T(8,128)(2,1)}, u32[]{:S(2)}, u32[]{:S(2)}) collective-permute-start(bf16[256,4,384]{2,0,1:T(8,128)(2,1)} %bitcast.192), channel_id=1, source_target_pairs={{0,4},{4,0},{1,5},{5,1},{2,6},{6,2},{3,7},{7,3},{8,12},{12,8},{9,1... | collective-permute-start | bytes 2359304 | tf_op jit(solution)/shard_map/ppermute | solution.py:372
  265.6 33.2 %collective-permute-start.9 = (bf16[4,96,256]{2,1,0:T(8,128)(2,1)}, bf16[4,96,256]{2,1,0:T(8,128)(2,1)}, u32[]{:S(2)}, u32[]{:S(2)}) collective-permute-start(bf16[4,96,256]{2,1,0:T(8,128)(2,1)} %bitcast.72), channel_id=1, source_target_pairs={{0,4},{4,0},{1,5},{5,1},{2,6},{6,2},{3,7},{7,3},{8,12},{12,8},{9,1... | collective-permute-start | bytes 589832 | tf_op jit(solution)/shard_map/ppermute | solution.py:372
  274.9 23.9 %collective-permute-start.8 = (bf16[256,3072]{1,0:T(8,128)(2,1)S(1)}, bf16[256,3072]{1,0:T(8,128)(2,1)}, u32[]{:S(2)}, u32[]{:S(2)}) collective-permute-start(bf16[256,3072]{1,0:T(8,128)(2,1)S(1)} %get-tuple-element.105.grad_hidden), channel_id=1, source_target_pairs={{0,4},{4,0},{1,5},{5,1},{2,6},{6,2},{3,7},{7,3},{8,12},{12,8},{9,1... | collective-permute-start | bytes 4718600 | tf_op jit(solution)/shard_map/ppermute | solution.py:372
  277.4 21.4 %collective-permute-start.6 = (bf16[256,768]{1,0:T(8,128)(2,1)S(1)}, bf16[256,768]{1,0:T(8,128)(2,1)}, u32[]{:S(2)}, u32[]{:S(2)}) collective-permute-start(bf16[256,768]{1,0:T(8,128)(2,1)S(1)} %get-tuple-element.107.grad_low), channel_id=1, source_target_pairs={{0,4},{4,0},{1,5},{5,1},{2,6},{6,2},{3,7},{7,3},{8,12},{12,8},{9,1... | collective-permute-start | bytes 1179656 | tf_op jit(solution)/shard_map/ppermute | solution.py:372
  283.4 15.4 %collective-permute-start.10 = (bf16[256,768]{1,0:T(8,128)(2,1)S(1)}, bf16[256,768]{1,0:T(8,128)(2,1)}, u32[]{:S(2)}, u32[]{:S(2)}) collective-permute-start(bf16[256,768]{1,0:T(8,128)(2,1)S(1)} %get-tuple-element.109.grad_attn), channel_id=1, source_target_pairs={{0,4},{4,0},{1,5},{5,1},{2,6},{6,2},{3,7},{7,3},{8,12},{12,8},{9,1... | collective-permute-start | bytes 1179656 | tf_op jit(solution)/shard_map/ppermute | solution.py:372
  284.2 14.5 %collective-permute-start.7 = (bf16[4,96,256]{2,1,0:T(8,128)(2,1)}, bf16[4,96,256]{2,1,0:T(8,128)(2,1)}, u32[]{:S(2)}, u32[]{:S(2)}) collective-permute-start(bf16[4,96,256]{2,1,0:T(8,128)(2,1)} %get-tuple-element.132), channel_id=1, source_target_pairs={{0,4},{4,0},{1,5},{5,1},{2,6},{6,2},{3,7},{7,3},{8,12},{12,8},{9,1... | collective-permute-start | bytes 589832 | tf_op jit(solution)/shard_map/ppermute | solution.py:372
  286.1 20.2 %all-to-all-start.7 = ((bf16[16,64,192]{2,1,0:T(8,128)(2,1)}), bf16[16,64,192]{2,1,0:T(8,128)(2,1)}, u32[]{:S(2)}, u32[]{:S(2)}) async-start(bf16[16,64,192]{2,1,0:T(8,128)(2,1)} %bitcast.61), calls=%async_computation.7 | async-start | bytes 1048576 | tf_op jit(solution)/shard_map/all_to_all | solution.py:368
  290.2 87.5 %reduce-scatter.2.cloned.1.call-start = ((), (), s32[]{:S(2)}) async-start(), calls=%async_computation.13 | async-start | bytes 6881280 | tf_op jit(solution)/shard_map/reduce_scatter | solution.py:563
  322.2 11.4 %copy-start.56 = (bf16[768]{0:T(1024)(128)(2,1)S(1)}, bf16[768]{0:T(1024)(128)(2,1)}, u32[]{:S(2)}) copy-start(bf16[768]{0:T(1024)(128)(2,1)} %get-tuple-element.106) | copy-start | bytes 4612
  322.2 11.5 %copy-start.61 = (bf16[3072]{0:T(1024)(128)(2,1)S(1)}, bf16[3072]{0:T(1024)(128)(2,1)}, u32[]{:S(2)}) copy-start(bf16[3072]{0:T(1024)(128)(2,1)} %get-tuple-element.104) | copy-start | bytes 18436
  322.2 11.5 %copy-start.5 = (bf16[16,64,384]{2,1,0:T(8,128)(2,1)S(1)}, bf16[16,64,384]{2,1,0:T(8,128)(2,1)}, u32[]{:S(2)}) copy-start(bf16[16,64,384]{2,1,0:T(8,128)(2,1)} %copy-done.4) | copy-start | bytes 2359300
  322.2 11.5 %copy-start.9 = (bf16[1024,384]{1,0:T(8,128)(2,1)S(1)}, bf16[1024,384]{1,0:T(8,128)(2,1)}, u32[]{:S(2)}) copy-start(bf16[1024,384]{1,0:T(8,128)(2,1)} %copy-done.8) | copy-start | bytes 2359300
  322.2 2.4 collective-permute-start.11
  325.7 21.7 %all-to-all-start.9 = ((bf16[16,64,384]{2,1,0:T(8,128)(2,1)}), bf16[16,64,384]{2,1,0:T(8,128)(2,1)}, u32[]{:S(2)}, u32[]{:S(2)}) async-start(bf16[16,64,384]{2,1,0:T(8,128)(2,1)} %bitcast.78), calls=%async_computation.10 | async-start | bytes 1572864 | tf_op jit(solution)/shard_map/all_to_all | solution.py:368
  349.7 35.0 %copy-start.19 = (f32[256,768]{1,0:T(8,128)S(1)}, f32[256,768]{1,0:T(8,128)}, u32[]{:S(2)}) copy-start(f32[256,768]{1,0:T(8,128)} %copy-done.17) | copy-start | bytes 2359300
  349.7 35.0 %copy-start.63 = (f32[768]{0:T(1024)S(1)}, f32[768]{0:T(1024)}, u32[]{:S(2)}) copy-start(f32[768]{0:T(1024)} %copy-done.62) | copy-start | bytes 9220
  377.7 27.4 %all-to-all-start.8 = ((bf16[8,112,768]{2,1,0:T(8,128)(2,1)}), bf16[8,112,768]{2,1,0:T(8,128)(2,1)S(1)}, u32[]{:S(2)}, u32[]{:S(2)}) async-start(bf16[8,112,768]{2,1,0:T(8,128)(2,1)} %bitcast.230), calls=%async_computation.9 | async-start | bytes 2752512 | tf_op jit(solution)/shard_map/all_to_all | solution.py:368
  435.9 6.6 %collective-permute-start.12 = (bf16[8,176,768]{2,1,0:T(8,128)(2,1)S(1)}, bf16[8,176,768]{2,1,0:T(8,128)(2,1)}, u32[]{:S(2)}, u32[]{:S(2)}) collective-permute-start(bf16[8,176,768]{2,1,0:T(8,128)(2,1)S(1)} %all_to_all.65.own), channel_id=1, source_target_pairs={{0,4},{4,0},{1,5},{5,1},{2,6},{6,2},{3,7},{7,3},{8,12},{12,8},{9,1... | collective-permute-start | bytes 6488072 | tf_op jit(solution)/shard_map/ppermute | solution.py:372
  (41 other events, 185.4 us)
Sparse Core Ops, SparseCore 0:
  10.9 70.4 all-gather.2
  306.4 71.2 reduce-scatter.1
